TPU v7x, 512 devices: a whole 4x8x8 slice. The times are simulated.
512 devices in a mesh: dp: 16 (over y, core), rows: 16 (over x, z_hi), cols: 2 (over z_lo).
Axes of the slice: x: 4, y: 8, z: 8 (z_hi: 4, z_lo: 2; z = z_hi * 2 + z_lo), core: 2. Of those that a mesh axis runs over, the one named last changes fastest.
Arguments:
- c3: bfloat16 [16, 128, 128, 512], P('dp', 'rows', 'cols'), may hold values from -6 to 6
- c4: bfloat16 [16, 64, 64, 1024], P('dp', 'rows', 'cols'), may hold values from -6 to 6
- top_down: bfloat16 [16, 32, 32, 256], P('dp', 'rows', 'cols'), may hold values from -6 to 6
- lat3_weight: bfloat16 [512, 256], replicated, may hold values from -0.25 to 0.25
- lat4_weight: bfloat16 [1024, 256], replicated, may hold values from -0.1875 to 0.1875
- conv_weight: bfloat16 [2304, 256], replicated, may hold values from -0.125 to 0.125
- p3_cot: bfloat16 [16, 128, 128, 256], P('dp', 'rows', 'cols'), may hold values from -6 to 6
- m4_cot: bfloat16 [16, 64, 64, 256], P('dp', 'rows', 'cols'), may hold values from -6 to 6
Outputs:
- p3: bfloat16 [16, 128, 128, 256], P('dp', 'rows', 'cols')
- c3_grad: bfloat16 [16, 128, 128, 512], P('dp', 'rows', 'cols')
- c4_grad: bfloat16 [16, 64, 64, 1024], P('dp', 'rows', 'cols')
- top_grad: bfloat16 [16, 32, 32, 256], P('dp', 'rows', 'cols')
- weight_grads: float32 [3840, 256], P('dp')
All inputs are finite; a program needn't handle non-finite values.
Results may differ from a plain program's by a relative error of at most 0.02.
Values may be sent and summed in bfloat16 or wider, within the bound.
No kernel may reach another device: no remote copies, remote signals or barrier semaphores. Data moves between devices by JAX's collectives and lax.ppermute only.
A program may use at most 64 MiB of HBM per device.

v0:
```python
import math

import jax
import jax.numpy as jnp
from jax import lax
from jax.sharding import PartitionSpec as P


def padded_2(shard, sides, width):
    for axis, dim in sides:
        devices, length = (lax.axis_size(axis), shard.shape[dim])
        up = [(i, (i + 1) % devices) for i in range(devices - 1)]
        down = [(j, i) for i, j in up]
        last = lax.slice_in_dim(shard, length - width, length, axis=dim)
        initial = lax.slice_in_dim(shard, 0, width, axis=dim)
        before = lax.ppermute(last, axis, up)
        after = lax.ppermute(initial, axis, down)
        shard = jnp.concatenate([before, shard, after], axis=dim)
    return shard


def upsample(field):
    return jnp.repeat(jnp.repeat(field, 2, axis=1), 2, axis=2)


def downsum(field):
    count, height, width, depth = field.shape
    return field.reshape(count, height // 2, 2, width // 2, 2, depth).sum(axis=(2, 4))


def shards(c3, c4, top_down, lat3_weight, lat4_weight, conv_weight, p3_cot, m4_cot):
    count, fine_h, fine_w, depth3 = c3.shape
    depth4 = c4.shape[3]
    chans = conv_weight.shape[1]
    coarse_h = fine_h // 2
    coarse_w = fine_w // 2
    c3_flat = c3.reshape(-1, depth3)
    c4_flat = c4.reshape(-1, depth4)
    lat4 = jnp.dot(c4_flat, lat4_weight, preferred_element_type=jnp.float32).reshape(
        count, coarse_h, coarse_w, chans
    )
    m4 = lat4 + upsample(top_down.astype(jnp.float32))
    lat3 = jnp.dot(c3_flat, lat3_weight, preferred_element_type=jnp.float32).reshape(
        count, fine_h, fine_w, chans
    )
    m3 = (lat3 + upsample(m4)).astype(jnp.bfloat16)
    padded = padded_2(m3, (("rows", 1), ("cols", 2)), 1)
    patches = jnp.concatenate(
        [padded[:, a : a + fine_h, b : b + fine_w, :] for a in range(3) for b in range(3)], axis=-1
    ).reshape(-1, 9 * chans)
    p3 = jnp.dot(patches, conv_weight, preferred_element_type=jnp.float32).astype(jnp.bfloat16)
    cot_pad = padded_2(p3_cot, (("rows", 1), ("cols", 2)), 1)
    cot_patches = jnp.concatenate(
        [
            cot_pad[:, 2 - a : 2 - a + fine_h, 2 - b : 2 - b + fine_w, :]
            for a in range(3)
            for b in range(3)
        ],
        axis=-1,
    ).reshape(-1, 9 * chans)
    flipped = conv_weight.reshape(9, chans, chans).transpose(0, 2, 1).reshape(9 * chans, chans)
    m3_grad = jnp.dot(cot_patches, flipped, preferred_element_type=jnp.float32)
    m3_grad_b = m3_grad.astype(jnp.bfloat16)
    c3_grad = jnp.dot(m3_grad_b, lat3_weight.T, preferred_element_type=jnp.float32).astype(
        jnp.bfloat16
    )
    m4_grad = m4_cot.astype(jnp.float32) + downsum(m3_grad.reshape(count, fine_h, fine_w, chans))
    m4_grad_b = m4_grad.astype(jnp.bfloat16).reshape(-1, chans)
    c4_grad = jnp.dot(m4_grad_b, lat4_weight.T, preferred_element_type=jnp.float32).astype(
        jnp.bfloat16
    )
    top_grad = downsum(m4_grad).astype(jnp.bfloat16)
    total_pixels = (
        count
        * fine_h
        * fine_w
        * lax.axis_size("dp")
        * lax.axis_size("rows")
        * lax.axis_size("cols")
    )
    scale = 1.0 / math.sqrt(total_pixels)
    grad3 = jnp.dot(c3_flat.T, m3_grad_b, preferred_element_type=jnp.float32)
    grad4 = jnp.dot(c4_flat.T, m4_grad_b, preferred_element_type=jnp.float32)
    gradc = jnp.dot(patches.T, p3_cot.reshape(-1, chans), preferred_element_type=jnp.float32)
    term = jnp.concatenate([grad3, grad4, gradc], axis=0) * scale
    summed = lax.psum(term, ("dp", "rows", "cols"))
    rows_each = term.shape[0] // lax.axis_size("dp")
    weight_grads = lax.dynamic_slice_in_dim(summed, lax.axis_index("dp") * rows_each, rows_each, 0)
    return (
        p3.reshape(count, fine_h, fine_w, chans),
        c3_grad.reshape(count, fine_h, fine_w, depth3),
        c4_grad.reshape(count, coarse_h, coarse_w, depth4),
        top_grad,
        weight_grads,
    )


def solution(mesh):
    placed = (
        P("dp", "rows", "cols", None),
        P("dp", "rows", "cols", None),
        P("dp", "rows", "cols", None),
        P(),
        P(),
        P(),
        P("dp", "rows", "cols", None),
        P("dp", "rows", "cols", None),
    )
    return jax.shard_map(
        shards,
        mesh=mesh,
        in_specs=placed,
        out_specs=(
            P("dp", "rows", "cols", None),
            P("dp", "rows", "cols", None),
            P("dp", "rows", "cols", None),
            P("dp", "rows", "cols", None),
            P("dp", None),
        ),
        check_vma=False,
    )
```

profile of v0, /device:TPU:1, one launch (start us, length us, event | category | flops | bytes accessed | tf_op | source)
XLA Modules:
  0.0 356.9 jit_solution(13939308309571147296)
XLA Ops:
  7.2 0.8 bitcast_convert_fusion
  8.2 1.5 convolution_add_fusion.1
  9.9 0.4 broadcast_in_dim.27
  10.6 1.3 collective-permute-start.1
  11.9 7.3 %collective-permute-start = (bf16[1,1,64,256]{3,2,1,0:T(8,128)(2,1)S(1)}, bf16[1,1,64,256]{3,2,1,0:T(8,128)(2,1)S(1)}, u32[]{:S(2)}, u32[]{:S(2)}) collective-permute-start(bf16[1,1,64,256]{3,2,1,0:T(8,128)(2,1)S(1)} %get-tuple-element.27), channel_id=1, source_target_pairs={{0,2},{2,4},{4,6},{6,8},{8,10},{10,12},{12,14},{14,16},{16,18},{18... | collective-permute-start | bytes 98312 | tf_op jit(solution)/shard_map/ppermute | solution.py:16
  19.2 7.0 %collective-permute-start.4 = (bf16[1,1,64,256]{3,2,1,0:T(8,128)(2,1)S(1)}, bf16[1,1,64,256]{3,2,1,0:T(8,128)(2,1)S(1)}, u32[]{:S(2)}, u32[]{:S(2)}) collective-permute-start(bf16[1,1,64,256]{3,2,1,0:T(8,128)(2,1)S(1)} %get-tuple-element.26), channel_id=1, source_target_pairs={{0,2},{2,4},{4,6},{6,8},{8,10},{10,12},{12,14},{14,16},{16,18},{18... | collective-permute-start | bytes 98312 | tf_op jit(solution)/shard_map/ppermute | solution.py:16
  26.2 1.3 collective-permute-start.5
  27.5 1.6 copy.17
  29.1 1.3 collective-permute-start.3
  30.4 4.0 %collective-permute-start.2 = (bf16[1,10,1,256]{3,2,1,0:T(2,128)(2,1)S(1)}, bf16[1,10,1,256]{3,2,1,0:T(2,128)(2,1)S(1)}, u32[]{:S(2)}, u32[]{:S(2)}) collective-permute-start(bf16[1,10,1,256]{3,2,1,0:T(2,128)(2,1)S(1)} %get-tuple-element.24), channel_id=1, source_target_pairs={{0,1},{2,3},{4,5},{6,7},{8,9},{10,11},{12,13},{14,15},{16,17},{18,... | collective-permute-start | bytes 15368 | tf_op jit(solution)/shard_map/ppermute | solution.py:16
  34.5 1.3 collective-permute-start.6
  35.8 4.0 %collective-permute-start.7 = (bf16[1,10,1,256]{3,2,1,0:T(2,128)(2,1)S(1)}, bf16[1,10,1,256]{3,2,1,0:T(2,128)(2,1)S(1)}, u32[]{:S(2)}, u32[]{:S(2)}) collective-permute-start(bf16[1,10,1,256]{3,2,1,0:T(2,128)(2,1)S(1)} %get-tuple-element.19), channel_id=1, source_target_pairs={{0,1},{2,3},{4,5},{6,7},{8,9},{10,11},{12,13},{14,15},{16,17},{18,... | collective-permute-start | bytes 15368 | tf_op jit(solution)/shard_map/ppermute | solution.py:16
  40.2 1.0 constant_dynamic-update-slice_fusion.15
  41.2 0.8 constant_dynamic-update-slice_fusion.14
  42.0 1.0 constant_dynamic-update-slice_fusion.13
  43.0 1.4 copy-done.19
  45.0 0.8 copy-done.5
  45.8 0.8 fusion.27
  46.9 4.0 %convolution_bitcast_fusion = f32[2304,256]{1,0:T(8,128)} fusion(bf16[1,8,64,2304]{3,2,1,0:T(8,128)(2,1)} %copy-done.19, bf16[1,8,64,256]{3,2,1,0:T(8,128)(2,1)S(1)} %copy-done.1), kind=kOutput, calls=%fused_computation | convolution fusion | flops 603979776 | bytes 4980736 | tf_op jit(solution)/shard_map/dot_general | solution.py:84
  50.9 0.4 reduce_sum.20
  51.3 1.3 convolution_bitcast_fusion.1
  52.6 1.6 copy.19
  54.5 1.0 copy.18
  55.5 3.9 %maximum_multiply_fusion = f32[3840,256]{1,0:T(8,128)} fusion(f32[2304,256]{1,0:T(8,128)} %convolution_bitcast_fusion, f32[1024,256]{1,0:T(8,128)S(1)} %copy.19, f32[512,256]{1,0:T(8,128)} %copy.18), kind=kLoop, calls=%fused_computation.1 | loop fusion | flops 2949120 | bytes 7864320 | tf_op jit(solution)/shard_map/mul | solution.py:85
  59.5 0.7 reshape.107
  60.2 1.6 reduce_sum.22
  62.2 0.7 copy-done.2
  62.9 1.0 convolution_convert_fusion.1
  63.9 1.1 convolution_convert_fusion
  65.0 1.5 convolution_convert_fusion.2
  66.5 281.9 %all-reduce.2.cloned.1.call-done = f32[3840,256]{1,0:T(8,128)} async-done(((f32[3840,256]{1,0:T(8,128)}), f32[3840,256]{1,0:T(8,128)}) %all-reduce.2.cloned.1.call-update) | async-done | bytes 3932176 | tf_op jit(solution)/shard_map/psum | solution.py:86
  348.4 1.7 constant_dynamic-slice_fusion
  (88 shorter events, 2.6 us)
Async XLA Ops:
  7.2 3.1 copy-start
  7.2 3.1 copy-start.13
  7.2 341.2 %all-reduce.2.cloned.1.call-start = ((), (), s32[]{:S(2)}) async-start(), calls=%async_computation | async-start | bytes 7864320 | tf_op jit(solution)/shard_map/psum | solution.py:86
  8.2 11.0 %copy-start.1 = (bf16[1,8,64,256]{3,2,1,0:T(8,128)(2,1)S(1)}, bf16[1,8,64,256]{3,2,1,0:T(8,128)(2,1)}, u32[]{:S(2)}) copy-start(bf16[1,8,64,256]{3,2,1,0:T(8,128)(2,1)} %param.14) | copy-start | bytes 786436
  8.2 19.3 %copy-start.3 = (bf16[2304,256]{1,0:T(8,128)(2,1)S(1)}, bf16[2304,256]{1,0:T(8,128)(2,1)}, u32[]{:S(2)}) copy-start(bf16[2304,256]{1,0:T(8,128)(2,1)} %param.13) | copy-start | bytes 3538948
  10.6 18.5 %collective-permute-start.1 = (bf16[1,1,64,256]{3,2,1,0:T(8,128)(2,1)S(1)}, bf16[1,1,64,256]{3,2,1,0:T(8,128)(2,1)S(1)}, u32[]{:S(2)}, u32[]{:S(2)}) collective-permute-start(bf16[1,1,64,256]{3,2,1,0:T(8,128)(2,1)S(1)} %get-tuple-element.28), channel_id=1, source_target_pairs={{2,0},{4,2},{6,4},{8,6},{10,8},{12,10},{14,12},{16,14},{18,16},{20... | collective-permute-start | bytes 98312 | tf_op jit(solution)/shard_map/ppermute | solution.py:17
  11.9 17.2 %collective-permute-start = (bf16[1,1,64,256]{3,2,1,0:T(8,128)(2,1)S(1)}, bf16[1,1,64,256]{3,2,1,0:T(8,128)(2,1)S(1)}, u32[]{:S(2)}, u32[]{:S(2)}) collective-permute-start(bf16[1,1,64,256]{3,2,1,0:T(8,128)(2,1)S(1)} %get-tuple-element.27), channel_id=1, source_target_pairs={{0,2},{2,4},{4,6},{6,8},{8,10},{10,12},{12,14},{14,16},{16,18},{18... | collective-permute-start | bytes 98312 | tf_op jit(solution)/shard_map/ppermute | solution.py:16
  19.2 15.2 %collective-permute-start.4 = (bf16[1,1,64,256]{3,2,1,0:T(8,128)(2,1)S(1)}, bf16[1,1,64,256]{3,2,1,0:T(8,128)(2,1)S(1)}, u32[]{:S(2)}, u32[]{:S(2)}) collective-permute-start(bf16[1,1,64,256]{3,2,1,0:T(8,128)(2,1)S(1)} %get-tuple-element.26), channel_id=1, source_target_pairs={{0,2},{2,4},{4,6},{6,8},{8,10},{10,12},{12,14},{14,16},{16,18},{18... | collective-permute-start | bytes 98312 | tf_op jit(solution)/shard_map/ppermute | solution.py:16
  26.2 8.2 %collective-permute-start.5 = (bf16[1,1,64,256]{3,2,1,0:T(8,128)(2,1)S(1)}, bf16[1,1,64,256]{3,2,1,0:T(8,128)(2,1)S(1)}, u32[]{:S(2)}, u32[]{:S(2)}) collective-permute-start(bf16[1,1,64,256]{3,2,1,0:T(8,128)(2,1)S(1)} %get-tuple-element.25), channel_id=1, source_target_pairs={{2,0},{4,2},{6,4},{8,6},{10,8},{12,10},{14,12},{16,14},{18,16},{20... | collective-permute-start | bytes 98312 | tf_op jit(solution)/shard_map/ppermute | solution.py:17
  29.1 10.7 %collective-permute-start.3 = (bf16[1,10,1,256]{3,2,1,0:T(2,128)(2,1)S(1)}, bf16[1,10,1,256]{3,2,1,0:T(2,128)(2,1)S(1)}, u32[]{:S(2)}, u32[]{:S(2)}) collective-permute-start(bf16[1,10,1,256]{3,2,1,0:T(2,128)(2,1)S(1)} %get-tuple-element.23), channel_id=1, source_target_pairs={{1,0},{3,2},{5,4},{7,6},{9,8},{11,10},{13,12},{15,14},{17,16},{19,... | collective-permute-start | bytes 15368 | tf_op jit(solution)/shard_map/ppermute | solution.py:17
  30.4 9.4 %collective-permute-start.2 = (bf16[1,10,1,256]{3,2,1,0:T(2,128)(2,1)S(1)}, bf16[1,10,1,256]{3,2,1,0:T(2,128)(2,1)S(1)}, u32[]{:S(2)}, u32[]{:S(2)}) collective-permute-start(bf16[1,10,1,256]{3,2,1,0:T(2,128)(2,1)S(1)} %get-tuple-element.24), channel_id=1, source_target_pairs={{0,1},{2,3},{4,5},{6,7},{8,9},{10,11},{12,13},{14,15},{16,17},{18,... | collective-permute-start | bytes 15368 | tf_op jit(solution)/shard_map/ppermute | solution.py:16
  34.5 9.9 %collective-permute-start.6 = (bf16[1,10,1,256]{3,2,1,0:T(2,128)(2,1)S(1)}, bf16[1,10,1,256]{3,2,1,0:T(2,128)(2,1)S(1)}, u32[]{:S(2)}, u32[]{:S(2)}) collective-permute-start(bf16[1,10,1,256]{3,2,1,0:T(2,128)(2,1)S(1)} %get-tuple-element.20), channel_id=1, source_target_pairs={{1,0},{3,2},{5,4},{7,6},{9,8},{11,10},{13,12},{15,14},{17,16},{19,... | collective-permute-start | bytes 15368 | tf_op jit(solution)/shard_map/ppermute | solution.py:17
  35.8 8.8 %collective-permute-start.7 = (bf16[1,10,1,256]{3,2,1,0:T(2,128)(2,1)S(1)}, bf16[1,10,1,256]{3,2,1,0:T(2,128)(2,1)S(1)}, u32[]{:S(2)}, u32[]{:S(2)}) collective-permute-start(bf16[1,10,1,256]{3,2,1,0:T(2,128)(2,1)S(1)} %get-tuple-element.19), channel_id=1, source_target_pairs={{0,1},{2,3},{4,5},{6,7},{8,9},{10,11},{12,13},{14,15},{16,17},{18,... | collective-permute-start | bytes 15368 | tf_op jit(solution)/shard_map/ppermute | solution.py:16
  43.0 1.4 copy-start.19
  44.5 1.3 copy-start.5
  46.9 4.4 %copy-start.18 = (bf16[1,4,32,256]{3,2,1,0:T(8,128)(2,1)S(1)}, bf16[1,4,32,256]{3,2,1,0:T(8,128)(2,1)}, u32[]{:S(2)}) copy-start(bf16[1,4,32,256]{3,2,1,0:T(8,128)(2,1)} %param.15) | copy-start | bytes 196612
  46.9 4.4 %copy-start.15 = (bf16[1,4,32,1024]{3,2,1,0:T(8,128)(2,1)S(1)}, bf16[1,4,32,1024]{3,2,1,0:T(8,128)(2,1)}, u32[]{:S(2)}) copy-start(bf16[1,4,32,1024]{3,2,1,0:T(8,128)(2,1)} %param.9) | copy-start | bytes 786436
  51.3 3.2 copy-start.16
  59.4 2.4 copy-start.11
  59.4 2.5 copy-start.12
  59.4 2.5 copy-start.9
  59.4 2.6 copy-start.10
  59.5 2.6 copy-start.6
  59.5 2.6 copy-start.7
  59.5 2.6 copy-start.8
  61.8 1.0 copy-start.2
  61.8 1.0 copy-start.17
  61.9 2.0 copy-start.14
  62.0 3.0 copy-start.4
Sparse Core Ops, SparseCore 0:
  59.6 288.8 all-reduce.1
where the time goes:
time: 358 us; the launch traced here: 357 us
  waiting for transfers between devices  282 us (79%)
  starting transfers between devices  27.5 us (8%)
  between operations  14.7 us (4%)
  local copies, waits for them, and re-layouts  12.9 us (4%)
  matrix products  11.7 us (3%)
  other arithmetic  8.11 us (2%)
    psum x1, waiting for transfers between devices, shards(): summed = lax.psum(term, ('dp', 'rows', 'cols'))  282 us
    ppermute x4, starting transfers between devices, padded_2(): before = lax.ppermute(last, axis, up)  22.3 us
  transfers between devices with their start and end apart: 9, of which 1 were waited for; matrix products, arithmetic and copies ran while one was open for 3% of the time, Pallas kernels for 0%

commit v1 on v0

v1 whole, which is shorter than its diff:
```python
import functools
import math

import jax
import jax.numpy as jnp
from jax import lax
from jax.experimental import pallas as pl
from jax.experimental.pallas import tpu as pltpu
from jax.sharding import PartitionSpec as P

F32 = jnp.float32
BF16 = jnp.bfloat16
ROWS = ("x", "z_hi")
LIMIT = 32 * 1024 * 1024
NT = (((1,), (1,)), ((), ()))
TN = (((0,), (0,)), ((), ()))


def dot(lhs, rhs, dims=(((1,), (0,)), ((), ()))):
    return lax.dot_general(lhs, rhs, dims, preferred_element_type=F32)


def call(kernel, out_shape, scratch, flops, moved, *args):
    in_vmem = pl.BlockSpec(memory_space=pltpu.VMEM)
    return pl.pallas_call(
        kernel,
        out_shape=out_shape,
        in_specs=[in_vmem] * len(args),
        out_specs=[in_vmem] * len(out_shape),
        scratch_shapes=scratch,
        compiler_params=pltpu.CompilerParams(vmem_limit_bytes=LIMIT),
        cost_estimate=pl.CostEstimate(flops=flops, bytes_accessed=moved, transcendentals=0),
    )(*args)


def merge_kernel(width4, c3, c4, top, lat3, lat4, m3, up4):
    n4, n5 = c4.shape[0], top.shape[0]
    n3 = c3.shape[0]
    width3, width5 = 2 * width4, width4 // 2
    row = lax.broadcasted_iota(jnp.int32, (n4, n5), 0)
    col = lax.broadcasted_iota(jnp.int32, (n4, n5), 1)
    source = (row // width4 // 2) * width5 + (row % width4) // 2
    pick = jnp.where(source == col, 1.0, 0.0).astype(BF16)
    m4 = dot(c4[...], lat4[...]) + dot(pick, top[...])
    up4[0, pl.ds(0, n4, stride=2), :] = m4[:, :128]
    up4[0, pl.ds(1, n4, stride=2), :] = m4[:, :128]
    up4[1, pl.ds(0, n4, stride=2), :] = m4[:, 128:]
    up4[1, pl.ds(1, n4, stride=2), :] = m4[:, 128:]
    lat = dot(c3[...], lat3[...])
    for y in range(n3 // width3):
        rows = slice(y * width3, (y + 1) * width3)
        above = slice((y // 2) * width3, (y // 2 + 1) * width3)
        m3[rows, :128] = (lat[rows, :128] + up4[0, above]).astype(BF16)
        m3[rows, 128:] = (lat[rows, 128:] + up4[1, above]).astype(BF16)


def fill_shifted(own, before, after, left, right, shifted, width):
    n = own.shape[0]
    shifted[1, 0:width] = before[...]
    shifted[1, width : width + n] = own[...]
    shifted[1, width + n :] = after[...]
    at = lax.broadcasted_iota(jnp.int32, (width, own.shape[1]), 0)
    for y in range(n // width + 2):
        rows = slice(y * width, (y + 1) * width)
        line = shifted[1, rows].astype(F32)
        to_left = pltpu.roll(line, 1, 0)
        to_right = pltpu.roll(line, width - 1, 0)
        shifted[0, rows] = jnp.where(at == 0, left[y : y + 1, :], to_left).astype(BF16)
        shifted[2, rows] = jnp.where(at == width - 1, right[y : y + 1, :], to_right).astype(BF16)


def pieces_of(block, each):
    per = each // 16
    return block // per // 2, (block // per) % 2, block % per


def grads_kernel(
    width, each, scale, core, cot, before, after, left, right, m3, c3, c4, conv, m4_cot,
    m3_grad_b, m4_grad_b, top_grad, term, shifted, sums, sums5,
):
    n3, chans = cot.shape
    n4 = c4.shape[0]
    me = core[0]
    per = each // 16

    def put(first, value):
        value = (value * scale).astype(BF16)
        for k in range(value.shape[0] // 16):
            y, owner, r = pieces_of(first // 16 + k, each)
            slot = jnp.where(me == owner, 0, 1)
            for h in range(2):
                p = h * 16 + r
                x, z_hi, z_lo = p // 8, (p // 2) % 4, p % 2
                term[slot, x * 2 + z_lo, y * 4 + z_hi] = value[
                    16 * k : 16 * k + 16, 128 * h : 128 * h + 128
                ]

    blank = jnp.zeros((16, 128), BF16)
    for y in range(8):
        for r in range(per, 16):
            for h in range(2):
                p = h * 16 + r
                x, z_hi, z_lo = p // 8, (p // 2) % 4, p % 2
                for slot in range(2):
                    term[slot, x * 2 + z_lo, y * 4 + z_hi] = blank

    fill_shifted(cot, before, after, left, right, shifted, width)

    def cot_at(a, b):
        return shifted[2 - b, (2 - a) * width : (2 - a) * width + n3]

    total = None
    for a in range(3):
        for b in range(3):
            tap = 3 * a + b
            weight = conv[tap * chans : (tap + 1) * chans]
            part = dot(cot_at(a, b), weight, NT)
            total = part if total is None else total + part
    m3_grad_b[...] = total.astype(BF16)
    for y in range(n4 // (width // 2)):
        pair = total[2 * y * width : (2 * y + 1) * width] + total[(2 * y + 1) * width : (2 * y + 2) * width]
        sums[0, y * width : (y + 1) * width] = pair[:, :128]
        sums[1, y * width : (y + 1) * width] = pair[:, 128:]
    for h in range(2):
        cols = slice(128 * h, 128 * h + 128)
        m4_grad = (
            m4_cot[:, cols].astype(F32)
            + sums[h, pl.ds(0, n4, stride=2), :]
            + sums[h, pl.ds(1, n4, stride=2), :]
        )
        m4_grad_b[:, cols] = m4_grad.astype(BF16)
        half = width // 2
        for y in range(n4 // width):
            sums5[h, y * half : (y + 1) * half] = (
                m4_grad[2 * y * half : (2 * y + 1) * half]
                + m4_grad[(2 * y + 1) * half : (2 * y + 2) * half]
            )
        n5 = n4 // 4
        top_grad[:, cols] = (
            sums5[h, pl.ds(0, n5, stride=2), :] + sums5[h, pl.ds(1, n5, stride=2), :]
        ).astype(BF16)

    depth3, depth4 = c3.shape[1], c4.shape[1]
    put(0, dot(c3[...], m3_grad_b[...], TN))
    put(depth3, dot(c4[...], m4_grad_b[...], TN))
    m3_t = m3[...].T
    for a in range(3):
        for b in range(3):
            tap = 3 * a + b
            put(depth3 + depth4 + tap * chans, dot(m3_t, cot_at(a, b)))


def outputs_kernel(
    width, m3, before, after, left, right, conv, m3_grad_b, lat3, m4_grad_b, lat4,
    p3, c3_grad, c4_grad, shifted,
):
    n3, chans = m3.shape
    fill_shifted(m3, before, after, left, right, shifted, width)
    total = None
    for a in range(3):
        for b in range(3):
            tap = 3 * a + b
            part = dot(shifted[b, a * width : a * width + n3], conv[tap * chans : (tap + 1) * chans])
            total = part if total is None else total + part
    p3[...] = total.astype(BF16)
    c3_grad[...] = dot(m3_grad_b[...], lat3[...], NT).astype(BF16)
    c4_grad[...] = dot(m4_grad_b[...], lat4[...], NT).astype(BF16)


def run_grads(width, each, scale, core, cot, cot_borders, m3, c3, c4, conv, m4_cot):
    n3, chans = cot.shape
    n4 = c4.shape[0]
    depth = c3.shape[1] + c4.shape[1] + conv.shape[0]
    in_vmem = pl.BlockSpec(memory_space=pltpu.VMEM)
    return pl.pallas_call(
        functools.partial(grads_kernel, width, each, scale),
        out_shape=[
            jax.ShapeDtypeStruct((n3, chans), BF16),
            jax.ShapeDtypeStruct((n4, chans), BF16),
            jax.ShapeDtypeStruct((n4 // 4, chans), BF16),
            jax.ShapeDtypeStruct((2, 8, 32, 16, 128), BF16),
        ],
        in_specs=[pl.BlockSpec(memory_space=pltpu.SMEM)] + [in_vmem] * 10,
        out_specs=[in_vmem] * 4,
        scratch_shapes=[
            pltpu.VMEM((3, n3 + 2 * width, chans), BF16),
            pltpu.VMEM((2, n3 // 2, 128), F32),
            pltpu.VMEM((2, n4 // 2, 128), F32),
        ],
        compiler_params=pltpu.CompilerParams(vmem_limit_bytes=LIMIT),
        cost_estimate=pl.CostEstimate(
            flops=2 * chans * (n3 * c3.shape[1] + n4 * c4.shape[1] + 18 * n3 * chans),
            bytes_accessed=2 * (n3 * c3.shape[1] + n4 * c4.shape[1] + 2 * depth * chans),
            transcendentals=0,
        ),
    )(core, cot, *cot_borders, m3, c3, c4, conv, m4_cot)


def run_outputs(width, m3, m3_borders, conv, m3_grad_b, lat3, m4_grad_b, lat4):
    n3, chans = m3.shape
    n4 = m4_grad_b.shape[0]
    depth3, depth4 = lat3.shape[0], lat4.shape[0]
    return call(
        functools.partial(outputs_kernel, width),
        [
            jax.ShapeDtypeStruct((n3, chans), BF16),
            jax.ShapeDtypeStruct((n3, depth3), BF16),
            jax.ShapeDtypeStruct((n4, depth4), BF16),
        ],
        [pltpu.VMEM((3, n3 + 2 * width, chans), BF16)],
        2 * chans * (n3 * depth3 + n4 * depth4 + 9 * n3 * chans),
        4 * (n3 * depth3 + n4 * depth4 + 9 * chans * chans),
        m3, *m3_borders, conv, m3_grad_b, lat3, m4_grad_b, lat4,
    )


def borders(tile):
    height, width, chans = tile.shape
    z_lo = lax.axis_index("z_lo")
    col = jnp.where(z_lo == 0, tile[:, -1], tile[:, 0])
    col = lax.ppermute(col, "z_lo", [(0, 1), (1, 0)])
    n_rows = lax.axis_size(ROWS)
    odd = lax.axis_index(ROWS) % 2 == 1
    pad = jnp.zeros((15, chans), tile.dtype)
    top = jnp.concatenate([tile[0], col[:1], pad], axis=0)
    bottom = jnp.concatenate([tile[-1], col[-1:], pad], axis=0)
    pairs = [(i, i + 1) for i in range(0, n_rows - 1, 2)]
    between = [(i, i + 1) for i in range(1, n_rows - 1, 2)]
    first = lax.ppermute(jnp.where(odd, top, bottom), ROWS, pairs + [(j, i) for i, j in pairs])
    second = lax.ppermute(
        jnp.where(odd, bottom, top), ROWS, between + [(j, i) for i, j in between]
    )
    before = jnp.where(odd, first, second)
    after = jnp.where(odd, second, first)
    sides = jnp.concatenate([before[width : width + 1], col, after[width : width + 1]], axis=0)
    sides = jnp.concatenate([sides, pad[: 14 - height]], axis=0).astype(F32)
    left = jnp.where(z_lo == 1, sides, 0.0)
    right = jnp.where(z_lo == 0, sides, 0.0)
    return before[:width], after[:width], left, right


def add_up(parts):
    return parts.astype(F32).sum(axis=0).astype(BF16)


def add_cores(term):
    got = lax.ppermute(term[1], "core", [(0, 1), (1, 0)])
    return (term[0].astype(F32) + got.astype(F32)).astype(BF16)


def reduce_grads(part):
    part = add_up(lax.all_to_all(part, ("x", "z_lo"), 0, 0, tiled=True))
    return add_up(lax.all_to_all(part, ("y", "z_hi"), 0, 0, tiled=True))


def share_grads(part, each):
    everywhere = ("x", "z_hi", "z_lo")
    n = lax.axis_size(everywhere)
    part = jnp.broadcast_to(part[None], (n,) + part.shape)
    part = lax.all_to_all(part, everywhere, 0, 0, tiled=True)
    halves = part.reshape(2, -1, part.shape[-1])[:, :each].astype(F32)
    return jnp.concatenate([halves[0], halves[1]], axis=1)


def shards(c3, c4, top_down, lat3_weight, lat4_weight, conv_weight, p3_cot, m4_cot):
    count, height, width, depth3 = c3.shape
    depth4 = c4.shape[3]
    chans = conv_weight.shape[1]
    n3 = height * width
    n4 = n3 // 4
    n5 = n4 // 4
    c3_flat = c3.reshape(n3, depth3)
    c4_flat = c4.reshape(n4, depth4)
    stacked = depth3 + depth4 + 9 * chans
    each = stacked // lax.axis_size(("y", "core"))
    total_pixels = n3 * lax.axis_size(("y", "core", "x", "z_hi", "z_lo"))
    scale = 1.0 / math.sqrt(total_pixels)

    cot_borders = borders(p3_cot[0])
    (m3,) = call(
        functools.partial(merge_kernel, width // 2),
        [jax.ShapeDtypeStruct((n3, chans), BF16)],
        [pltpu.VMEM((2, 2 * n4, 128), F32)],
        2 * chans * (n3 * depth3 + n4 * depth4),
        2 * (n3 * depth3 + n4 * depth4 + chans * (depth3 + depth4 + n3)),
        c3_flat, c4_flat, top_down.reshape(n5, chans), lat3_weight, lat4_weight,
    )
    core = lax.axis_index("core").astype(jnp.int32).reshape(1)
    m3_grad_b, m4_grad_b, top_grad, term = run_grads(
        width, each, scale, core, p3_cot.reshape(n3, chans), cot_borders, m3, c3_flat, c4_flat,
        conv_weight, m4_cot.reshape(n4, chans),
    )
    part = add_cores(term)
    part, m3 = lax.optimization_barrier((part, m3))
    weight_grads = share_grads(reduce_grads(part), each)
    m3_borders = borders(m3.reshape(height, width, chans))
    p3, c3_grad, c4_grad = run_outputs(
        width, m3, m3_borders, conv_weight, m3_grad_b, lat3_weight, m4_grad_b, lat4_weight
    )
    return (
        p3.reshape(count, height, width, chans),
        c3_grad.reshape(count, height, width, depth3),
        c4_grad.reshape(count, height // 2, width // 2, depth4),
        top_grad.reshape(top_down.shape),
        weight_grads,
    )


def solution(mesh):
    split = jax.sharding.Mesh(
        mesh.devices.reshape(8, 2, 4, 4, 2), ("y", "core", "x", "z_hi", "z_lo")
    )
    tiles = P(("y", "core"), ("x", "z_hi"), "z_lo", None)
    return jax.shard_map(
        shards,
        mesh=split,
        in_specs=(tiles, tiles, tiles, P(), P(), P(), tiles, tiles),
        out_specs=(tiles, tiles, tiles, tiles, P(("y", "core"), None)),
        check_vma=False,
    )
```

time: 358 us -> 105 us (0.29)
  the two profiles are of different devices: /device:TPU:1 before, /device:TPU:2 now
where the time goes in v1:
time: 105 us; the launch traced here: 104 us
  starting transfers between devices  52.4 us (50%)
  waiting for transfers between devices  32.9 us (31%)
  local copies, waits for them, and re-layouts  8.47 us (8%)
  Pallas kernels  5.26 us (5%)
  other arithmetic  4.42 us (4%)
    ppermute x2, starting transfers between devices, borders(): lax.ppermute(jnp.where(odd, bottom, top), ROWS, between + [(j, i) for i,...  12.5 us
    all_to_all x1, waiting for transfers between devices, reduce_grads(): return add_up(lax.all_to_all(part, ('y', 'z_hi'), 0, 0, tiled=True))  12.4 us
    all_to_all x1, starting transfers between devices, reduce_grads(): return add_up(lax.all_to_all(part, ('y', 'z_hi'), 0, 0, tiled=True))  11.9 us
    ppermute x2, waiting for transfers between devices, borders(): col = lax.ppermute(col, 'z_lo', [(0, 1), (1, 0)])  10.7 us
    ppermute x2, starting transfers between devices, borders(): col = lax.ppermute(col, 'z_lo', [(0, 1), (1, 0)])  7.65 us
    all_to_all x1, waiting for transfers between devices, share_grads(): part = lax.all_to_all(part, everywhere, 0, 0, tiled=True)  7.14 us
    ppermute x2, starting transfers between devices, borders(): lax.ppermute(jnp.where(odd, top, bottom), ROWS, pairs + [(j, i) for i, j...  6.77 us
    unnamed x21, local copies, waits for them, and re-layouts  6.58 us
  transfers between devices with their start and end apart: 10, of which 5 were waited for; matrix products, arithmetic and copies ran while one was open for 3% of the time, Pallas kernels for 2%

profile of v1, /device:TPU:2, one launch (start us, length us, event | category | flops | bytes accessed | tf_op | source)
XLA Modules:
  0.0 104.4 jit_solution(17772823368836958540)
XLA Ops:
  0.7 1.1 %copy.27 = bf16[1,8,64,256]{3,1,2,0:T(8,128)(2,1)S(1)} copy(bf16[1,8,64,256]{3,2,1,0:T(8,128)(2,1)} %param.14) | data formatting | bytes 524288 | tf_op args[6]
  1.8 4.3 %collective-permute-start = (bf16[8,256]{1,0:T(8,128)(2,1)S(1)}, bf16[8,256]{1,0:T(8,128)(2,1)S(1)}, u32[]{:S(2)}, u32[]{:S(2)}) collective-permute-start(bf16[8,256]{1,0:T(8,128)(2,1)S(1)} %fusion.1), channel_id=1, source_target_pairs={{0,1},{1,0},{2,3},{3,2},{4,5},{5,4},{6,7},{7,6},{8,9},{9,8},{10,11... | collective-permute-start | bytes 12296 | tf_op jit(solution)/shard_map/ppermute | solution.py:221
  6.1 0.8 slice_bitcast_fusion.4
  7.0 0.7 collective-permute-done
  7.7 0.1 broadcast_select_fusion.6
  7.8 10.6 %collective-permute-start.2 = (bf16[80,256]{1,0:T(8,128)(2,1)S(1)}, bf16[80,256]{1,0:T(8,128)(2,1)S(1)}, u32[]{:S(2)}, u32[]{:S(2)}) collective-permute-start(bf16[80,256]{1,0:T(8,128)(2,1)S(1)} %get-tuple-element.37), channel_id=1, source_target_pairs={{2,4},{6,8},{10,12},{14,16},{18,20},{22,24},{26,28},{4,2},{8,6},{1... | collective-permute-start | bytes 122888 | tf_op jit(solution)/shard_map/ppermute | solution.py:230
  18.3 2.5 %collective-permute-start.1 = (bf16[80,256]{1,0:T(8,128)(2,1)S(1)}, bf16[80,256]{1,0:T(8,128)(2,1)S(1)}, u32[]{:S(2)}, u32[]{:S(2)}) collective-permute-start(bf16[80,256]{1,0:T(8,128)(2,1)S(1)} %get-tuple-element.38), channel_id=1, source_target_pairs={{0,2},{4,6},{8,10},{12,14},{16,18},{20,22},{24,26},{28,30},{2,0},{... | collective-permute-start | bytes 122888 | tf_op jit(solution)/shard_map/ppermute | solution.py:229
  20.9 1.0 copy-done
  22.0 1.0 copy-done.1
  23.0 0.9 copy-done.4
  24.0 0.9 copy-done.5
  24.9 0.7 copy-done.7
  25.6 0.4 shard_map.119.m3
  26.2 0.7 copy-done.8
  26.9 3.0 %shard_map.120 = (bf16[512,256]{1,0:T(8,128)(2,1)S(1)}, bf16[128,256]{1,0:T(8,128)(2,1)S(1)}, bf16[32,256]{1,0:T(8,128)(2,1)}, bf16[2,8,32,16,128]{4,3,2,1,0:T(8,128)(2,1)S(1)}) custom-call(s32[1]{0:T(128)} %bitcast.core, bf16[512,256]{1,0:T(8,128)(2,1)S(1)} %bitcast.35, bf16[64,256]{1,0:T(8,128)(2,1)S(1)} %slice.108.before, ...), custom_call_target="tpu_custom_call" | custom-call | flops 1409286144 | bytes 4718592 | tf_op jit(solution)/shard_map/pallas_call | solution.py:175
  29.9 0.2 slice_bitcast_fusion
  30.1 1.9 %collective-permute-start.3 = (bf16[8,32,16,128]{3,2,1,0:T(8,128)(2,1)S(1)}, bf16[8,32,16,128]{3,2,1,0:T(8,128)(2,1)S(1)}, u32[]{:S(2)}, u32[]{:S(2)}) collective-permute-start(bf16[8,32,16,128]{3,2,1,0:T(8,128)(2,1)S(1)} %slice_bitcast_fusion), channel_id=1, source_target_pairs={{0,32},{32,0},{1,33},{33,1},{2,34},{34,2},{3,35},{35,3},{4,36},{36... | collective-permute-start | bytes 3145736 | tf_op jit(solution)/shard_map/ppermute | solution.py:247
  32.0 2.6 %collective-permute-done.3 = bf16[8,32,16,128]{3,2,1,0:T(8,128)(2,1)S(1)} collective-permute-done((bf16[8,32,16,128]{3,2,1,0:T(8,128)(2,1)S(1)}, bf16[8,32,16,128]{3,2,1,0:T(8,128)(2,1)S(1)}, u32[]{:S(2)}, u32[]{:S(2)}) %collective-permute-start.3) | collective-permute-done | bytes 1048608 | tf_op jit(solution)/shard_map/ppermute | solution.py:247
  34.6 1.2 %fusion = bf16[8,32,16,128]{3,2,1,0:T(8,128)(2,1)} fusion(bf16[8,32,16,128]{3,2,1,0:T(8,128)(2,1)S(1)} %collective-permute-done.3, bf16[2,8,32,16,128]{4,3,2,1,0:T(8,128)(2,1)S(1)} %get-tuple-element.14), kind=kLoop, calls=%fused_computation.1 | loop fusion | flops 2097152 | bytes 3145728 | tf_op jit(solution)/shard_map/convert_element_type | solution.py:248
  35.9 5.9 %all-to-all-start = ((bf16[8,32,16,128]{3,2,1,0:T(8,128)(2,1)}), bf16[8,32,16,128]{3,2,1,0:T(8,128)(2,1)}, u32[]{:S(2)}, u32[]{:S(2)}) async-start(bf16[8,32,16,128]{3,2,1,0:T(8,128)(2,1)} %fusion), calls=%async_computation | async-start | bytes 2097152 | tf_op jit(solution)/shard_map/all_to_all | solution.py:252
  41.8 3.4 %collective-permute-start.4 = (bf16[8,256]{1,0:T(8,128)(2,1)S(1)}, bf16[8,256]{1,0:T(8,128)(2,1)S(1)}, u32[]{:S(2)}, u32[]{:S(2)}) collective-permute-start(bf16[8,256]{1,0:T(8,128)(2,1)S(1)} %fusion.2), channel_id=1, source_target_pairs={{0,1},{1,0},{2,3},{3,2},{4,5},{5,4},{6,7},{7,6},{8,9},{9,8},{10,11... | collective-permute-start | bytes 12296 | tf_op jit(solution)/shard_map/ppermute | solution.py:221
  45.2 10.0 %collective-permute-done.4 = bf16[8,256]{1,0:T(8,128)(2,1)S(1)} collective-permute-done((bf16[8,256]{1,0:T(8,128)(2,1)S(1)}, bf16[8,256]{1,0:T(8,128)(2,1)S(1)}, u32[]{:S(2)}, u32[]{:S(2)}) %collective-permute-start.4) | collective-permute-done | bytes 4128 | tf_op jit(solution)/shard_map/ppermute | solution.py:221
  55.3 1.9 %collective-permute-start.6 = (bf16[80,256]{1,0:T(8,128)(2,1)S(1)}, bf16[80,256]{1,0:T(8,128)(2,1)S(1)}, u32[]{:S(2)}, u32[]{:S(2)}) collective-permute-start(bf16[80,256]{1,0:T(8,128)(2,1)S(1)} %get-tuple-element.35), channel_id=1, source_target_pairs={{2,4},{6,8},{10,12},{14,16},{18,20},{22,24},{26,28},{4,2},{8,6},{1... | collective-permute-start | bytes 122888 | tf_op jit(solution)/shard_map/ppermute | solution.py:230
  57.2 4.3 %collective-permute-start.5 = (bf16[80,256]{1,0:T(8,128)(2,1)S(1)}, bf16[80,256]{1,0:T(8,128)(2,1)S(1)}, u32[]{:S(2)}, u32[]{:S(2)}) collective-permute-start(bf16[80,256]{1,0:T(8,128)(2,1)S(1)} %get-tuple-element.36), channel_id=1, source_target_pairs={{0,2},{4,6},{8,10},{12,14},{16,18},{20,22},{24,26},{28,30},{2,0},{... | collective-permute-start | bytes 122888 | tf_op jit(solution)/shard_map/ppermute | solution.py:229
  61.6 2.1 %reduce_sum.24 = bf16[32,16,128]{2,1,0:T(8,128)(2,1)} reduce(bf16[8,32,16,128]{3,2,1,0:T(8,128)(2,1)} %all-to-all-done, bf16[]{:T(256)} %constant.39.clone.1), dimensions={0}, to_apply=%region_0.1 | reduce | flops 458752 | bytes 1179650 | tf_op jit(solution)/shard_map/reduce_sum | solution.py:243
  63.6 11.9 %all-to-all-start.1 = ((bf16[32,16,128]{2,1,0:T(8,128)(2,1)}), bf16[32,16,128]{2,1,0:T(8,128)(2,1)S(1)}, u32[]{:S(2)}, u32[]{:S(2)}) async-start(bf16[32,16,128]{2,1,0:T(8,128)(2,1)} %reduce_sum.24), calls=%async_computation.1 | async-start | bytes 262144 | tf_op jit(solution)/shard_map/all_to_all | solution.py:253
  75.6 12.4 %all-to-all-done.1 = bf16[32,16,128]{2,1,0:T(8,128)(2,1)S(1)} async-done(((bf16[32,16,128]{2,1,0:T(8,128)(2,1)}), bf16[32,16,128]{2,1,0:T(8,128)(2,1)S(1)}, u32[]{:S(2)}, u32[]{:S(2)}) %all-to-all-start.1) | async-done | bytes 131104 | tf_op jit(solution)/shard_map/all_to_all | solution.py:253
  88.0 0.7 broadcast_in_dim.14
  88.7 5.8 %all-to-all-start.2 = ((bf16[32,16,128]{2,1,0:T(8,128)(2,1)}), bf16[32,16,128]{2,1,0:T(8,128)(2,1)S(1)}, u32[]{:S(2)}, u32[]{:S(2)}) async-start(bf16[32,16,128]{2,1,0:T(8,128)(2,1)} %broadcast_in_dim.14), calls=%async_computation.2 | async-start | bytes 262144 | tf_op jit(solution)/shard_map/all_to_all | solution.py:260
  94.6 1.9 %shard_map.121 = (bf16[512,256]{1,0:T(8,128)(2,1)}, bf16[512,512]{1,0:T(8,128)(2,1)}, bf16[128,1024]{1,0:T(8,128)(2,1)}) custom-call(bf16[512,256]{1,0:T(8,128)(2,1)S(1)} %shard_map.119.m3, bf16[64,256]{1,0:T(8,128)(2,1)S(1)} %slice.116.before, bf16[64,256]{1,0:T(8,128)(2,1)S(1)} %slice.117.after, f32[16,256]{1,0:T(8,128)S(1)} %get-tuple-element.40.left, ...), custom_call_target="tpu_custom_call" | custom-call | flops 805306368 | bytes 3932160 | tf_op jit(solution)/shard_map/pallas_call | solution.py:25
  96.5 7.1 %all-to-all-done.2 = bf16[32,16,128]{2,1,0:T(8,128)(2,1)S(1)} async-done(((bf16[32,16,128]{2,1,0:T(8,128)(2,1)}), bf16[32,16,128]{2,1,0:T(8,128)(2,1)S(1)}, u32[]{:S(2)}, u32[]{:S(2)}) %all-to-all-start.2) | async-done | bytes 131104 | tf_op jit(solution)/shard_map/all_to_all | solution.py:260
  103.7 0.7 pad_maximum_fusion
  (45 shorter events, 0.6 us)
Async XLA Ops:
  0.6 25.5 %copy-start.3 = (bf16[1,8,64,256]{3,2,1,0:T(8,128)(2,1)S(1)}, bf16[1,8,64,256]{3,2,1,0:T(8,128)(2,1)}, u32[]{:S(2)}) copy-start(bf16[1,8,64,256]{3,2,1,0:T(8,128)(2,1)} %param.14) | copy-start | bytes 786436
  0.6 25.5 %copy-start.9 = (bf16[1,4,32,256]{3,2,1,0:T(8,128)(2,1)S(1)}, bf16[1,4,32,256]{3,2,1,0:T(8,128)(2,1)}, u32[]{:S(2)}) copy-start(bf16[1,4,32,256]{3,2,1,0:T(8,128)(2,1)} %param.15) | copy-start | bytes 196612
  1.8 5.9 %collective-permute-start = (bf16[8,256]{1,0:T(8,128)(2,1)S(1)}, bf16[8,256]{1,0:T(8,128)(2,1)S(1)}, u32[]{:S(2)}, u32[]{:S(2)}) collective-permute-start(bf16[8,256]{1,0:T(8,128)(2,1)S(1)} %fusion.1), channel_id=1, source_target_pairs={{0,1},{1,0},{2,3},{3,2},{4,5},{5,4},{6,7},{7,6},{8,9},{9,8},{10,11... | collective-permute-start | bytes 12296 | tf_op jit(solution)/shard_map/ppermute | solution.py:221
  7.8 18.2 %collective-permute-start.2 = (bf16[80,256]{1,0:T(8,128)(2,1)S(1)}, bf16[80,256]{1,0:T(8,128)(2,1)S(1)}, u32[]{:S(2)}, u32[]{:S(2)}) collective-permute-start(bf16[80,256]{1,0:T(8,128)(2,1)S(1)} %get-tuple-element.37), channel_id=1, source_target_pairs={{2,4},{6,8},{10,12},{14,16},{18,20},{22,24},{26,28},{4,2},{8,6},{1... | collective-permute-start | bytes 122888 | tf_op jit(solution)/shard_map/ppermute | solution.py:230
  18.3 7.7 %collective-permute-start.1 = (bf16[80,256]{1,0:T(8,128)(2,1)S(1)}, bf16[80,256]{1,0:T(8,128)(2,1)S(1)}, u32[]{:S(2)}, u32[]{:S(2)}) collective-permute-start(bf16[80,256]{1,0:T(8,128)(2,1)S(1)} %get-tuple-element.38), channel_id=1, source_target_pairs={{0,2},{4,6},{8,10},{12,14},{16,18},{20,22},{24,26},{28,30},{2,0},{... | collective-permute-start | bytes 122888 | tf_op jit(solution)/shard_map/ppermute | solution.py:229
  20.9 1.0 copy-start
  22.0 1.0 copy-start.1
  23.0 0.9 copy-start.4
  24.0 0.9 copy-start.5
  24.9 0.7 copy-start.7
  25.6 1.3 %copy-start.8 = (bf16[2304,256]{1,0:T(8,128)(2,1)S(1)}, bf16[2304,256]{1,0:T(8,128)(2,1)}, u32[]{:S(2)}) copy-start(bf16[2304,256]{1,0:T(8,128)(2,1)} %conv.3) | copy-start | bytes 3538948
  30.1 4.6 %collective-permute-start.3 = (bf16[8,32,16,128]{3,2,1,0:T(8,128)(2,1)S(1)}, bf16[8,32,16,128]{3,2,1,0:T(8,128)(2,1)S(1)}, u32[]{:S(2)}, u32[]{:S(2)}) collective-permute-start(bf16[8,32,16,128]{3,2,1,0:T(8,128)(2,1)S(1)} %slice_bitcast_fusion), channel_id=1, source_target_pairs={{0,32},{32,0},{1,33},{33,1},{2,34},{34,2},{3,35},{35,3},{4,36},{36... | collective-permute-start | bytes 3145736 | tf_op jit(solution)/shard_map/ppermute | solution.py:247
  35.9 58.7 %copy-start.2 = (bf16[1024,256]{1,0:T(8,128)(2,1)S(1)}, bf16[1024,256]{1,0:T(8,128)(2,1)}, u32[]{:S(2)}) copy-start(bf16[1024,256]{1,0:T(8,128)(2,1)} %lat4.3) | copy-start | bytes 1572868
  35.9 58.7 %copy-start.6 = (bf16[512,256]{1,0:T(8,128)(2,1)S(1)}, bf16[512,256]{1,0:T(8,128)(2,1)}, u32[]{:S(2)}) copy-start(bf16[512,256]{1,0:T(8,128)(2,1)} %lat3.3) | copy-start | bytes 786436
  35.9 25.7 %all-to-all-start = ((bf16[8,32,16,128]{3,2,1,0:T(8,128)(2,1)}), bf16[8,32,16,128]{3,2,1,0:T(8,128)(2,1)}, u32[]{:S(2)}, u32[]{:S(2)}) async-start(bf16[8,32,16,128]{3,2,1,0:T(8,128)(2,1)} %fusion), calls=%async_computation | async-start | bytes 2097152 | tf_op jit(solution)/shard_map/all_to_all | solution.py:252
  41.8 13.4 %collective-permute-start.4 = (bf16[8,256]{1,0:T(8,128)(2,1)S(1)}, bf16[8,256]{1,0:T(8,128)(2,1)S(1)}, u32[]{:S(2)}, u32[]{:S(2)}) collective-permute-start(bf16[8,256]{1,0:T(8,128)(2,1)S(1)} %fusion.2), channel_id=1, source_target_pairs={{0,1},{1,0},{2,3},{3,2},{4,5},{5,4},{6,7},{7,6},{8,9},{9,8},{10,11... | collective-permute-start | bytes 12296 | tf_op jit(solution)/shard_map/ppermute | solution.py:221
  55.3 20.2 %collective-permute-start.6 = (bf16[80,256]{1,0:T(8,128)(2,1)S(1)}, bf16[80,256]{1,0:T(8,128)(2,1)S(1)}, u32[]{:S(2)}, u32[]{:S(2)}) collective-permute-start(bf16[80,256]{1,0:T(8,128)(2,1)S(1)} %get-tuple-element.35), channel_id=1, source_target_pairs={{2,4},{6,8},{10,12},{14,16},{18,20},{22,24},{26,28},{4,2},{8,6},{1... | collective-permute-start | bytes 122888 | tf_op jit(solution)/shard_map/ppermute | solution.py:230
  57.2 18.3 %collective-permute-start.5 = (bf16[80,256]{1,0:T(8,128)(2,1)S(1)}, bf16[80,256]{1,0:T(8,128)(2,1)S(1)}, u32[]{:S(2)}, u32[]{:S(2)}) collective-permute-start(bf16[80,256]{1,0:T(8,128)(2,1)S(1)} %get-tuple-element.36), channel_id=1, source_target_pairs={{0,2},{4,6},{8,10},{12,14},{16,18},{20,22},{24,26},{28,30},{2,0},{... | collective-permute-start | bytes 122888 | tf_op jit(solution)/shard_map/ppermute | solution.py:229
  63.6 24.3 %all-to-all-start.1 = ((bf16[32,16,128]{2,1,0:T(8,128)(2,1)}), bf16[32,16,128]{2,1,0:T(8,128)(2,1)S(1)}, u32[]{:S(2)}, u32[]{:S(2)}) async-start(bf16[32,16,128]{2,1,0:T(8,128)(2,1)} %reduce_sum.24), calls=%async_computation.1 | async-start | bytes 262144 | tf_op jit(solution)/shard_map/all_to_all | solution.py:253
  88.7 14.9 %all-to-all-start.2 = ((bf16[32,16,128]{2,1,0:T(8,128)(2,1)}), bf16[32,16,128]{2,1,0:T(8,128)(2,1)S(1)}, u32[]{:S(2)}, u32[]{:S(2)}) async-start(bf16[32,16,128]{2,1,0:T(8,128)(2,1)} %broadcast_in_dim.14), calls=%async_computation.2 | async-start | bytes 262144 | tf_op jit(solution)/shard_map/all_to_all | solution.py:260

commit v2 on v1

v2 whole, which is shorter than its diff:
```python
import functools
import math

import jax
import jax.numpy as jnp
from jax import lax
from jax.experimental import pallas as pl
from jax.experimental.pallas import tpu as pltpu
from jax.sharding import PartitionSpec as P

F32 = jnp.float32
BF16 = jnp.bfloat16
ROWS = ("x_hi", "x_lo", "z_hi")
NEAR = ("x_lo", "y_lo", "z_lo")
FAR = ("x_hi", "y_hi", "z_hi")
SHARED = ("x_hi", "x_lo", "z_hi", "z_lo")
LIMIT = 32 * 1024 * 1024
NT = (((1,), (1,)), ((), ()))
TN = (((0,), (0,)), ((), ()))


def dot(lhs, rhs, dims=(((1,), (0,)), ((), ()))):
    return lax.dot_general(lhs, rhs, dims, preferred_element_type=F32)


def place_of_device():
    return lax.axis_index("core"), lax.axis_index("z_lo"), lax.axis_index("z_hi") % 2


def call(kernel, out_shape, scratch, flops, moved, fetched, held=()):
    in_vmem = pl.BlockSpec(memory_space=pltpu.VMEM)
    n, m, k = len(fetched), len(held), len(out_shape)

    def body(*refs):
        sources, refs = refs[:n], refs[n:]
        held_refs, refs = refs[:m], refs[m:]
        outs, refs = refs[:k], refs[k:]
        arrived, refs = refs[:n], refs[n:]
        if n == 0:
            kernel(place_of_device(), *held_refs, *outs, *refs)
            return
        copies = [
            pltpu.make_async_copy(source, target, refs[0].at[i])
            for i, (source, target) in enumerate(zip(sources, arrived))
        ]
        for copy in copies:
            copy.start()
        waits = [copy.wait for copy in copies]
        kernel(place_of_device(), waits, *arrived, *held_refs, *outs, *refs[1:])

    return pl.pallas_call(
        body,
        out_shape=list(out_shape) + [jax.ShapeDtypeStruct(x.shape, x.dtype) for x in fetched],
        in_specs=[pl.BlockSpec(memory_space=pltpu.HBM)] * n + [in_vmem] * m,
        out_specs=[in_vmem] * (k + n),
        scratch_shapes=([pltpu.SemaphoreType.DMA((n,))] if n else []) + scratch,
        compiler_params=pltpu.CompilerParams(vmem_limit_bytes=LIMIT),
        cost_estimate=pl.CostEstimate(flops=flops, bytes_accessed=moved, transcendentals=0),
    )(*[pltpu.with_memory_space_constraint(x, pltpu.HBM) for x in fetched], *held)


def merge_kernel(
    width4, place, waits, c4, lat4, top, c3, lat3, cot, conv, m4_cot,
    m3, col, row_a, row_b, up4,
):
    n4, n5 = c4.shape[0], top.shape[0]
    n3 = c3.shape[0]
    width3, width5 = 2 * width4, width4 // 2
    row = lax.broadcasted_iota(jnp.int32, (n4, n5), 0)
    at = lax.broadcasted_iota(jnp.int32, (n4, n5), 1)
    source = (row // width4 // 2) * width5 + (row % width4) // 2
    pick = jnp.where(source == at, 1.0, 0.0).astype(BF16)
    for wait in waits[:3]:
        wait()
    m4 = dot(c4[...], lat4[...]) + dot(pick, top[...])
    for h in range(2):
        half = m4[:, 128 * h : 128 * h + 128]
        up4[h, pl.ds(0, n4, stride=2), :] = half
        up4[h, pl.ds(1, n4, stride=2), :] = half
    for wait in waits[3:5]:
        wait()
    lat = dot(c3[...], lat3[...])
    for y in range(n3 // width3):
        rows = slice(y * width3, (y + 1) * width3)
        above = slice((y // 2) * width3, (y // 2 + 1) * width3)
        for h in range(2):
            cols = slice(128 * h, 128 * h + 128)
            m3[rows, cols] = (lat[rows, cols] + up4[h, above]).astype(BF16)
    waits[5]()
    edge = jnp.where(place[1] == 0, width3 - 1, 0)
    lines = n3 // width3
    row = lax.broadcasted_iota(jnp.int32, (2 * lines, n3), 0)
    at = lax.broadcasted_iota(jnp.int32, (2 * lines, n3), 1)
    take_cot = jnp.where(at == row * width3 + edge, 1.0, 0.0).astype(BF16)
    take_m3 = jnp.where(at == (row - lines) * width3 + edge, 1.0, 0.0).astype(BF16)
    col[...] = (dot(take_cot, cot[...]) + dot(take_m3, m3[...])).astype(BF16)
    odd = place[2] == 1
    first = pl.multiple_of(jnp.where(odd, 0, n3 - width3), width3)
    second = pl.multiple_of(jnp.where(odd, n3 - width3, 0), width3)
    for start, out in ((first, row_a), (second, row_b)):
        out[:width3] = cot[pl.ds(start, width3)]
        out[width3 : 2 * width3] = m3[pl.ds(start, width3)]
        out[2 * width3 :] = jnp.zeros((2 * lines, out.shape[1]), BF16)
    for wait in waits[6:]:
        wait()


def fill_shifted(place, field, own, row_a, row_b, col, shifted, width):
    n, chans = own.shape
    lines = n // width
    z_lo, odd = place[1], place[2] == 1
    rows = slice(field * width, (field + 1) * width)
    corner = slice(2 * width, 2 * width + 2 * lines)
    line_a, line_b = row_a[rows].astype(F32), row_b[rows].astype(F32)
    ends_a, ends_b = row_a[corner].astype(F32), row_b[corner].astype(F32)
    first, last = field * lines, (field + 1) * lines - 1
    sides = col[...].astype(F32)
    before = jnp.where(odd, ends_a, ends_b)[last : last + 1]
    after = jnp.where(odd, ends_b, ends_a)[first : first + 1]
    sides = [before] + [sides[first + y : first + y + 1] for y in range(lines)] + [after]
    at = lax.broadcasted_iota(jnp.int32, (width, chans), 0)
    to_the_left = jnp.where(z_lo == 1, 1.0, 0.0)
    to_the_right = 1.0 - to_the_left
    for y in range(lines + 2):
        if y == 0:
            line = jnp.where(odd, line_a, line_b)
            shifted[1, :width] = line.astype(BF16)
        elif y == lines + 1:
            line = jnp.where(odd, line_b, line_a)
            shifted[1, y * width :] = line.astype(BF16)
        else:
            line = own[(y - 1) * width : y * width]
            shifted[1, y * width : (y + 1) * width] = line
            line = line.astype(F32)
        rows = slice(y * width, (y + 1) * width)
        left, right = sides[y] * to_the_left, sides[y] * to_the_right
        shifted[0, rows] = jnp.where(at == 0, left, pltpu.roll(line, 1, 0)).astype(BF16)
        shifted[2, rows] = jnp.where(
            at == width - 1, right, pltpu.roll(line, width - 1, 0)
        ).astype(BF16)


def pieces_of(block, each):
    per = each // 16
    return block // per // 2, (block // per) % 2, block % per


def groups_of(y, piece):
    x, z_hi, z_lo = piece // 8, (piece // 2) % 4, piece % 2
    return (x % 2) * 4 + (y % 2) * 2 + z_lo, (x // 2) * 16 + (y // 2) * 4 + z_hi


def grads_kernel(
    width, each, scale, place, cot, conv, m4_cot, c3, c4, m3, row_a, row_b, col,
    m3_grad_b, m4_grad_b, top_grad, term, shifted, sums, sums5,
):
    n3, chans = cot.shape
    n4 = c4.shape[0]
    me = place[0]
    per = each // 16

    def put(first, value):
        value = (value * scale).astype(BF16)
        for k in range(value.shape[0] // 16):
            y, owner, r = pieces_of(first // 16 + k, each)
            slot = jnp.where(me == owner, 0, 1)
            for h in range(2):
                near, far = groups_of(y, h * 16 + r)
                term[slot, near, far] = value[16 * k : 16 * k + 16, 128 * h : 128 * h + 128]

    blank = jnp.zeros((16, 128), BF16)
    for y in range(8):
        for r in range(per, 16):
            for h in range(2):
                near, far = groups_of(y, h * 16 + r)
                for slot in range(2):
                    term[slot, near, far] = blank

    fill_shifted(place, 0, cot, row_a, row_b, col, shifted, width)

    def cot_at(a, b):
        return shifted[2 - b, (2 - a) * width : (2 - a) * width + n3]

    total = None
    for a in range(3):
        for b in range(3):
            tap = 3 * a + b
            weight = conv[tap * chans : (tap + 1) * chans]
            part = dot(cot_at(a, b), weight, NT)
            total = part if total is None else total + part
    m3_grad_b[...] = total.astype(BF16)
    for y in range(n4 // (width // 2)):
        pair = total[2 * y * width : (2 * y + 1) * width] + total[(2 * y + 1) * width : (2 * y + 2) * width]
        sums[0, y * width : (y + 1) * width] = pair[:, :128]
        sums[1, y * width : (y + 1) * width] = pair[:, 128:]
    for h in range(2):
        cols = slice(128 * h, 128 * h + 128)
        m4_grad = (
            m4_cot[:, cols].astype(F32)
            + sums[h, pl.ds(0, n4, stride=2), :]
            + sums[h, pl.ds(1, n4, stride=2), :]
        )
        m4_grad_b[:, cols] = m4_grad.astype(BF16)
        half = width // 2
        for y in range(n4 // width):
            sums5[h, y * half : (y + 1) * half] = (
                m4_grad[2 * y * half : (2 * y + 1) * half]
                + m4_grad[(2 * y + 1) * half : (2 * y + 2) * half]
            )
        n5 = n4 // 4
        top_grad[:, cols] = (
            sums5[h, pl.ds(0, n5, stride=2), :] + sums5[h, pl.ds(1, n5, stride=2), :]
        ).astype(BF16)

    depth3, depth4 = c3.shape[1], c4.shape[1]
    put(0, dot(c3[...], m3_grad_b[...], TN))
    put(depth3, dot(c4[...], m4_grad_b[...], TN))
    m3_t = m3[...].T
    for a in range(3):
        for b in range(3):
            tap = 3 * a + b
            put(depth3 + depth4 + tap * chans, dot(m3_t, cot_at(a, b)))


def outputs_kernel(
    width, place, conv, lat3, lat4, m3, row_a, row_b, col, m3_grad_b, m4_grad_b,
    p3, c3_grad, c4_grad, shifted,
):
    n3, chans = m3.shape
    fill_shifted(place, 1, m3, row_a, row_b, col, shifted, width)
    total = None
    for a in range(3):
        for b in range(3):
            tap = 3 * a + b
            part = dot(shifted[b, a * width : a * width + n3], conv[tap * chans : (tap + 1) * chans])
            total = part if total is None else total + part
    p3[...] = total.astype(BF16)
    c3_grad[...] = dot(m3_grad_b[...], lat3[...], NT).astype(BF16)
    c4_grad[...] = dot(m4_grad_b[...], lat4[...], NT).astype(BF16)


def shape_of(*dims):
    return jax.ShapeDtypeStruct(dims, BF16)


def run_merge(width, c3, c4, top, lat3, lat4, cot, conv, m4_cot):
    n3, n4, chans = c3.shape[0], c4.shape[0], lat3.shape[1]
    lines = n3 // width
    border = shape_of(2 * width + 2 * lines, chans)
    return call(
        functools.partial(merge_kernel, width // 2),
        [shape_of(n3, chans), shape_of(2 * lines, chans), border, border],
        [pltpu.VMEM((2, 2 * n4, 128), F32)],
        2 * chans * (c3.size + c4.size),
        2 * (c3.size + c4.size + lat3.size + lat4.size + 2 * cot.size + conv.size),
        (c4, lat4, top, c3, lat3, cot, conv, m4_cot),
    )


def run_grads(width, each, scale, cot, conv, m4_cot, c3, c4, m3, row_a, row_b, col):
    n3, chans = cot.shape
    n4 = c4.shape[0]
    return call(
        functools.partial(grads_kernel, width, each, scale),
        [
            shape_of(n3, chans),
            shape_of(n4, chans),
            shape_of(n4 // 4, chans),
            shape_of(2, 8, 32, 16, 128),
        ],
        [
            pltpu.VMEM((3, n3 + 2 * width, chans), BF16),
            pltpu.VMEM((2, n3 // 2, 128), F32),
            pltpu.VMEM((2, n4 // 2, 128), F32),
        ],
        2 * chans * (c3.size + c4.size + 2 * 9 * n3 * chans),
        2 * (c3.size + c4.size + 2 * conv.size),
        (),
        (cot, conv, m4_cot, c3, c4, m3, row_a, row_b, col),
    )


def run_outputs(width, conv, lat3, lat4, m3, row_a, row_b, col, m3_grad_b, m4_grad_b):
    n3, chans = m3.shape
    n4 = m4_grad_b.shape[0]
    return call(
        functools.partial(outputs_kernel, width),
        [shape_of(n3, chans), shape_of(n3, lat3.shape[0]), shape_of(n4, lat4.shape[0])],
        [pltpu.VMEM((3, n3 + 2 * width, chans), BF16)],
        2 * chans * (n3 * lat3.shape[0] + n4 * lat4.shape[0] + 9 * n3 * chans),
        4 * (n3 * lat3.shape[0] + n4 * lat4.shape[0] + conv.size),
        (),
        (conv, lat3, lat4, m3, row_a, row_b, col, m3_grad_b, m4_grad_b),
    )


def swap_borders(col, row_a, row_b):
    col = lax.ppermute(col, "z_lo", [(0, 1), (1, 0)])
    n_rows = lax.axis_size(ROWS)
    pairs = [(i, i + 1) for i in range(0, n_rows - 1, 2)]
    between = [(i, i + 1) for i in range(1, n_rows - 1, 2)]
    start = (row_a.shape[0] - col.shape[0], 0)
    row_a = lax.dynamic_update_slice(row_a, col, start)
    row_b = lax.dynamic_update_slice(row_b, col, start)
    row_a = lax.ppermute(row_a, ROWS, pairs + [(j, i) for i, j in pairs])
    row_b = lax.ppermute(row_b, ROWS, between + [(j, i) for i, j in between])
    return row_a, row_b, col


def add_kernel(count, *refs):
    parts, out = refs[:-1], refs[-1]
    total = None
    for part in parts:
        for i in range(part.shape[0]):
            value = part[i].astype(F32)
            total = value if total is None else total + value
    total = total.astype(BF16)
    if count is None:
        out[...] = total
    else:
        for i in range(count):
            out[i] = total


def add_up(*parts, count=None):
    shape = parts[0].shape[1:]
    in_vmem = pl.BlockSpec(memory_space=pltpu.VMEM)
    return pl.pallas_call(
        functools.partial(add_kernel, count),
        out_shape=shape_of(*shape) if count is None else shape_of(count, *shape),
        in_specs=[in_vmem] * len(parts),
        out_specs=in_vmem,
        compiler_params=pltpu.CompilerParams(vmem_limit_bytes=LIMIT),
        cost_estimate=pl.CostEstimate(
            flops=sum(p.size for p in parts),
            bytes_accessed=2 * sum(p.size for p in parts),
            transcendentals=0,
        ),
    )(*parts)


def add_grads(term, each):
    _, near, far, rows, cols = term.shape
    got = lax.ppermute(term[1], "core", [(0, 1), (1, 0)])
    part = add_up(term[:1].reshape(1, -1, cols), got.reshape(1, -1, cols))
    part = lax.all_to_all(part.reshape(near, far * rows, cols), NEAR, 0, 0, tiled=True)
    part = add_up(part)
    part = lax.all_to_all(part.reshape(far, rows, cols), FAR, 0, 0, tiled=True)
    part = add_up(part, count=lax.axis_size(SHARED))
    part = lax.all_to_all(part, SHARED, 0, 0, tiled=True)
    halves = part.reshape(2, -1, cols)[:, :each].astype(F32)
    return jnp.concatenate([halves[0], halves[1]], axis=1)


def shards(c3, c4, top_down, lat3_weight, lat4_weight, conv_weight, p3_cot, m4_cot):
    count, height, width, depth3 = c3.shape
    depth4 = c4.shape[3]
    chans = conv_weight.shape[1]
    n3 = height * width
    n4 = n3 // 4
    n5 = n4 // 4
    stacked = depth3 + depth4 + 9 * chans
    owners = lax.axis_size(("y_hi", "y_lo", "core"))
    each = stacked // owners
    total_pixels = n3 * owners * lax.axis_size(SHARED)
    scale = 1.0 / math.sqrt(total_pixels)

    m3, col, row_a, row_b, *fetched = run_merge(
        width, c3.reshape(n3, depth3), c4.reshape(n4, depth4), top_down.reshape(n5, chans),
        lat3_weight, lat4_weight, p3_cot.reshape(n3, chans), conv_weight, m4_cot.reshape(n4, chans),
    )
    c4_v, lat4_v, _, c3_v, lat3_v, cot_v, conv_v, m4_cot_v = fetched
    borders = swap_borders(col, row_a, row_b)
    m3_grad_b, m4_grad_b, top_grad, term = run_grads(
        width, each, scale, cot_v, conv_v, m4_cot_v, c3_v, c4_v, m3, *borders
    )
    weight_grads = add_grads(term, each)
    p3, c3_grad, c4_grad = run_outputs(
        width, conv_v, lat3_v, lat4_v, m3, *borders, m3_grad_b, m4_grad_b
    )
    return (
        p3.reshape(count, height, width, chans),
        c3_grad.reshape(count, height, width, depth3),
        c4_grad.reshape(count, height // 2, width // 2, depth4),
        top_grad.reshape(top_down.shape),
        weight_grads,
    )


def solution(mesh):
    split = jax.sharding.Mesh(
        mesh.devices.reshape(4, 2, 2, 2, 2, 4, 2),
        ("y_hi", "y_lo", "core", "x_hi", "x_lo", "z_hi", "z_lo"),
    )
    owners = ("y_hi", "y_lo", "core")
    tiles = P(owners, ROWS, "z_lo", None)
    return jax.shard_map(
        shards,
        mesh=split,
        in_specs=(tiles, tiles, tiles, P(), P(), P(), tiles, tiles),
        out_specs=(tiles, tiles, tiles, tiles, P(owners, None)),
        check_vma=False,
    )
```

time: 105 us -> 94.8 us (0.903)
  the two profiles are of different devices: /device:TPU:2 before, /device:TPU:8 now
where the time goes in v2:
time: 94.8 us; the launch traced here: 94.5 us
  blocking collectives  45.8 us (48%)
  starting transfers between devices  23.1 us (24%)
  waiting for transfers between devices  15 us (16%)
  Pallas kernels  8.75 us (9%)
    all_to_all x1, blocking collectives, add_grads(): part = lax.all_to_all(part.reshape(far, rows, cols), FAR, 0, 0, tiled=True)  24.3 us
    all_to_all x1, blocking collectives, add_grads(): lax.all_to_all(part.reshape(near, far * rows, cols), NEAR, 0, 0, tiled=True)  21.5 us
    ppermute x1, starting transfers between devices, swap_borders(): row_a = lax.ppermute(row_a, ROWS, pairs + [(j, i) for i, j in pairs])  12.4 us
    all_to_all x1, waiting for transfers between devices, add_grads(): part = lax.all_to_all(part, SHARED, 0, 0, tiled=True)  8.43 us
    pallas_call x3, Pallas kernels, call(): pl.pallas_call(body, out_shape=list(out_shape) + [jax.ShapeDtypeStruct(x....  7.68 us
    ppermute x1, starting transfers between devices, swap_borders(): col = lax.ppermute(col, 'z_lo', [(0, 1), (1, 0)])  4.28 us
    all_to_all x1, starting transfers between devices, add_grads(): part = lax.all_to_all(part, SHARED, 0, 0, tiled=True)  3.86 us
    ppermute x1, waiting for transfers between devices, add_grads(): got = lax.ppermute(term[1], 'core', [(0, 1), (1, 0)])  2.63 us
  transfers between devices with their start and end apart: 5, of which 4 were waited for; matrix products, arithmetic and copies ran while one was open for 0% of the time, Pallas kernels for 2%

profile of v2, /device:TPU:8, one launch (start us, length us, event | category | flops | bytes accessed | tf_op | source)
XLA Modules:
  0.0 94.5 jit_solution(9440147234930956938)
XLA Ops:
  0.6 2.8 %shard_map.119 = (bf16[512,256]{1,0:T(8,128)(2,1)S(1)}, bf16[16,256]{1,0:T(8,128)(2,1)S(1)}, bf16[144,256]{1,0:T(8,128)(2,1)S(1)}, bf16[144,256]{1,0:T(8,128)(2,...) custom-call(bf16[128,1024]{1,0:T(8,128)(2,1)} %bitcast.26, ...), custom_call_target="tpu_custom_call" | custom-call | flops 201326592 | bytes 3276800 | tf_op jit(solution)/shard_map/pallas_call | solution.py:51
  3.4 4.3 %collective-permute-start = (bf16[16,256]{1,0:T(8,128)(2,1)S(1)}, bf16[16,256]{1,0:T(8,128)(2,1)S(1)}, u32[]{:S(2)}, u32[]{:S(2)}) collective-permute-start(bf16[16,256]{1,0:T(8,128)(2,1)S(1)} %get-tuple-element.28), channel_id=1, source_target_pairs={{0,1},{1,0},{2,3},{3,2},{4,5},{5,4},{6,7},{7,6},{8,9},{9,8},{10,11... | collective-permute-start | bytes 24584 | tf_op jit(solution)/shard_map/ppermute | solution.py:298
  7.7 1.6 %collective-permute-done.refs_8_.refs_6_ = bf16[16,256]{1,0:T(8,128)(2,1)S(1)} collective-permute-done((bf16[16,256]{1,0:T(8,128)(2,1)S(1)}, bf16[16,256]{1,0:T(8,128)(2,1)S(1)}, u32[]{:S(2)}, u32[]{:S(2)}) %collective-permute-start) | collective-permute-done | bytes 8224 | tf_op jit(solution)/shard_map/ppermute | solution.py:298
  9.3 0.7 collective-permute-start.2
  10.0 12.4 %collective-permute-start.1 = (bf16[144,256]{1,0:T(8,128)(2,1)S(1)}, bf16[144,256]{1,0:T(8,128)(2,1)S(1)}, u32[]{:S(2)}, u32[]{:S(2)}) collective-permute-start(bf16[144,256]{1,0:T(8,128)(2,1)S(1)} %get-tuple-element.46), channel_id=1, source_target_pairs={{0,2},{4,6},{8,10},{12,14},{16,18},{20,22},{24,26},{28,30},{2,0},{... | collective-permute-start | bytes 221192 | tf_op jit(solution)/shard_map/ppermute | solution.py:305
  22.4 0.0 collective-permute-done.2.refs_7_.refs_5_
  22.4 2.3 %collective-permute-done.1.refs_6_.refs_4_ = bf16[144,256]{1,0:T(8,128)(2,1)S(1)} collective-permute-done((bf16[144,256]{1,0:T(8,128)(2,1)S(1)}, bf16[144,256]{1,0:T(8,128)(2,1)S(1)}, u32[]{:S(2)}, u32[]{:S(2)}) %collective-permute-start.1) | collective-permute-done | bytes 73760 | tf_op jit(solution)/shard_map/ppermute | solution.py:305
  24.7 3.0 %shard_map.120 = (bf16[512,256]{1,0:T(8,128)(2,1)S(1)}, bf16[128,256]{1,0:T(8,128)(2,1)S(1)}, bf16[32,256]{1,0:T(8,128)(2,1)}, bf16[2,8,32,16,128]{4,3,2,1,0:T(8,128)(2,1)S(1)}) custom-call(bf16[512,256]{1,0:T(8,128)(2,1)S(1)} %get-tuple-element.30.refs_0_, bf16[2304,256]{1,0:T(8,128)(2,1)S(1)} %get-tuple-element.23.refs_1_.refs_0_, ...), custom_call_target="tpu_custom_call" | custom-call | flops 1409286144 | bytes 3145728 | tf_op jit(solution)/shard_map/pallas_call | solution.py:51
  27.7 0.4 slice_bitcast_fusion
  28.0 1.9 %collective-permute-start.3 = (bf16[8,32,16,128]{3,2,1,0:T(8,128)(2,1)S(1)}, bf16[8,32,16,128]{3,2,1,0:T(8,128)(2,1)S(1)}, u32[]{:S(2)}, u32[]{:S(2)}) collective-permute-start(bf16[8,32,16,128]{3,2,1,0:T(8,128)(2,1)S(1)} %get-tuple-element.41), channel_id=1, source_target_pairs={{0,32},{32,0},{1,33},{33,1},{2,34},{34,2},{3,35},{35,3},{4,36},{36... | collective-permute-start | bytes 3145736 | tf_op jit(solution)/shard_map/ppermute | solution.py:344
  30.0 2.6 %collective-permute-done.3 = bf16[8,32,16,128]{3,2,1,0:T(8,128)(2,1)S(1)} collective-permute-done((bf16[8,32,16,128]{3,2,1,0:T(8,128)(2,1)S(1)}, bf16[8,32,16,128]{3,2,1,0:T(8,128)(2,1)S(1)}, u32[]{:S(2)}, u32[]{:S(2)}) %collective-permute-start.3) | collective-permute-done | bytes 1048608 | tf_op jit(solution)/shard_map/ppermute | solution.py:344
  32.6 0.2 shard_map.122
  32.8 21.5 %all_to_all.15.refs_0_ = bf16[8,512,128]{2,1,0:T(8,128)(2,1)S(1)} all-to-all(bf16[8,512,128]{2,1,0:T(8,128)(2,1)S(1)} %bitcast.20), channel_id=1, replica_groups=mesh['y_hi'=4,'y_lo'=2,'core'=2,'x_hi'=2,'x_lo'=2,'z_hi'=4,'z_lo'=2] {'x..., dimensions={0} | all-to-all | bytes 2097152 | tf_op jit(solution)/shard_map/all_to_all | solution.py:346
  54.4 0.1 shard_map.123
  54.5 24.3 %all_to_all.16.refs_0_ = bf16[32,16,128]{2,1,0:T(8,128)(2,1)S(1)} all-to-all(bf16[32,16,128]{2,1,0:T(8,128)(2,1)S(1)} %bitcast.23), channel_id=1, replica_groups=mesh['y_hi'=4,'y_lo'=2,'core'=2,'x_hi'=2,'x_lo'=2,'z_hi'=4,'z_lo'=2] {'x..., dimensions={0} | all-to-all | bytes 262144 | tf_op jit(solution)/shard_map/all_to_all | solution.py:348
  78.8 0.7 shard_map.124
  79.5 3.9 %all-to-all-start.2 = ((bf16[32,16,128]{2,1,0:T(8,128)(2,1)}), bf16[32,16,128]{2,1,0:T(8,128)(2,1)S(1)}, u32[]{:S(2)}, u32[]{:S(2)}) async-start(bf16[32,16,128]{2,1,0:T(8,128)(2,1)} %shard_map.124), calls=%async_computation.2 | async-start | bytes 262144 | tf_op jit(solution)/shard_map/all_to_all | solution.py:350
  83.4 1.9 %shard_map.121 = (bf16[512,256]{1,0:T(8,128)(2,1)}, bf16[512,512]{1,0:T(8,128)(2,1)}, bf16[128,1024]{1,0:T(8,128)(2,1)}) custom-call(bf16[2304,256]{1,0:T(8,128)(2,1)S(1)} %get-tuple-element.23.refs_1_.refs_0_, bf16[512,256]{1,0:T(8,128)(2,1)S(1)} %get-tuple-element.24.refs_1_, bf16[1024,256]{1,0:T(8,128)(2,1)S(1)} %get-tuple-element.25.refs_2_, ...), custom_call_target="tpu_custom_call" | custom-call | flops 805306368 | bytes 3932160 | tf_op jit(solution)/shard_map/pallas_call | solution.py:51
  85.3 8.4 %all-to-all-done.2 = bf16[32,16,128]{2,1,0:T(8,128)(2,1)S(1)} async-done(((bf16[32,16,128]{2,1,0:T(8,128)(2,1)}), bf16[32,16,128]{2,1,0:T(8,128)(2,1)S(1)}, u32[]{:S(2)}, u32[]{:S(2)}) %all-to-all-start.2) | async-done | bytes 131104 | tf_op jit(solution)/shard_map/all_to_all | solution.py:350
  93.7 0.7 pad_maximum_fusion
  (3 shorter events, 0.0 us)
Async XLA Ops:
  3.4 5.9 %collective-permute-start = (bf16[16,256]{1,0:T(8,128)(2,1)S(1)}, bf16[16,256]{1,0:T(8,128)(2,1)S(1)}, u32[]{:S(2)}, u32[]{:S(2)}) collective-permute-start(bf16[16,256]{1,0:T(8,128)(2,1)S(1)} %get-tuple-element.28), channel_id=1, source_target_pairs={{0,1},{1,0},{2,3},{3,2},{4,5},{5,4},{6,7},{7,6},{8,9},{9,8},{10,11... | collective-permute-start | bytes 24584 | tf_op jit(solution)/shard_map/ppermute | solution.py:298
  9.3 13.0 %collective-permute-start.2 = (bf16[144,256]{1,0:T(8,128)(2,1)S(1)}, bf16[144,256]{1,0:T(8,128)(2,1)S(1)}, u32[]{:S(2)}, u32[]{:S(2)}) collective-permute-start(bf16[144,256]{1,0:T(8,128)(2,1)S(1)} %get-tuple-element.45), channel_id=1, source_target_pairs={{2,4},{6,8},{10,12},{14,16},{18,20},{22,24},{26,28},{4,2},{8,6},{1... | collective-permute-start | bytes 221192 | tf_op jit(solution)/shard_map/ppermute | solution.py:306
  10.0 14.7 %collective-permute-start.1 = (bf16[144,256]{1,0:T(8,128)(2,1)S(1)}, bf16[144,256]{1,0:T(8,128)(2,1)S(1)}, u32[]{:S(2)}, u32[]{:S(2)}) collective-permute-start(bf16[144,256]{1,0:T(8,128)(2,1)S(1)} %get-tuple-element.46), channel_id=1, source_target_pairs={{0,2},{4,6},{8,10},{12,14},{16,18},{20,22},{24,26},{28,30},{2,0},{... | collective-permute-start | bytes 221192 | tf_op jit(solution)/shard_map/ppermute | solution.py:305
  28.0 4.6 %collective-permute-start.3 = (bf16[8,32,16,128]{3,2,1,0:T(8,128)(2,1)S(1)}, bf16[8,32,16,128]{3,2,1,0:T(8,128)(2,1)S(1)}, u32[]{:S(2)}, u32[]{:S(2)}) collective-permute-start(bf16[8,32,16,128]{3,2,1,0:T(8,128)(2,1)S(1)} %get-tuple-element.41), channel_id=1, source_target_pairs={{0,32},{32,0},{1,33},{33,1},{2,34},{34,2},{3,35},{35,3},{4,36},{36... | collective-permute-start | bytes 3145736 | tf_op jit(solution)/shard_map/ppermute | solution.py:344
  79.5 14.2 %all-to-all-start.2 = ((bf16[32,16,128]{2,1,0:T(8,128)(2,1)}), bf16[32,16,128]{2,1,0:T(8,128)(2,1)S(1)}, u32[]{:S(2)}, u32[]{:S(2)}) async-start(bf16[32,16,128]{2,1,0:T(8,128)(2,1)} %shard_map.124), calls=%async_computation.2 | async-start | bytes 262144 | tf_op jit(solution)/shard_map/all_to_all | solution.py:350

commit v3 on v2

--- a/solution.py
+++ b/solution.py
@@ -10,10 +10,10 @@
 
 F32 = jnp.float32
 BF16 = jnp.bfloat16
-ROWS = ("x_hi", "x_lo", "z_hi")
-NEAR = ("x_lo", "y_lo", "z_lo")
-FAR = ("x_hi", "y_hi", "z_hi")
-SHARED = ("x_hi", "x_lo", "z_hi", "z_lo")
+ROWS = ("x", "z_hi")
+OWNERS = ("y", "core")
+SHARED = ("x", "z_hi", "z_lo")
+SIZES = {"x": 4, "y": 8, "z": 8}
 LIMIT = 32 * 1024 * 1024
 NT = (((1,), (1,)), ((), ()))
 TN = (((0,), (0,)), ((), ()))
@@ -145,9 +145,23 @@
     return block // per // 2, (block // per) % 2, block % per
 
 
-def groups_of(y, piece):
-    x, z_hi, z_lo = piece // 8, (piece // 2) % 4, piece % 2
-    return (x % 2) * 4 + (y % 2) * 2 + z_lo, (x // 2) * 16 + (y // 2) * 4 + z_hi
+def groups_of(core, x, y, z):
+    x, y, z = (x + core) % SIZES["x"], (y + core) % SIZES["y"], (z + core) % SIZES["z"]
+    return (x % 2) * 4 + (y % 2) * 2 + z % 2, (x // 2) * 16 + (y // 2) * 4 + z // 2
+
+
+def group_lists():
+    near, far = {}, {}
+    index = 0
+    for y in range(SIZES["y"]):
+        for core in range(2):
+            for x in range(SIZES["x"]):
+                for z in range(SIZES["z"]):
+                    in_near, in_far = groups_of(core, x, y, z)
+                    near.setdefault((core, in_far), [None] * 8)[in_near] = index
+                    far.setdefault((core, in_near), [None] * 32)[in_far] = index
+                    index += 1
+    return list(near.values()), list(far.values())
 
 
 def grads_kernel(
@@ -165,16 +179,16 @@
             y, owner, r = pieces_of(first // 16 + k, each)
             slot = jnp.where(me == owner, 0, 1)
             for h in range(2):
-                near, far = groups_of(y, h * 16 + r)
+                p = h * 16 + r
+                near, far = groups_of(owner, p // SIZES["z"], y, p % SIZES["z"])
                 term[slot, near, far] = value[16 * k : 16 * k + 16, 128 * h : 128 * h + 128]
 
     blank = jnp.zeros((16, 128), BF16)
-    for y in range(8):
-        for r in range(per, 16):
-            for h in range(2):
-                near, far = groups_of(y, h * 16 + r)
-                for slot in range(2):
-                    term[slot, near, far] = blank
+    for y in range(SIZES["y"]):
+        for p in [h * 16 + r for r in range(per, 16) for h in range(2)]:
+            for owner in range(2):
+                near, far = groups_of(owner, p // SIZES["z"], y, p % SIZES["z"])
+                term[jnp.where(me == owner, 0, 1), near, far] = blank
 
     fill_shifted(place, 0, cot, row_a, row_b, col, shifted, width)
 
@@ -340,12 +354,14 @@
 
 
 def add_grads(term, each):
+    everyone = OWNERS + SHARED
+    near_groups, far_groups = group_lists()
     _, near, far, rows, cols = term.shape
     got = lax.ppermute(term[1], "core", [(0, 1), (1, 0)])
     part = add_up(term[:1].reshape(1, -1, cols), got.reshape(1, -1, cols))
-    part = lax.all_to_all(part.reshape(near, far * rows, cols), NEAR, 0, 0, tiled=True)
+    part = lax.all_to_all(part.reshape(near, far * rows, cols), everyone, 0, 0, axis_index_groups=near_groups, tiled=True)
     part = add_up(part)
-    part = lax.all_to_all(part.reshape(far, rows, cols), FAR, 0, 0, tiled=True)
+    part = lax.all_to_all(part.reshape(far, rows, cols), everyone, 0, 0, axis_index_groups=far_groups, tiled=True)
     part = add_up(part, count=lax.axis_size(SHARED))
     part = lax.all_to_all(part, SHARED, 0, 0, tiled=True)
     halves = part.reshape(2, -1, cols)[:, :each].astype(F32)
@@ -360,7 +376,7 @@
     n4 = n3 // 4
     n5 = n4 // 4
     stacked = depth3 + depth4 + 9 * chans
-    owners = lax.axis_size(("y_hi", "y_lo", "core"))
+    owners = lax.axis_size(OWNERS)
     each = stacked // owners
     total_pixels = n3 * owners * lax.axis_size(SHARED)
     scale = 1.0 / math.sqrt(total_pixels)
@@ -389,15 +405,13 @@
 
 def solution(mesh):
     split = jax.sharding.Mesh(
-        mesh.devices.reshape(4, 2, 2, 2, 2, 4, 2),
-        ("y_hi", "y_lo", "core", "x_hi", "x_lo", "z_hi", "z_lo"),
-    )
-    owners = ("y_hi", "y_lo", "core")
-    tiles = P(owners, ROWS, "z_lo", None)
+        mesh.devices.reshape(8, 2, 4, 4, 2), ("y", "core", "x", "z_hi", "z_lo")
+    )
+    tiles = P(OWNERS, ROWS, "z_lo", None)
     return jax.shard_map(
         shards,
         mesh=split,
         in_specs=(tiles, tiles, tiles, P(), P(), P(), tiles, tiles),
-        out_specs=(tiles, tiles, tiles, tiles, P(owners, None)),
+        out_specs=(tiles, tiles, tiles, tiles, P(OWNERS, None)),
         check_vma=False,
     )

time: 94.8 us -> 91.9 us (0.969)
  the two profiles are of different devices: /device:TPU:8 before, /device:TPU:1 now
where the time goes in v3:
time: 91.9 us; the launch traced here: 91.6 us
  blocking collectives  40.9 us (45%)
  starting transfers between devices  27.2 us (30%)
  waiting for transfers between devices  12.9 us (14%)
  Pallas kernels  8.75 us (10%)
    all_to_all x1, blocking collectives, add_grads(): lax.all_to_all(part.reshape(far, rows, cols), everyone, 0, 0, axis_index_...  22.4 us
    all_to_all x1, blocking collectives, add_grads(): lax.all_to_all(part.reshape(near, far * rows, cols), everyone, 0, 0, axis...  18.5 us
    ppermute x1, starting transfers between devices, swap_borders(): row_a = lax.ppermute(row_a, ROWS, pairs + [(j, i) for i, j in pairs])  11.5 us
    pallas_call x3, Pallas kernels, call(): pl.pallas_call(body, out_shape=list(out_shape) + [jax.ShapeDtypeStruct(x....  7.68 us
    all_to_all x1, waiting for transfers between devices, add_grads(): part = lax.all_to_all(part, SHARED, 0, 0, tiled=True)  7.55 us
    all_to_all x1, starting transfers between devices, add_grads(): part = lax.all_to_all(part, SHARED, 0, 0, tiled=True)  5.59 us
    ppermute x1, starting transfers between devices, swap_borders(): col = lax.ppermute(col, 'z_lo', [(0, 1), (1, 0)])  4.83 us
    ppermute x1, starting transfers between devices, add_grads(): got = lax.ppermute(term[1], 'core', [(0, 1), (1, 0)])  4.58 us
  transfers between devices with their start and end apart: 5, of which 4 were waited for; matrix products, arithmetic and copies ran while one was open for 0% of the time, Pallas kernels for 2%

profile of v3, /device:TPU:1, one launch (start us, length us, event | category | flops | bytes accessed | tf_op | source)
XLA Modules:
  0.0 91.6 jit_solution(984517550345736168)
XLA Ops:
  0.6 2.8 %shard_map.119 = (bf16[512,256]{1,0:T(8,128)(2,1)S(1)}, bf16[16,256]{1,0:T(8,128)(2,1)S(1)}, bf16[144,256]{1,0:T(8,128)(2,1)S(1)}, bf16[144,256]{1,0:T(8,128)(2,...) custom-call(bf16[128,1024]{1,0:T(8,128)(2,1)} %bitcast.26, ...), custom_call_target="tpu_custom_call" | custom-call | flops 201326592 | bytes 3276800 | tf_op jit(solution)/shard_map/pallas_call | solution.py:51
  3.4 4.8 %collective-permute-start = (bf16[16,256]{1,0:T(8,128)(2,1)S(1)}, bf16[16,256]{1,0:T(8,128)(2,1)S(1)}, u32[]{:S(2)}, u32[]{:S(2)}) collective-permute-start(bf16[16,256]{1,0:T(8,128)(2,1)S(1)} %get-tuple-element.28), channel_id=1, source_target_pairs={{0,1},{1,0},{2,3},{3,2},{4,5},{5,4},{6,7},{7,6},{8,9},{9,8},{10,11... | collective-permute-start | bytes 24584 | tf_op jit(solution)/shard_map/ppermute | solution.py:312
  8.3 1.0 %collective-permute-done.refs_8_.refs_6_ = bf16[16,256]{1,0:T(8,128)(2,1)S(1)} collective-permute-done((bf16[16,256]{1,0:T(8,128)(2,1)S(1)}, bf16[16,256]{1,0:T(8,128)(2,1)S(1)}, u32[]{:S(2)}, u32[]{:S(2)}) %collective-permute-start) | collective-permute-done | bytes 8224 | tf_op jit(solution)/shard_map/ppermute | solution.py:312
  9.3 0.7 collective-permute-start.2
  9.9 11.5 %collective-permute-start.1 = (bf16[144,256]{1,0:T(8,128)(2,1)S(1)}, bf16[144,256]{1,0:T(8,128)(2,1)S(1)}, u32[]{:S(2)}, u32[]{:S(2)}) collective-permute-start(bf16[144,256]{1,0:T(8,128)(2,1)S(1)} %get-tuple-element.46), channel_id=1, source_target_pairs={{0,2},{4,6},{8,10},{12,14},{16,18},{20,22},{24,26},{28,30},{2,0},{... | collective-permute-start | bytes 221192 | tf_op jit(solution)/shard_map/ppermute | solution.py:319
  21.5 0.0 collective-permute-done.2.refs_7_.refs_5_
  21.5 2.0 %collective-permute-done.1.refs_6_.refs_4_ = bf16[144,256]{1,0:T(8,128)(2,1)S(1)} collective-permute-done((bf16[144,256]{1,0:T(8,128)(2,1)S(1)}, bf16[144,256]{1,0:T(8,128)(2,1)S(1)}, u32[]{:S(2)}, u32[]{:S(2)}) %collective-permute-start.1) | collective-permute-done | bytes 73760 | tf_op jit(solution)/shard_map/ppermute | solution.py:319
  23.5 3.0 %shard_map.120 = (bf16[512,256]{1,0:T(8,128)(2,1)S(1)}, bf16[128,256]{1,0:T(8,128)(2,1)S(1)}, bf16[32,256]{1,0:T(8,128)(2,1)}, bf16[2,8,32,16,128]{4,3,2,1,0:T(8,128)(2,1)S(1)}) custom-call(bf16[512,256]{1,0:T(8,128)(2,1)S(1)} %get-tuple-element.30.refs_0_, bf16[2304,256]{1,0:T(8,128)(2,1)S(1)} %get-tuple-element.23.refs_1_.refs_0_, ...), custom_call_target="tpu_custom_call" | custom-call | flops 1409286144 | bytes 3145728 | tf_op jit(solution)/shard_map/pallas_call | solution.py:51
  26.5 0.4 slice_bitcast_fusion
  26.9 4.6 %collective-permute-start.3 = (bf16[8,32,16,128]{3,2,1,0:T(8,128)(2,1)S(1)}, bf16[8,32,16,128]{3,2,1,0:T(8,128)(2,1)S(1)}, u32[]{:S(2)}, u32[]{:S(2)}) collective-permute-start(bf16[8,32,16,128]{3,2,1,0:T(8,128)(2,1)S(1)} %get-tuple-element.41), channel_id=1, source_target_pairs={{0,32},{32,0},{1,33},{33,1},{2,34},{34,2},{3,35},{35,3},{4,36},{36... | collective-permute-start | bytes 3145736 | tf_op jit(solution)/shard_map/ppermute | solution.py:360
  31.5 2.3 %collective-permute-done.3 = bf16[8,32,16,128]{3,2,1,0:T(8,128)(2,1)S(1)} collective-permute-done((bf16[8,32,16,128]{3,2,1,0:T(8,128)(2,1)S(1)}, bf16[8,32,16,128]{3,2,1,0:T(8,128)(2,1)S(1)}, u32[]{:S(2)}, u32[]{:S(2)}) %collective-permute-start.3) | collective-permute-done | bytes 1048608 | tf_op jit(solution)/shard_map/ppermute | solution.py:360
  33.7 0.2 shard_map.122
  34.0 18.5 %all_to_all.15.refs_0_ = bf16[8,512,128]{2,1,0:T(8,128)(2,1)S(1)} all-to-all(bf16[8,512,128]{2,1,0:T(8,128)(2,1)S(1)} %bitcast.20), channel_id=1, replica_groups={{0,1,64,65,8,9,72,73},{2,3,66,67,10,11,74,75},{4,5,68,69,12,13,76,77},{..., dimensions={0} | all-to-all | bytes 2097152 | tf_op jit(solution)/shard_map/all_to_all | solution.py:362
  52.5 0.1 shard_map.123
  52.7 22.4 %all_to_all.16.refs_0_ = bf16[32,16,128]{2,1,0:T(8,128)(2,1)S(1)} all-to-all(bf16[32,16,128]{2,1,0:T(8,128)(2,1)S(1)} %bitcast.23), channel_id=1, replica_groups={{0,2,4,6,128,130,132,134,256,258,260,262,384,386,388,390,16,18,20,22,14..., dimensions={0} | all-to-all | bytes 262144 | tf_op jit(solution)/shard_map/all_to_all | solution.py:364
  75.0 0.7 shard_map.124
  75.7 5.6 %all-to-all-start.2 = ((bf16[32,16,128]{2,1,0:T(8,128)(2,1)}), bf16[32,16,128]{2,1,0:T(8,128)(2,1)S(1)}, u32[]{:S(2)}, u32[]{:S(2)}) async-start(bf16[32,16,128]{2,1,0:T(8,128)(2,1)} %shard_map.124), calls=%async_computation.2 | async-start | bytes 262144 | tf_op jit(solution)/shard_map/all_to_all | solution.py:366
  81.3 1.9 %shard_map.121 = (bf16[512,256]{1,0:T(8,128)(2,1)}, bf16[512,512]{1,0:T(8,128)(2,1)}, bf16[128,1024]{1,0:T(8,128)(2,1)}) custom-call(bf16[2304,256]{1,0:T(8,128)(2,1)S(1)} %get-tuple-element.23.refs_1_.refs_0_, bf16[512,256]{1,0:T(8,128)(2,1)S(1)} %get-tuple-element.24.refs_1_, bf16[1024,256]{1,0:T(8,128)(2,1)S(1)} %get-tuple-element.25.refs_2_, ...), custom_call_target="tpu_custom_call" | custom-call | flops 805306368 | bytes 3932160 | tf_op jit(solution)/shard_map/pallas_call | solution.py:51
  83.2 7.5 %all-to-all-done.2 = bf16[32,16,128]{2,1,0:T(8,128)(2,1)S(1)} async-done(((bf16[32,16,128]{2,1,0:T(8,128)(2,1)}), bf16[32,16,128]{2,1,0:T(8,128)(2,1)S(1)}, u32[]{:S(2)}, u32[]{:S(2)}) %all-to-all-start.2) | async-done | bytes 131104 | tf_op jit(solution)/shard_map/all_to_all | solution.py:366
  90.8 0.7 pad_maximum_fusion
  (3 shorter events, 0.0 us)
Async XLA Ops:
  3.4 5.9 %collective-permute-start = (bf16[16,256]{1,0:T(8,128)(2,1)S(1)}, bf16[16,256]{1,0:T(8,128)(2,1)S(1)}, u32[]{:S(2)}, u32[]{:S(2)}) collective-permute-start(bf16[16,256]{1,0:T(8,128)(2,1)S(1)} %get-tuple-element.28), channel_id=1, source_target_pairs={{0,1},{1,0},{2,3},{3,2},{4,5},{5,4},{6,7},{7,6},{8,9},{9,8},{10,11... | collective-permute-start | bytes 24584 | tf_op jit(solution)/shard_map/ppermute | solution.py:312
  9.3 12.2 %collective-permute-start.2 = (bf16[144,256]{1,0:T(8,128)(2,1)S(1)}, bf16[144,256]{1,0:T(8,128)(2,1)S(1)}, u32[]{:S(2)}, u32[]{:S(2)}) collective-permute-start(bf16[144,256]{1,0:T(8,128)(2,1)S(1)} %get-tuple-element.45), channel_id=1, source_target_pairs={{2,4},{6,8},{10,12},{14,16},{18,20},{22,24},{26,28},{4,2},{8,6},{1... | collective-permute-start | bytes 221192 | tf_op jit(solution)/shard_map/ppermute | solution.py:320
  9.9 13.6 %collective-permute-start.1 = (bf16[144,256]{1,0:T(8,128)(2,1)S(1)}, bf16[144,256]{1,0:T(8,128)(2,1)S(1)}, u32[]{:S(2)}, u32[]{:S(2)}) collective-permute-start(bf16[144,256]{1,0:T(8,128)(2,1)S(1)} %get-tuple-element.46), channel_id=1, source_target_pairs={{0,2},{4,6},{8,10},{12,14},{16,18},{20,22},{24,26},{28,30},{2,0},{... | collective-permute-start | bytes 221192 | tf_op jit(solution)/shard_map/ppermute | solution.py:319
  26.9 6.9 %collective-permute-start.3 = (bf16[8,32,16,128]{3,2,1,0:T(8,128)(2,1)S(1)}, bf16[8,32,16,128]{3,2,1,0:T(8,128)(2,1)S(1)}, u32[]{:S(2)}, u32[]{:S(2)}) collective-permute-start(bf16[8,32,16,128]{3,2,1,0:T(8,128)(2,1)S(1)} %get-tuple-element.41), channel_id=1, source_target_pairs={{0,32},{32,0},{1,33},{33,1},{2,34},{34,2},{3,35},{35,3},{4,36},{36... | collective-permute-start | bytes 3145736 | tf_op jit(solution)/shard_map/ppermute | solution.py:360
  75.7 15.1 %all-to-all-start.2 = ((bf16[32,16,128]{2,1,0:T(8,128)(2,1)}), bf16[32,16,128]{2,1,0:T(8,128)(2,1)S(1)}, u32[]{:S(2)}, u32[]{:S(2)}) async-start(bf16[32,16,128]{2,1,0:T(8,128)(2,1)} %shard_map.124), calls=%async_computation.2 | async-start | bytes 262144 | tf_op jit(solution)/shard_map/all_to_all | solution.py:366

commit v4 on v3

--- a/solution.py
+++ b/solution.py
@@ -145,9 +145,9 @@
     return block // per // 2, (block // per) % 2, block % per
 
 
-def groups_of(core, x, y, z):
-    x, y, z = (x + core) % SIZES["x"], (y + core) % SIZES["y"], (z + core) % SIZES["z"]
-    return (x % 2) * 4 + (y % 2) * 2 + z % 2, (x // 2) * 16 + (y // 2) * 4 + z // 2
+def groups_of(core, x_lo, y, z):
+    y, z = (y + core) % SIZES["y"], (z + core) % SIZES["z"]
+    return x_lo * 4 + (y % 2) * 2 + z % 2, (y // 2) * (SIZES["z"] // 2) + z // 2
 
 
 def group_lists():
@@ -156,39 +156,45 @@
     for y in range(SIZES["y"]):
         for core in range(2):
             for x in range(SIZES["x"]):
+                pair, x_lo = divmod((x + core) % SIZES["x"], 2)
                 for z in range(SIZES["z"]):
-                    in_near, in_far = groups_of(core, x, y, z)
-                    near.setdefault((core, in_far), [None] * 8)[in_near] = index
-                    far.setdefault((core, in_near), [None] * 32)[in_far] = index
+                    in_near, in_far = groups_of(core, x_lo, y, z)
+                    near.setdefault((core, pair, in_far), [None] * 8)[in_near] = index
+                    far.setdefault((core, pair, in_near), [None] * 16)[in_far] = index
                     index += 1
     return list(near.values()), list(far.values())
 
 
 def grads_kernel(
     width, each, scale, place, cot, conv, m4_cot, c3, c4, m3, row_a, row_b, col,
-    m3_grad_b, m4_grad_b, top_grad, term, shifted, sums, sums5,
+    m3_grad_b, m4_grad_b, top_grad, own, other, shifted, sums, sums5,
 ):
     n3, chans = cot.shape
     n4 = c4.shape[0]
     me = place[0]
-    per = each // 16
+    def store(blocks):
+        for core in range(2):
+
+            @pl.when(me == core)
+            def _():
+                for owner, near, far, value in blocks:
+                    (own if owner == core else other)[near, far] = value
 
     def put(first, value):
         value = (value * scale).astype(BF16)
+        blocks = []
         for k in range(value.shape[0] // 16):
-            y, owner, r = pieces_of(first // 16 + k, each)
-            slot = jnp.where(me == owner, 0, 1)
-            for h in range(2):
-                p = h * 16 + r
-                near, far = groups_of(owner, p // SIZES["z"], y, p % SIZES["z"])
-                term[slot, near, far] = value[16 * k : 16 * k + 16, 128 * h : 128 * h + 128]
-
-    blank = jnp.zeros((16, 128), BF16)
+            y, owner, p = pieces_of(first // 16 + k, each)
+            near, far = groups_of(owner, p // SIZES["z"], y, p % SIZES["z"])
+            blocks.append((owner, near, far, value[16 * k : 16 * k + 16]))
+        store(blocks)
+
+    blank = jnp.zeros((16, chans), BF16)
     for y in range(SIZES["y"]):
-        for p in [h * 16 + r for r in range(per, 16) for h in range(2)]:
+        for p in range(each // 16, 16):
             for owner in range(2):
                 near, far = groups_of(owner, p // SIZES["z"], y, p % SIZES["z"])
-                term[jnp.where(me == owner, 0, 1), near, far] = blank
+                store([(owner, near, far, blank)])
 
     fill_shifted(place, 0, cot, row_a, row_b, col, shifted, width)
 
@@ -280,7 +286,8 @@
             shape_of(n3, chans),
             shape_of(n4, chans),
             shape_of(n4 // 4, chans),
-            shape_of(2, 8, 32, 16, 128),
+            shape_of(8, 16, 16, chans),
+            shape_of(8, 16, 16, chans),
         ],
         [
             pltpu.VMEM((3, n3 + 2 * width, chans), BF16),
@@ -353,19 +360,39 @@
     )(*parts)
 
 
-def add_grads(term, each):
+def finish_kernel(parts, out):
+    core = lax.axis_index("core")
+    rows = parts.shape[2]
+    for x_lo in range(2):
+        x = jnp.where(core == x_lo, 0, 1)
+        for z in range(parts.shape[1]):
+            first = (x_lo * parts.shape[1] + z) * rows
+            if first < out.shape[0]:
+                value = parts[x, z].astype(F32) + parts[x + 2, z].astype(F32)
+                out[first : first + rows] = value
+
+
+def add_grads(own, other, each):
     everyone = OWNERS + SHARED
     near_groups, far_groups = group_lists()
-    _, near, far, rows, cols = term.shape
-    got = lax.ppermute(term[1], "core", [(0, 1), (1, 0)])
-    part = add_up(term[:1].reshape(1, -1, cols), got.reshape(1, -1, cols))
-    part = lax.all_to_all(part.reshape(near, far * rows, cols), everyone, 0, 0, axis_index_groups=near_groups, tiled=True)
-    part = add_up(part)
-    part = lax.all_to_all(part.reshape(far, rows, cols), everyone, 0, 0, axis_index_groups=far_groups, tiled=True)
+    near, far, rows, cols = own.shape
+    got = lax.ppermute(other, "core", [(0, 1), (1, 0)])
+    part = add_up(own.reshape(1, -1, cols), got.reshape(1, -1, cols))
+    part = part.reshape(near, far * rows, cols)
+    part = lax.all_to_all(part, everyone, 0, 0, axis_index_groups=near_groups, tiled=True)
+    part = add_up(part).reshape(far, rows, cols)
+    part = lax.all_to_all(part, everyone, 0, 0, axis_index_groups=far_groups, tiled=True)
     part = add_up(part, count=lax.axis_size(SHARED))
     part = lax.all_to_all(part, SHARED, 0, 0, tiled=True)
-    halves = part.reshape(2, -1, cols)[:, :each].astype(F32)
-    return jnp.concatenate([halves[0], halves[1]], axis=1)
+    part = part.reshape(SIZES["x"], SIZES["z"], rows, cols)
+    in_vmem = pl.BlockSpec(memory_space=pltpu.VMEM)
+    return pl.pallas_call(
+        finish_kernel,
+        out_shape=jax.ShapeDtypeStruct((each, cols), F32),
+        in_specs=[in_vmem],
+        out_specs=in_vmem,
+        compiler_params=pltpu.CompilerParams(vmem_limit_bytes=LIMIT),
+    )(part)
 
 
 def shards(c3, c4, top_down, lat3_weight, lat4_weight, conv_weight, p3_cot, m4_cot):
@@ -387,10 +414,10 @@
     )
     c4_v, lat4_v, _, c3_v, lat3_v, cot_v, conv_v, m4_cot_v = fetched
     borders = swap_borders(col, row_a, row_b)
-    m3_grad_b, m4_grad_b, top_grad, term = run_grads(
+    m3_grad_b, m4_grad_b, top_grad, own, other = run_grads(
         width, each, scale, cot_v, conv_v, m4_cot_v, c3_v, c4_v, m3, *borders
     )
-    weight_grads = add_grads(term, each)
+    weight_grads = add_grads(own, other, each)
     p3, c3_grad, c4_grad = run_outputs(
         width, conv_v, lat3_v, lat4_v, m3, *borders, m3_grad_b, m4_grad_b
     )

time: 91.9 us -> 93.3 us (1.015)
  Pallas kernels: 8.75 us -> 12.2 us
  blocking collectives: 40.9 us -> 37.6 us
  waiting for transfers between devices: 12.9 us -> 14.8 us
    all_to_all x2, blocking collectives: 40.9 us -> 37.7 us  [the longest x1 19.1 us: add_grads(): lax.all_to_all(part, everyone, 0, 0, axis_index_groups=far_groups, tiled=...]
    pallas_call x3, Pallas kernels: 7.68 us -> 10.3 us  [call(): pl.pallas_call(body, out_shape=list(out_shape) + [jax.ShapeDtypeStruct(x....]
    all_to_all x1, waiting for transfers between devices: 7.55 us -> 9.45 us  [add_grads(): part = lax.all_to_all(part, SHARED, 0, 0, tiled=True)]
where the time goes in v4:
time: 93.3 us; the launch traced here: 92.9 us
  blocking collectives  37.6 us (40%)
  starting transfers between devices  27.6 us (30%)
  waiting for transfers between devices  14.8 us (16%)
  Pallas kernels  12.2 us (13%)
    all_to_all x1, blocking collectives, add_grads(): lax.all_to_all(part, everyone, 0, 0, axis_index_groups=far_groups, tiled=...  19.1 us
    all_to_all x1, blocking collectives, add_grads(): lax.all_to_all(part, everyone, 0, 0, axis_index_groups=near_groups, tiled...  18.5 us
    ppermute x1, starting transfers between devices, swap_borders(): row_a = lax.ppermute(row_a, ROWS, pairs + [(j, i) for i, j in pairs])  11.5 us
    pallas_call x3, Pallas kernels, call(): pl.pallas_call(body, out_shape=list(out_shape) + [jax.ShapeDtypeStruct(x....  10.3 us
    all_to_all x1, waiting for transfers between devices, add_grads(): part = lax.all_to_all(part, SHARED, 0, 0, tiled=True)  9.45 us
    all_to_all x1, starting transfers between devices, add_grads(): part = lax.all_to_all(part, SHARED, 0, 0, tiled=True)  6.07 us
    ppermute x1, starting transfers between devices, swap_borders(): col = lax.ppermute(col, 'z_lo', [(0, 1), (1, 0)])  4.83 us
    ppermute x1, starting transfers between devices, add_grads(): got = lax.ppermute(other, 'core', [(0, 1), (1, 0)])  4.55 us
  transfers between devices with their start and end apart: 5, of which 4 were waited for; matrix products, arithmetic and copies ran while one was open for 0% of the time, Pallas kernels for 2%

profile of v4, /device:TPU:1, one launch (start us, length us, event | category | flops | bytes accessed | tf_op | source)
XLA Modules:
  0.0 92.9 jit_solution(15528740114152861595)
XLA Ops:
  0.6 2.8 %shard_map.119 = (bf16[512,256]{1,0:T(8,128)(2,1)S(1)}, bf16[16,256]{1,0:T(8,128)(2,1)S(1)}, bf16[144,256]{1,0:T(8,128)(2,1)S(1)}, bf16[144,256]{1,0:T(8,128)(2,...) custom-call(bf16[128,1024]{1,0:T(8,128)(2,1)} %bitcast.20, ...), custom_call_target="tpu_custom_call" | custom-call | flops 201326592 | bytes 3276800 | tf_op jit(solution)/shard_map/pallas_call | solution.py:51
  3.4 4.8 %collective-permute-start = (bf16[16,256]{1,0:T(8,128)(2,1)S(1)}, bf16[16,256]{1,0:T(8,128)(2,1)S(1)}, u32[]{:S(2)}, u32[]{:S(2)}) collective-permute-start(bf16[16,256]{1,0:T(8,128)(2,1)S(1)} %get-tuple-element.29), channel_id=1, source_target_pairs={{0,1},{1,0},{2,3},{3,2},{4,5},{5,4},{6,7},{7,6},{8,9},{9,8},{10,11... | collective-permute-start | bytes 24584 | tf_op jit(solution)/shard_map/ppermute | solution.py:319
  8.3 1.0 %collective-permute-done.refs_8_.refs_6_ = bf16[16,256]{1,0:T(8,128)(2,1)S(1)} collective-permute-done((bf16[16,256]{1,0:T(8,128)(2,1)S(1)}, bf16[16,256]{1,0:T(8,128)(2,1)S(1)}, u32[]{:S(2)}, u32[]{:S(2)}) %collective-permute-start) | collective-permute-done | bytes 8224 | tf_op jit(solution)/shard_map/ppermute | solution.py:319
  9.3 0.7 collective-permute-start.2
  9.9 11.5 %collective-permute-start.1 = (bf16[144,256]{1,0:T(8,128)(2,1)S(1)}, bf16[144,256]{1,0:T(8,128)(2,1)S(1)}, u32[]{:S(2)}, u32[]{:S(2)}) collective-permute-start(bf16[144,256]{1,0:T(8,128)(2,1)S(1)} %get-tuple-element.44), channel_id=1, source_target_pairs={{0,2},{4,6},{8,10},{12,14},{16,18},{20,22},{24,26},{28,30},{2,0},{... | collective-permute-start | bytes 221192 | tf_op jit(solution)/shard_map/ppermute | solution.py:326
  21.5 0.0 collective-permute-done.2.refs_7_.refs_5_
  21.5 2.0 %collective-permute-done.1.refs_6_.refs_4_ = bf16[144,256]{1,0:T(8,128)(2,1)S(1)} collective-permute-done((bf16[144,256]{1,0:T(8,128)(2,1)S(1)}, bf16[144,256]{1,0:T(8,128)(2,1)S(1)}, u32[]{:S(2)}, u32[]{:S(2)}) %collective-permute-start.1) | collective-permute-done | bytes 73760 | tf_op jit(solution)/shard_map/ppermute | solution.py:326
  23.5 5.6 %shard_map.120 = (bf16[512,256]{1,0:T(8,128)(2,1)S(1)}, bf16[128,256]{1,0:T(8,128)(2,1)S(1)}, bf16[32,256]{1,0:T(8,128)(2,1)}, bf16[8,16,16,256]{3,2,1,0:T(8,128)(2,1)S(1)}, bf16[8,16,16,256]{3,2,1,0:T(8,128)(2,1)S(1)}) custom-call(bf16[512,256]{1,0:T(8,128)(2,1)S(1)} %get-tuple-element.31.refs_0_, bf16[2304,256]{1,0:T(8,128)(2,1)S(1)} %get-tuple-element.24.refs_1_.refs_0_, ...), custom_call_target="tpu_custom_call" | custom-call | flops 1409286144 | bytes 3145728 | tf_op jit(solution)/shard_map/pallas_call | solution.py:51
  29.1 4.5 %collective-permute-start.3 = (bf16[8,16,16,256]{3,2,1,0:T(8,128)(2,1)S(1)}, bf16[8,16,16,256]{3,2,1,0:T(8,128)(2,1)S(1)}, u32[]{:S(2)}, u32[]{:S(2)}) collective-permute-start(bf16[8,16,16,256]{3,2,1,0:T(8,128)(2,1)S(1)} %get-tuple-element.42), channel_id=1, source_target_pairs={{0,32},{32,0},{1,33},{33,1},{2,34},{34,2},{3,35},{35,3},{4,36},{36... | collective-permute-start | bytes 3145736 | tf_op jit(solution)/shard_map/ppermute | solution.py:379
  33.7 2.3 %collective-permute-done.3 = bf16[8,16,16,256]{3,2,1,0:T(8,128)(2,1)S(1)} collective-permute-done((bf16[8,16,16,256]{3,2,1,0:T(8,128)(2,1)S(1)}, bf16[8,16,16,256]{3,2,1,0:T(8,128)(2,1)S(1)}, u32[]{:S(2)}, u32[]{:S(2)}) %collective-permute-start.3) | collective-permute-done | bytes 1048608 | tf_op jit(solution)/shard_map/ppermute | solution.py:379
  36.0 0.2 shard_map.122
  36.2 18.5 %all_to_all.15.refs_0_ = bf16[8,256,256]{2,1,0:T(8,128)(2,1)S(1)} all-to-all(bf16[8,256,256]{2,1,0:T(8,128)(2,1)S(1)} %bitcast.14), channel_id=1, replica_groups={{0,1,64,65,8,9,72,73},{2,3,66,67,10,11,74,75},{4,5,68,69,12,13,76,77},{..., dimensions={0} | all-to-all | bytes 2097152 | tf_op jit(solution)/shard_map/all_to_all | solution.py:382
  54.8 0.1 shard_map.123
  54.9 19.1 %all_to_all.16.refs_0_ = bf16[16,16,256]{2,1,0:T(8,128)(2,1)S(1)} all-to-all(bf16[16,16,256]{2,1,0:T(8,128)(2,1)S(1)} %bitcast.18), channel_id=1, replica_groups={{0,2,4,6,128,130,132,134,256,258,260,262,384,386,388,390},{1,3,5,7,129,..., dimensions={0} | all-to-all | bytes 262144 | tf_op jit(solution)/shard_map/all_to_all | solution.py:384
  74.0 0.7 shard_map.124
  74.7 6.1 %all-to-all-start.2 = ((bf16[32,16,256]{2,1,0:T(8,128)(2,1)}), bf16[32,16,256]{2,1,0:T(8,128)(2,1)S(1)}, u32[]{:S(2)}, u32[]{:S(2)}) async-start(bf16[32,16,256]{2,1,0:T(8,128)(2,1)} %shard_map.124), calls=%async_computation.2 | async-start | bytes 524288 | tf_op jit(solution)/shard_map/all_to_all | solution.py:386
  80.8 1.9 %shard_map.121 = (bf16[512,256]{1,0:T(8,128)(2,1)}, bf16[512,512]{1,0:T(8,128)(2,1)}, bf16[128,1024]{1,0:T(8,128)(2,1)}) custom-call(bf16[2304,256]{1,0:T(8,128)(2,1)S(1)} %get-tuple-element.24.refs_1_.refs_0_, bf16[512,256]{1,0:T(8,128)(2,1)S(1)} %get-tuple-element.25.refs_1_, bf16[1024,256]{1,0:T(8,128)(2,1)S(1)} %get-tuple-element.26.refs_2_, ...), custom_call_target="tpu_custom_call" | custom-call | flops 805306368 | bytes 3932160 | tf_op jit(solution)/shard_map/pallas_call | solution.py:51
  82.7 9.5 %all-to-all-done.2 = bf16[32,16,256]{2,1,0:T(8,128)(2,1)S(1)} async-done(((bf16[32,16,256]{2,1,0:T(8,128)(2,1)}), bf16[32,16,256]{2,1,0:T(8,128)(2,1)S(1)}, u32[]{:S(2)}, u32[]{:S(2)}) %all-to-all-start.2) | async-done | bytes 262176 | tf_op jit(solution)/shard_map/all_to_all | solution.py:386
  92.2 0.7 shard_map.125
  (1 shorter events, 0.0 us)
Async XLA Ops:
  3.4 5.9 %collective-permute-start = (bf16[16,256]{1,0:T(8,128)(2,1)S(1)}, bf16[16,256]{1,0:T(8,128)(2,1)S(1)}, u32[]{:S(2)}, u32[]{:S(2)}) collective-permute-start(bf16[16,256]{1,0:T(8,128)(2,1)S(1)} %get-tuple-element.29), channel_id=1, source_target_pairs={{0,1},{1,0},{2,3},{3,2},{4,5},{5,4},{6,7},{7,6},{8,9},{9,8},{10,11... | collective-permute-start | bytes 24584 | tf_op jit(solution)/shard_map/ppermute | solution.py:319
  9.3 12.2 %collective-permute-start.2 = (bf16[144,256]{1,0:T(8,128)(2,1)S(1)}, bf16[144,256]{1,0:T(8,128)(2,1)S(1)}, u32[]{:S(2)}, u32[]{:S(2)}) collective-permute-start(bf16[144,256]{1,0:T(8,128)(2,1)S(1)} %get-tuple-element.43), channel_id=1, source_target_pairs={{2,4},{6,8},{10,12},{14,16},{18,20},{22,24},{26,28},{4,2},{8,6},{1... | collective-permute-start | bytes 221192 | tf_op jit(solution)/shard_map/ppermute | solution.py:327
  9.9 13.6 %collective-permute-start.1 = (bf16[144,256]{1,0:T(8,128)(2,1)S(1)}, bf16[144,256]{1,0:T(8,128)(2,1)S(1)}, u32[]{:S(2)}, u32[]{:S(2)}) collective-permute-start(bf16[144,256]{1,0:T(8,128)(2,1)S(1)} %get-tuple-element.44), channel_id=1, source_target_pairs={{0,2},{4,6},{8,10},{12,14},{16,18},{20,22},{24,26},{28,30},{2,0},{... | collective-permute-start | bytes 221192 | tf_op jit(solution)/shard_map/ppermute | solution.py:326
  29.1 6.8 %collective-permute-start.3 = (bf16[8,16,16,256]{3,2,1,0:T(8,128)(2,1)S(1)}, bf16[8,16,16,256]{3,2,1,0:T(8,128)(2,1)S(1)}, u32[]{:S(2)}, u32[]{:S(2)}) collective-permute-start(bf16[8,16,16,256]{3,2,1,0:T(8,128)(2,1)S(1)} %get-tuple-element.42), channel_id=1, source_target_pairs={{0,32},{32,0},{1,33},{33,1},{2,34},{34,2},{3,35},{35,3},{4,36},{36... | collective-permute-start | bytes 3145736 | tf_op jit(solution)/shard_map/ppermute | solution.py:379
  74.7 17.4 %all-to-all-start.2 = ((bf16[32,16,256]{2,1,0:T(8,128)(2,1)}), bf16[32,16,256]{2,1,0:T(8,128)(2,1)S(1)}, u32[]{:S(2)}, u32[]{:S(2)}) async-start(bf16[32,16,256]{2,1,0:T(8,128)(2,1)} %shard_map.124), calls=%async_computation.2 | async-start | bytes 524288 | tf_op jit(solution)/shard_map/all_to_all | solution.py:386

commit v5 on v3

--- a/solution.py
+++ b/solution.py
@@ -60,8 +60,7 @@
 
 
 def merge_kernel(
-    width4, place, waits, c4, lat4, top, c3, lat3, cot, conv, m4_cot,
-    m3, col, row_a, row_b, up4,
+    width4, place, waits, c4, lat4, top, c3, lat3, cot, m3, col, row_a, row_b, up4,
 ):
     n4, n5 = c4.shape[0], top.shape[0]
     n3 = c3.shape[0]
@@ -101,43 +100,43 @@
         out[:width3] = cot[pl.ds(start, width3)]
         out[width3 : 2 * width3] = m3[pl.ds(start, width3)]
         out[2 * width3 :] = jnp.zeros((2 * lines, out.shape[1]), BF16)
-    for wait in waits[6:]:
-        wait()
-
-
-def fill_shifted(place, field, own, row_a, row_b, col, shifted, width):
-    n, chans = own.shape
-    lines = n // width
-    z_lo, odd = place[1], place[2] == 1
+
+
+def shift_line(line, left, right):
+    width = line.shape[0]
+    at = lax.broadcasted_iota(jnp.int32, line.shape, 0)
+    before = jnp.where(at == 0, left, pltpu.roll(line, 1, 0))
+    after = jnp.where(at == width - 1, right, pltpu.roll(line, width - 1, 0))
+    return before.astype(BF16), line.astype(BF16), after.astype(BF16)
+
+
+def outer_lines(place, field, row_a, row_b, lines, width):
+    odd = place[2] == 1
     rows = slice(field * width, (field + 1) * width)
     corner = slice(2 * width, 2 * width + 2 * lines)
     line_a, line_b = row_a[rows].astype(F32), row_b[rows].astype(F32)
     ends_a, ends_b = row_a[corner].astype(F32), row_b[corner].astype(F32)
     first, last = field * lines, (field + 1) * lines - 1
+    return (
+        (jnp.where(odd, line_a, line_b), jnp.where(odd, ends_a, ends_b)[last : last + 1]),
+        (jnp.where(odd, line_b, line_a), jnp.where(odd, ends_b, ends_a)[first : first + 1]),
+    )
+
+
+def fill_line(place, shifted, y, line, side):
+    to_the_left = jnp.where(place[1] == 1, 1.0, 0.0)
+    width = line.shape[0]
+    planes = shift_line(line, side * to_the_left, side * (1.0 - to_the_left))
+    for i in range(3):
+        shifted[i, y * width : (y + 1) * width] = planes[i]
+
+
+def fill_inner(place, field, own, col, shifted, width):
+    lines = own.shape[0] // width
     sides = col[...].astype(F32)
-    before = jnp.where(odd, ends_a, ends_b)[last : last + 1]
-    after = jnp.where(odd, ends_b, ends_a)[first : first + 1]
-    sides = [before] + [sides[first + y : first + y + 1] for y in range(lines)] + [after]
-    at = lax.broadcasted_iota(jnp.int32, (width, chans), 0)
-    to_the_left = jnp.where(z_lo == 1, 1.0, 0.0)
-    to_the_right = 1.0 - to_the_left
-    for y in range(lines + 2):
-        if y == 0:
-            line = jnp.where(odd, line_a, line_b)
-            shifted[1, :width] = line.astype(BF16)
-        elif y == lines + 1:
-            line = jnp.where(odd, line_b, line_a)
-            shifted[1, y * width :] = line.astype(BF16)
-        else:
-            line = own[(y - 1) * width : y * width]
-            shifted[1, y * width : (y + 1) * width] = line
-            line = line.astype(F32)
-        rows = slice(y * width, (y + 1) * width)
-        left, right = sides[y] * to_the_left, sides[y] * to_the_right
-        shifted[0, rows] = jnp.where(at == 0, left, pltpu.roll(line, 1, 0)).astype(BF16)
-        shifted[2, rows] = jnp.where(
-            at == width - 1, right, pltpu.roll(line, width - 1, 0)
-        ).astype(BF16)
+    for y in range(lines):
+        side = sides[field * lines + y : field * lines + y + 1]
+        fill_line(place, shifted, y + 1, own[y * width : (y + 1) * width].astype(F32), side)
 
 
 def pieces_of(block, each):
@@ -164,11 +163,29 @@
     return list(near.values()), list(far.values())
 
 
+def early_kernel(width, place, cot, conv, m3, col, partial, gradc, shifted):
+    n3, chans = cot.shape
+    blank = jnp.zeros((3, width, chans), BF16)
+    shifted[:, :width] = blank
+    shifted[:, n3 + width :] = blank
+    fill_inner(place, 0, cot, col, shifted, width)
+    m3_t = m3[...].T
+    total = None
+    for a in range(3):
+        for b in range(3):
+            tap = slice((3 * a + b) * chans, (3 * a + b + 1) * chans)
+            field = shifted[2 - b, (2 - a) * width : (2 - a) * width + n3]
+            part = dot(field, conv[tap], NT)
+            total = part if total is None else total + part
+            gradc[tap] = dot(m3_t, field)
+    partial[...] = total
+
+
 def grads_kernel(
-    width, each, scale, place, cot, conv, m4_cot, c3, c4, m3, row_a, row_b, col,
-    m3_grad_b, m4_grad_b, top_grad, term, shifted, sums, sums5,
+    width, each, scale, place, partial, gradc, conv, m4_cot, c3, c4, m3, row_a, row_b,
+    m3_grad_b, m4_grad_b, top_grad, term, total, sums, sums5,
 ):
-    n3, chans = cot.shape
+    n3, chans = partial.shape
     n4 = c4.shape[0]
     me = place[0]
     per = each // 16
@@ -190,19 +207,22 @@
                 near, far = groups_of(owner, p // SIZES["z"], y, p % SIZES["z"])
                 term[jnp.where(me == owner, 0, 1), near, far] = blank
 
-    fill_shifted(place, 0, cot, row_a, row_b, col, shifted, width)
-
-    def cot_at(a, b):
-        return shifted[2 - b, (2 - a) * width : (2 - a) * width + n3]
-
-    total = None
-    for a in range(3):
+    before, after = outer_lines(place, 0, row_a, row_b, n3 // width, width)
+    to_the_left = jnp.where(place[1] == 1, 1.0, 0.0)
+    total[...] = partial[...]
+    added = {}
+    for a, rows, (line, side) in (
+        (2, slice(0, width), before),
+        (0, slice(n3 - width, n3), after),
+    ):
+        planes = shift_line(line, side * to_the_left, side * (1.0 - to_the_left))
+        part = total[rows]
         for b in range(3):
             tap = 3 * a + b
-            weight = conv[tap * chans : (tap + 1) * chans]
-            part = dot(cot_at(a, b), weight, NT)
-            total = part if total is None else total + part
-    m3_grad_b[...] = total.astype(BF16)
+            part = part + dot(planes[2 - b], conv[tap * chans : (tap + 1) * chans], NT)
+            added[tap] = (rows, planes[2 - b])
+        total[rows] = part
+    m3_grad_b[...] = total[...].astype(BF16)
     for y in range(n4 // (width // 2)):
         pair = total[2 * y * width : (2 * y + 1) * width] + total[(2 * y + 1) * width : (2 * y + 2) * width]
         sums[0, y * width : (y + 1) * width] = pair[:, :128]
@@ -229,11 +249,12 @@
     depth3, depth4 = c3.shape[1], c4.shape[1]
     put(0, dot(c3[...], m3_grad_b[...], TN))
     put(depth3, dot(c4[...], m4_grad_b[...], TN))
-    m3_t = m3[...].T
-    for a in range(3):
-        for b in range(3):
-            tap = 3 * a + b
-            put(depth3 + depth4 + tap * chans, dot(m3_t, cot_at(a, b)))
+    for tap in range(9):
+        value = gradc[tap * chans : (tap + 1) * chans]
+        if tap in added:
+            rows, plane = added[tap]
+            value = value + dot(m3[rows], plane, TN)
+        put(depth3 + depth4 + tap * chans, value)
 
 
 def outputs_kernel(
@@ -241,7 +262,10 @@
     p3, c3_grad, c4_grad, shifted,
 ):
     n3, chans = m3.shape
-    fill_shifted(place, 1, m3, row_a, row_b, col, shifted, width)
+    fill_inner(place, 1, m3, col, shifted, width)
+    before, after = outer_lines(place, 1, row_a, row_b, n3 // width, width)
+    fill_line(place, shifted, 0, *before)
+    fill_line(place, shifted, n3 // width + 1, *after)
     total = None
     for a in range(3):
         for b in range(3):
@@ -257,7 +281,7 @@
     return jax.ShapeDtypeStruct(dims, BF16)
 
 
-def run_merge(width, c3, c4, top, lat3, lat4, cot, conv, m4_cot):
+def run_merge(width, c3, c4, top, lat3, lat4, cot):
     n3, n4, chans = c3.shape[0], c4.shape[0], lat3.shape[1]
     lines = n3 // width
     border = shape_of(2 * width + 2 * lines, chans)
@@ -266,13 +290,36 @@
         [shape_of(n3, chans), shape_of(2 * lines, chans), border, border],
         [pltpu.VMEM((2, 2 * n4, 128), F32)],
         2 * chans * (c3.size + c4.size),
-        2 * (c3.size + c4.size + lat3.size + lat4.size + 2 * cot.size + conv.size),
-        (c4, lat4, top, c3, lat3, cot, conv, m4_cot),
-    )
-
-
-def run_grads(width, each, scale, cot, conv, m4_cot, c3, c4, m3, row_a, row_b, col):
+        2 * (c3.size + c4.size + lat3.size + lat4.size + 2 * cot.size),
+        (c4, lat4, top, c3, lat3, cot),
+    )
+
+
+def fetch_kernel(place, waits, *refs):
+    for wait in waits:
+        wait()
+
+
+def run_fetch(after, *arrays):
+    moved = 2 * sum(x.size for x in arrays)
+    return call(fetch_kernel, [], [], 0, moved, arrays, (after,))
+
+
+def run_early(width, cot, conv, m3, col):
     n3, chans = cot.shape
+    return call(
+        functools.partial(early_kernel, width),
+        [jax.ShapeDtypeStruct((n3, chans), F32), jax.ShapeDtypeStruct(conv.shape, F32)],
+        [pltpu.VMEM((3, n3 + 2 * width, chans), BF16)],
+        2 * chans * 2 * 9 * n3 * chans,
+        8 * conv.size,
+        (),
+        (cot, conv, m3, col),
+    )
+
+
+def run_grads(width, each, scale, partial, gradc, conv, m4_cot, c3, c4, m3, row_a, row_b):
+    n3, chans = partial.shape
     n4 = c4.shape[0]
     return call(
         functools.partial(grads_kernel, width, each, scale),
@@ -283,14 +330,14 @@
             shape_of(2, 8, 32, 16, 128),
         ],
         [
-            pltpu.VMEM((3, n3 + 2 * width, chans), BF16),
+            pltpu.VMEM((n3, chans), F32),
             pltpu.VMEM((2, n3 // 2, 128), F32),
             pltpu.VMEM((2, n4 // 2, 128), F32),
         ],
-        2 * chans * (c3.size + c4.size + 2 * 9 * n3 * chans),
-        2 * (c3.size + c4.size + 2 * conv.size),
+        2 * chans * (c3.size + c4.size + 6 * width * chans),
+        2 * (c3.size + c4.size + 4 * conv.size),
         (),
-        (cot, conv, m4_cot, c3, c4, m3, row_a, row_b, col),
+        (partial, gradc, conv, m4_cot, c3, c4, m3, row_a, row_b),
     )
 
 
@@ -383,12 +430,14 @@
 
     m3, col, row_a, row_b, *fetched = run_merge(
         width, c3.reshape(n3, depth3), c4.reshape(n4, depth4), top_down.reshape(n5, chans),
-        lat3_weight, lat4_weight, p3_cot.reshape(n3, chans), conv_weight, m4_cot.reshape(n4, chans),
-    )
-    c4_v, lat4_v, _, c3_v, lat3_v, cot_v, conv_v, m4_cot_v = fetched
+        lat3_weight, lat4_weight, p3_cot.reshape(n3, chans),
+    )
+    c4_v, lat4_v, _, c3_v, lat3_v, cot_v = fetched
+    conv_v, m4_cot_v = run_fetch(m3, conv_weight, m4_cot.reshape(n4, chans))
     borders = swap_borders(col, row_a, row_b)
+    partial, gradc = run_early(width, cot_v, conv_v, m3, borders[2])
     m3_grad_b, m4_grad_b, top_grad, term = run_grads(
-        width, each, scale, cot_v, conv_v, m4_cot_v, c3_v, c4_v, m3, *borders
+        width, each, scale, partial, gradc, conv_v, m4_cot_v, c3_v, c4_v, m3, *borders[:2]
     )
     weight_grads = add_grads(term, each)
     p3, c3_grad, c4_grad = run_outputs(

time: 91.9 us -> 90.1 us (0.980)
  waiting for transfers between devices: 12.9 us -> 10.4 us
    ppermute x1, waiting for transfers between devices: 2.02 us -> 0.59 us  [swap_borders(): row_a = lax.ppermute(row_a, ROWS, pairs + [(j, i) for i, j in pairs])]
    ppermute x1, waiting for transfers between devices: 1.03 us -> 0.01 us  [swap_borders(): col = lax.ppermute(col, 'z_lo', [(0, 1), (1, 0)])]
    pallas_call x3 -> x5, Pallas kernels: 7.68 us -> 8.51 us  [call(): pl.pallas_call(body, out_shape=list(out_shape) + [jax.ShapeDtypeStruct(x....]
  transfers between devices with their start and end apart: 5 -> 5, of which waited for: 4 -> 3; matrix products, arithmetic and copies ran while one was open for 0% -> 0% of each run, Pallas kernels for 2% -> 5%
where the time goes in v5:
time: 90.1 us; the launch traced here: 89.7 us
  blocking collectives  40.9 us (45%)
  starting transfers between devices  26.9 us (30%)
  waiting for transfers between devices  10.4 us (12%)
  Pallas kernels  9.59 us (11%)
    all_to_all x1, blocking collectives, add_grads(): lax.all_to_all(part.reshape(far, rows, cols), everyone, 0, 0, axis_index_...  22.4 us
    all_to_all x1, blocking collectives, add_grads(): lax.all_to_all(part.reshape(near, far * rows, cols), everyone, 0, 0, axis...  18.5 us
    ppermute x1, starting transfers between devices, swap_borders(): row_a = lax.ppermute(row_a, ROWS, pairs + [(j, i) for i, j in pairs])  11.3 us
    pallas_call x5, Pallas kernels, call(): pl.pallas_call(body, out_shape=list(out_shape) + [jax.ShapeDtypeStruct(x....  8.51 us
    all_to_all x1, waiting for transfers between devices, add_grads(): part = lax.all_to_all(part, SHARED, 0, 0, tiled=True)  7.56 us
    all_to_all x1, starting transfers between devices, add_grads(): part = lax.all_to_all(part, SHARED, 0, 0, tiled=True)  5.59 us
    ppermute x1, starting transfers between devices, swap_borders(): col = lax.ppermute(col, 'z_lo', [(0, 1), (1, 0)])  4.83 us
    ppermute x1, starting transfers between devices, add_grads(): got = lax.ppermute(term[1], 'core', [(0, 1), (1, 0)])  4.54 us
  transfers between devices with their start and end apart: 5, of which 3 were waited for; matrix products, arithmetic and copies ran while one was open for 0% of the time, Pallas kernels for 5%

profile of v5, /device:TPU:1, one launch (start us, length us, event | category | flops | bytes accessed | tf_op | source)
XLA Modules:
  0.0 89.7 jit_solution(10286034686095001672)
XLA Ops:
  0.6 2.5 %shard_map.119 = (bf16[512,256]{1,0:T(8,128)(2,1)S(1)}, bf16[16,256]{1,0:T(8,128)(2,1)S(1)}, bf16[144,256]{1,0:T(8,128)(2,1)S(1)}, bf16[144,256]{1,0:T(8,128)(2,...) custom-call(bf16[128,1024]{1,0:T(8,128)(2,1)} %bitcast.26, ...), custom_call_target="tpu_custom_call" | custom-call | flops 201326592 | bytes 2097152 | tf_op jit(solution)/shard_map/pallas_call | solution.py:51
  3.2 4.8 %collective-permute-start = (bf16[16,256]{1,0:T(8,128)(2,1)S(1)}, bf16[16,256]{1,0:T(8,128)(2,1)S(1)}, u32[]{:S(2)}, u32[]{:S(2)}) collective-permute-start(bf16[16,256]{1,0:T(8,128)(2,1)S(1)} %get-tuple-element.30), channel_id=1, source_target_pairs={{0,1},{1,0},{2,3},{3,2},{4,5},{5,4},{6,7},{7,6},{8,9},{9,8},{10,11... | collective-permute-start | bytes 24584 | tf_op jit(solution)/shard_map/ppermute | solution.py:359
  8.0 1.3 %shard_map.120 = (bf16[2304,256]{1,0:T(8,128)(2,1)S(1)}, bf16[128,256]{1,0:T(8,128)(2,1)S(1)}) custom-call(bf16[2304,256]{1,0:T(8,128)(2,1)} %refs_0_.1, bf16[128,256]{1,0:T(8,128)(2,1)} %bitcast.28, bf16[512,256]{1,0:T(8,128)(2,1)S(1)} %get-tuple-element.25.refs_2_.refs_6_.refs_3_), custom_call_target="tpu_custom_call" | custom-call | bytes 1245184 | tf_op jit(solution)/shard_map/pallas_call | solution.py:51
  9.3 0.0 collective-permute-done.refs_3_.refs_6_
  9.3 0.7 collective-permute-start.2
  10.0 11.3 %collective-permute-start.1 = (bf16[144,256]{1,0:T(8,128)(2,1)S(1)}, bf16[144,256]{1,0:T(8,128)(2,1)S(1)}, u32[]{:S(2)}, u32[]{:S(2)}) collective-permute-start(bf16[144,256]{1,0:T(8,128)(2,1)S(1)} %get-tuple-element.50), channel_id=1, source_target_pairs={{0,2},{4,6},{8,10},{12,14},{16,18},{20,22},{24,26},{28,30},{2,0},{... | collective-permute-start | bytes 221192 | tf_op jit(solution)/shard_map/ppermute | solution.py:366
  21.3 1.4 %shard_map.121 = (f32[512,256]{1,0:T(8,128)S(1)}, f32[2304,256]{1,0:T(8,128)S(1)}) custom-call(bf16[512,256]{1,0:T(8,128)(2,1)S(1)} %get-tuple-element.32.refs_0_, bf16[2304,256]{1,0:T(8,128)(2,1)S(1)} %get-tuple-element.26.refs_1_.refs_2_.refs_0_, bf16[512,256]{1,0:T(8,128)(2,1)S(1)} %get-tuple-element.25.refs_2_.refs_6_.refs_3_, ...), custom_call_target="tpu_custom_call" | custom-call | flops 1207959552 | bytes 4718592 | tf_op jit(solution)/shard_map/pallas_call | solution.py:51
  22.7 0.0 collective-permute-done.2.refs_8_.refs_5_
  22.7 0.6 collective-permute-done.1.refs_7_.refs_4_
  23.3 1.4 %shard_map.122 = (bf16[512,256]{1,0:T(8,128)(2,1)S(1)}, bf16[128,256]{1,0:T(8,128)(2,1)S(1)}, bf16[32,256]{1,0:T(8,128)(2,1)}, bf16[2,8,32,16,128]{4,3,2,1,0:T(8,128)(2,1)S(1)}) custom-call(f32[512,256]{1,0:T(8,128)S(1)} %get-tuple-element.33.refs_0_, f32[2304,256]{1,0:T(8,128)S(1)} %get-tuple-element.34.refs_1_, ...), custom_call_target="tpu_custom_call" | custom-call | flops 251658240 | bytes 5505024 | tf_op jit(solution)/shard_map/pallas_call | solution.py:51
  24.7 0.4 slice_bitcast_fusion
  25.0 4.5 %collective-permute-start.3 = (bf16[8,32,16,128]{3,2,1,0:T(8,128)(2,1)S(1)}, bf16[8,32,16,128]{3,2,1,0:T(8,128)(2,1)S(1)}, u32[]{:S(2)}, u32[]{:S(2)}) collective-permute-start(bf16[8,32,16,128]{3,2,1,0:T(8,128)(2,1)S(1)} %get-tuple-element.45), channel_id=1, source_target_pairs={{0,32},{32,0},{1,33},{33,1},{2,34},{34,2},{3,35},{35,3},{4,36},{36... | collective-permute-start | bytes 3145736 | tf_op jit(solution)/shard_map/ppermute | solution.py:407
  29.6 2.3 %collective-permute-done.3 = bf16[8,32,16,128]{3,2,1,0:T(8,128)(2,1)S(1)} collective-permute-done((bf16[8,32,16,128]{3,2,1,0:T(8,128)(2,1)S(1)}, bf16[8,32,16,128]{3,2,1,0:T(8,128)(2,1)S(1)}, u32[]{:S(2)}, u32[]{:S(2)}) %collective-permute-start.3) | collective-permute-done | bytes 1048608 | tf_op jit(solution)/shard_map/ppermute | solution.py:407
  31.8 0.2 shard_map.124
  32.1 18.5 %all_to_all.15.refs_0_ = bf16[8,512,128]{2,1,0:T(8,128)(2,1)S(1)} all-to-all(bf16[8,512,128]{2,1,0:T(8,128)(2,1)S(1)} %bitcast.20), channel_id=1, replica_groups={{0,1,64,65,8,9,72,73},{2,3,66,67,10,11,74,75},{4,5,68,69,12,13,76,77},{..., dimensions={0} | all-to-all | bytes 2097152 | tf_op jit(solution)/shard_map/all_to_all | solution.py:409
  50.6 0.1 shard_map.125
  50.8 22.4 %all_to_all.16.refs_0_ = bf16[32,16,128]{2,1,0:T(8,128)(2,1)S(1)} all-to-all(bf16[32,16,128]{2,1,0:T(8,128)(2,1)S(1)} %bitcast.23), channel_id=1, replica_groups={{0,2,4,6,128,130,132,134,256,258,260,262,384,386,388,390,16,18,20,22,14..., dimensions={0} | all-to-all | bytes 262144 | tf_op jit(solution)/shard_map/all_to_all | solution.py:411
  73.2 0.7 shard_map.126
  73.8 5.6 %all-to-all-start.2 = ((bf16[32,16,128]{2,1,0:T(8,128)(2,1)}), bf16[32,16,128]{2,1,0:T(8,128)(2,1)S(1)}, u32[]{:S(2)}, u32[]{:S(2)}) async-start(bf16[32,16,128]{2,1,0:T(8,128)(2,1)} %shard_map.126), calls=%async_computation.2 | async-start | bytes 262144 | tf_op jit(solution)/shard_map/all_to_all | solution.py:413
  79.5 1.9 %shard_map.123 = (bf16[512,256]{1,0:T(8,128)(2,1)}, bf16[512,512]{1,0:T(8,128)(2,1)}, bf16[128,1024]{1,0:T(8,128)(2,1)}) custom-call(bf16[2304,256]{1,0:T(8,128)(2,1)S(1)} %get-tuple-element.26.refs_1_.refs_2_.refs_0_, bf16[512,256]{1,0:T(8,128)(2,1)S(1)} %get-tuple-element.27.refs_1_, bf16[1024,256]{1,0:T(8,128)(2,1)S(1)} %get-tuple-element.28.refs_2_, ...), custom_call_target="tpu_custom_call" | custom-call | flops 805306368 | bytes 3932160 | tf_op jit(solution)/shard_map/pallas_call | solution.py:51
  81.4 7.6 %all-to-all-done.2 = bf16[32,16,128]{2,1,0:T(8,128)(2,1)S(1)} async-done(((bf16[32,16,128]{2,1,0:T(8,128)(2,1)}), bf16[32,16,128]{2,1,0:T(8,128)(2,1)S(1)}, u32[]{:S(2)}, u32[]{:S(2)}) %all-to-all-start.2) | async-done | bytes 131104 | tf_op jit(solution)/shard_map/all_to_all | solution.py:413
  89.0 0.7 pad_maximum_fusion
  (3 shorter events, 0.0 us)
Async XLA Ops:
  3.2 6.1 %collective-permute-start = (bf16[16,256]{1,0:T(8,128)(2,1)S(1)}, bf16[16,256]{1,0:T(8,128)(2,1)S(1)}, u32[]{:S(2)}, u32[]{:S(2)}) collective-permute-start(bf16[16,256]{1,0:T(8,128)(2,1)S(1)} %get-tuple-element.30), channel_id=1, source_target_pairs={{0,1},{1,0},{2,3},{3,2},{4,5},{5,4},{6,7},{7,6},{8,9},{9,8},{10,11... | collective-permute-start | bytes 24584 | tf_op jit(solution)/shard_map/ppermute | solution.py:359
  9.3 13.4 %collective-permute-start.2 = (bf16[144,256]{1,0:T(8,128)(2,1)S(1)}, bf16[144,256]{1,0:T(8,128)(2,1)S(1)}, u32[]{:S(2)}, u32[]{:S(2)}) collective-permute-start(bf16[144,256]{1,0:T(8,128)(2,1)S(1)} %get-tuple-element.49), channel_id=1, source_target_pairs={{2,4},{6,8},{10,12},{14,16},{18,20},{22,24},{26,28},{4,2},{8,6},{1... | collective-permute-start | bytes 221192 | tf_op jit(solution)/shard_map/ppermute | solution.py:367
  10.0 13.3 %collective-permute-start.1 = (bf16[144,256]{1,0:T(8,128)(2,1)S(1)}, bf16[144,256]{1,0:T(8,128)(2,1)S(1)}, u32[]{:S(2)}, u32[]{:S(2)}) collective-permute-start(bf16[144,256]{1,0:T(8,128)(2,1)S(1)} %get-tuple-element.50), channel_id=1, source_target_pairs={{0,2},{4,6},{8,10},{12,14},{16,18},{20,22},{24,26},{28,30},{2,0},{... | collective-permute-start | bytes 221192 | tf_op jit(solution)/shard_map/ppermute | solution.py:366
  25.0 6.8 %collective-permute-start.3 = (bf16[8,32,16,128]{3,2,1,0:T(8,128)(2,1)S(1)}, bf16[8,32,16,128]{3,2,1,0:T(8,128)(2,1)S(1)}, u32[]{:S(2)}, u32[]{:S(2)}) collective-permute-start(bf16[8,32,16,128]{3,2,1,0:T(8,128)(2,1)S(1)} %get-tuple-element.45), channel_id=1, source_target_pairs={{0,32},{32,0},{1,33},{33,1},{2,34},{34,2},{3,35},{35,3},{4,36},{36... | collective-permute-start | bytes 3145736 | tf_op jit(solution)/shard_map/ppermute | solution.py:407
  73.8 15.1 %all-to-all-start.2 = ((bf16[32,16,128]{2,1,0:T(8,128)(2,1)}), bf16[32,16,128]{2,1,0:T(8,128)(2,1)S(1)}, u32[]{:S(2)}, u32[]{:S(2)}) async-start(bf16[32,16,128]{2,1,0:T(8,128)(2,1)} %shard_map.126), calls=%async_computation.2 | async-start | bytes 262144 | tf_op jit(solution)/shard_map/all_to_all | solution.py:413

commit v6 on v5

--- a/solution.py
+++ b/solution.py
@@ -368,6 +368,24 @@
     return row_a, row_b, col
 
 
+def add_cores_kernel(term, got, out):
+    out[...] = (term[0].astype(F32) + got[...].astype(F32)).astype(BF16)
+
+
+def add_cores(term, got):
+    in_vmem = pl.BlockSpec(memory_space=pltpu.VMEM)
+    return pl.pallas_call(
+        add_cores_kernel,
+        out_shape=shape_of(*got.shape),
+        in_specs=[in_vmem] * 2,
+        out_specs=in_vmem,
+        compiler_params=pltpu.CompilerParams(vmem_limit_bytes=LIMIT),
+        cost_estimate=pl.CostEstimate(
+            flops=got.size, bytes_accessed=6 * got.size, transcendentals=0
+        ),
+    )(term, got)
+
+
 def add_kernel(count, *refs):
     parts, out = refs[:-1], refs[-1]
     total = None
@@ -400,12 +418,11 @@
     )(*parts)
 
 
-def add_grads(term, each):
+def add_grads(term, got, each):
     everyone = OWNERS + SHARED
     near_groups, far_groups = group_lists()
     _, near, far, rows, cols = term.shape
-    got = lax.ppermute(term[1], "core", [(0, 1), (1, 0)])
-    part = add_up(term[:1].reshape(1, -1, cols), got.reshape(1, -1, cols))
+    part = add_cores(term, got)
     part = lax.all_to_all(part.reshape(near, far * rows, cols), everyone, 0, 0, axis_index_groups=near_groups, tiled=True)
     part = add_up(part)
     part = lax.all_to_all(part.reshape(far, rows, cols), everyone, 0, 0, axis_index_groups=far_groups, tiled=True)
@@ -439,10 +456,12 @@
     m3_grad_b, m4_grad_b, top_grad, term = run_grads(
         width, each, scale, partial, gradc, conv_v, m4_cot_v, c3_v, c4_v, m3, *borders[:2]
     )
-    weight_grads = add_grads(term, each)
+    got = lax.ppermute(term[1], "core", [(0, 1), (1, 0)])
     p3, c3_grad, c4_grad = run_outputs(
         width, conv_v, lat3_v, lat4_v, m3, *borders, m3_grad_b, m4_grad_b
     )
+    got, p3, c3_grad, c4_grad = lax.optimization_barrier((got, p3, c3_grad, c4_grad))
+    weight_grads = add_grads(term, got, each)
     return (
         p3.reshape(count, height, width, chans),
         c3_grad.reshape(count, height, width, depth3),

time: 90.1 us -> 89.5 us (level)
  blocking collectives: 40.9 us -> 56.3 us
  waiting for transfers between devices: 10.4 us -> 0.96 us
  starting transfers between devices: 26.9 us -> 21.3 us
    all_to_all x0 -> x1, blocking collectives: none -> 15.3 us  [add_grads(): part = lax.all_to_all(part, SHARED, 0, 0, tiled=True)]
    all_to_all x1 -> x0, waiting for transfers between devices: 7.56 us -> none  [add_grads(): part = lax.all_to_all(part, SHARED, 0, 0, tiled=True)]
    all_to_all x1 -> x0, starting transfers between devices: 5.59 us -> none  [add_grads(): part = lax.all_to_all(part, SHARED, 0, 0, tiled=True)]
    ppermute x1, waiting for transfers between devices: 2.26 us -> 0.36 us  [shards(): got = lax.ppermute(term[1], 'core', [(0, 1), (1, 0)])]
  transfers between devices with their start and end apart: 5 -> 4, of which waited for: 3 -> 2; matrix products, arithmetic and copies ran while one was open for 0% -> 0% of each run, Pallas kernels for 5% -> 5%
where the time goes in v6:
time: 89.5 us; the launch traced here: 89.1 us
  blocking collectives  56.3 us (63%)
  starting transfers between devices  21.3 us (24%)
  Pallas kernels  8.92 us (10%)
  waiting for transfers between devices  0.96 us (1%)
    all_to_all x1, blocking collectives, add_grads(): lax.all_to_all(part.reshape(far, rows, cols), everyone, 0, 0, axis_index_...  22.4 us
    all_to_all x1, blocking collectives, add_grads(): lax.all_to_all(part.reshape(near, far * rows, cols), everyone, 0, 0, axis...  18.5 us
    all_to_all x1, blocking collectives, add_grads(): part = lax.all_to_all(part, SHARED, 0, 0, tiled=True)  15.3 us
    ppermute x1, starting transfers between devices, swap_borders(): row_a = lax.ppermute(row_a, ROWS, pairs + [(j, i) for i, j in pairs])  11.3 us
    pallas_call x5, Pallas kernels, call(): pl.pallas_call(body, out_shape=list(out_shape) + [jax.ShapeDtypeStruct(x....  8.5 us
    ppermute x1, starting transfers between devices, swap_borders(): col = lax.ppermute(col, 'z_lo', [(0, 1), (1, 0)])  4.83 us
    ppermute x1, starting transfers between devices, shards(): got = lax.ppermute(term[1], 'core', [(0, 1), (1, 0)])  4.54 us
  transfers between devices with their start and end apart: 4, of which 2 were waited for; matrix products, arithmetic and copies ran while one was open for 0% of the time, Pallas kernels for 5%

profile of v6, /device:TPU:1, one launch (start us, length us, event | category | flops | bytes accessed | tf_op | source)
XLA Modules:
  0.0 89.1 jit_solution(7809716786127533907)
XLA Ops:
  0.6 2.5 %shard_map.119 = (bf16[512,256]{1,0:T(8,128)(2,1)S(1)}, bf16[16,256]{1,0:T(8,128)(2,1)S(1)}, bf16[144,256]{1,0:T(8,128)(2,1)S(1)}, bf16[144,256]{1,0:T(8,128)(2,...) custom-call(bf16[128,1024]{1,0:T(8,128)(2,1)} %bitcast.22, ...), custom_call_target="tpu_custom_call" | custom-call | flops 201326592 | bytes 2097152 | tf_op jit(solution)/shard_map/pallas_call | solution.py:51
  3.2 4.8 %collective-permute-start = (bf16[16,256]{1,0:T(8,128)(2,1)S(1)}, bf16[16,256]{1,0:T(8,128)(2,1)S(1)}, u32[]{:S(2)}, u32[]{:S(2)}) collective-permute-start(bf16[16,256]{1,0:T(8,128)(2,1)S(1)} %get-tuple-element.32), channel_id=1, source_target_pairs={{0,1},{1,0},{2,3},{3,2},{4,5},{5,4},{6,7},{7,6},{8,9},{9,8},{10,11... | collective-permute-start | bytes 24584 | tf_op jit(solution)/shard_map/ppermute | solution.py:359
  8.0 1.3 %shard_map.120 = (bf16[2304,256]{1,0:T(8,128)(2,1)S(1)}, bf16[128,256]{1,0:T(8,128)(2,1)S(1)}) custom-call(bf16[2304,256]{1,0:T(8,128)(2,1)} %refs_0_.1, bf16[128,256]{1,0:T(8,128)(2,1)} %bitcast.24, bf16[512,256]{1,0:T(8,128)(2,1)S(1)} %get-tuple-element.30.refs_2_.refs_6_.refs_3_), custom_call_target="tpu_custom_call" | custom-call | bytes 1245184 | tf_op jit(solution)/shard_map/pallas_call | solution.py:51
  9.3 0.0 collective-permute-done.refs_3_.refs_6_
  9.3 0.7 collective-permute-start.2
  10.0 11.3 %collective-permute-start.1 = (bf16[144,256]{1,0:T(8,128)(2,1)S(1)}, bf16[144,256]{1,0:T(8,128)(2,1)S(1)}, u32[]{:S(2)}, u32[]{:S(2)}) collective-permute-start(bf16[144,256]{1,0:T(8,128)(2,1)S(1)} %get-tuple-element.56), channel_id=1, source_target_pairs={{0,2},{4,6},{8,10},{12,14},{16,18},{20,22},{24,26},{28,30},{2,0},{... | collective-permute-start | bytes 221192 | tf_op jit(solution)/shard_map/ppermute | solution.py:366
  21.3 1.4 %shard_map.121 = (f32[512,256]{1,0:T(8,128)S(1)}, f32[2304,256]{1,0:T(8,128)S(1)}) custom-call(bf16[512,256]{1,0:T(8,128)(2,1)S(1)} %get-tuple-element.29.refs_0_, bf16[2304,256]{1,0:T(8,128)(2,1)S(1)} %get-tuple-element.31.refs_1_.refs_2_.refs_0_, bf16[512,256]{1,0:T(8,128)(2,1)S(1)} %get-tuple-element.30.refs_2_.refs_6_.refs_3_, ...), custom_call_target="tpu_custom_call" | custom-call | flops 1207959552 | bytes 4718592 | tf_op jit(solution)/shard_map/pallas_call | solution.py:51
  22.7 0.0 collective-permute-done.2.refs_8_.refs_5_
  22.7 0.6 collective-permute-done.1.refs_7_.refs_4_
  23.3 1.4 %shard_map.122 = (bf16[512,256]{1,0:T(8,128)(2,1)S(1)}, bf16[128,256]{1,0:T(8,128)(2,1)S(1)}, bf16[32,256]{1,0:T(8,128)(2,1)}, bf16[2,8,32,16,128]{4,3,2,1,0:T(8,128)(2,1)S(1)}) custom-call(f32[512,256]{1,0:T(8,128)S(1)} %get-tuple-element.33.refs_0_, f32[2304,256]{1,0:T(8,128)S(1)} %get-tuple-element.34.refs_1_, ...), custom_call_target="tpu_custom_call" | custom-call | flops 251658240 | bytes 5505024 | tf_op jit(solution)/shard_map/pallas_call | solution.py:51
  24.7 0.2 slice_bitcast_fusion
  24.8 4.5 %collective-permute-start.3 = (bf16[8,32,16,128]{3,2,1,0:T(8,128)(2,1)S(1)}, bf16[8,32,16,128]{3,2,1,0:T(8,128)(2,1)S(1)}, u32[]{:S(2)}, u32[]{:S(2)}) collective-permute-start(bf16[8,32,16,128]{3,2,1,0:T(8,128)(2,1)S(1)} %slice_bitcast_fusion), channel_id=1, source_target_pairs={{0,32},{32,0},{1,33},{33,1},{2,34},{34,2},{3,35},{35,3},{4,36},{36... | collective-permute-start | bytes 3145736 | tf_op jit(solution)/shard_map/ppermute | solution.py:459
  29.4 1.9 %shard_map.123 = (bf16[512,256]{1,0:T(8,128)(2,1)}, bf16[512,512]{1,0:T(8,128)(2,1)}, bf16[128,1024]{1,0:T(8,128)(2,1)}) custom-call(bf16[2304,256]{1,0:T(8,128)(2,1)S(1)} %get-tuple-element.31.refs_1_.refs_2_.refs_0_, bf16[512,256]{1,0:T(8,128)(2,1)S(1)} %get-tuple-element.41.refs_1_, bf16[1024,256]{1,0:T(8,128)(2,1)S(1)} %get-tuple-element.42.refs_2_, ...), custom_call_target="tpu_custom_call" | custom-call | flops 805306368 | bytes 3932160 | tf_op jit(solution)/shard_map/pallas_call | solution.py:51
  31.3 0.4 collective-permute-done.3.got
  31.7 0.2 shard_map.124
  31.9 18.5 %all_to_all.15.refs_0_ = bf16[8,512,128]{2,1,0:T(8,128)(2,1)S(1)} all-to-all(bf16[8,512,128]{2,1,0:T(8,128)(2,1)S(1)} %bitcast.18), channel_id=1, replica_groups={{0,1,64,65,8,9,72,73},{2,3,66,67,10,11,74,75},{4,5,68,69,12,13,76,77},{..., dimensions={0} | all-to-all | bytes 2097152 | tf_op jit(solution)/shard_map/all_to_all | solution.py:426
  50.4 0.1 shard_map.125
  50.6 22.4 %all_to_all.16.refs_0_ = bf16[32,16,128]{2,1,0:T(8,128)(2,1)S(1)} all-to-all(bf16[32,16,128]{2,1,0:T(8,128)(2,1)S(1)} %bitcast.19), channel_id=1, replica_groups={{0,2,4,6,128,130,132,134,256,258,260,262,384,386,388,390,16,18,20,22,14..., dimensions={0} | all-to-all | bytes 262144 | tf_op jit(solution)/shard_map/all_to_all | solution.py:428
  73.0 15.3 %all_to_all.17 = bf16[32,16,128]{2,1,0:T(8,128)(2,1)S(1)} all-to-all(bf16[32,16,128]{2,1,0:T(8,128)(2,1)S(1)} %shard_map.126), channel_id=1, replica_groups=mesh['y'=8,'core'=2,'x'=4,'z_hi'=4,'z_lo'=2] {'x','z_hi','z_lo'}, dimensions={0} | all-to-all | bytes 262144 | tf_op jit(solution)/shard_map/all_to_all | solution.py:430
  88.4 0.7 pad_maximum_fusion
  (4 shorter events, 0.1 us)
Async XLA Ops:
  3.2 6.1 %collective-permute-start = (bf16[16,256]{1,0:T(8,128)(2,1)S(1)}, bf16[16,256]{1,0:T(8,128)(2,1)S(1)}, u32[]{:S(2)}, u32[]{:S(2)}) collective-permute-start(bf16[16,256]{1,0:T(8,128)(2,1)S(1)} %get-tuple-element.32), channel_id=1, source_target_pairs={{0,1},{1,0},{2,3},{3,2},{4,5},{5,4},{6,7},{7,6},{8,9},{9,8},{10,11... | collective-permute-start | bytes 24584 | tf_op jit(solution)/shard_map/ppermute | solution.py:359
  9.3 13.4 %collective-permute-start.2 = (bf16[144,256]{1,0:T(8,128)(2,1)S(1)}, bf16[144,256]{1,0:T(8,128)(2,1)S(1)}, u32[]{:S(2)}, u32[]{:S(2)}) collective-permute-start(bf16[144,256]{1,0:T(8,128)(2,1)S(1)} %get-tuple-element.55), channel_id=1, source_target_pairs={{2,4},{6,8},{10,12},{14,16},{18,20},{22,24},{26,28},{4,2},{8,6},{1... | collective-permute-start | bytes 221192 | tf_op jit(solution)/shard_map/ppermute | solution.py:367
  10.0 13.3 %collective-permute-start.1 = (bf16[144,256]{1,0:T(8,128)(2,1)S(1)}, bf16[144,256]{1,0:T(8,128)(2,1)S(1)}, u32[]{:S(2)}, u32[]{:S(2)}) collective-permute-start(bf16[144,256]{1,0:T(8,128)(2,1)S(1)} %get-tuple-element.56), channel_id=1, source_target_pairs={{0,2},{4,6},{8,10},{12,14},{16,18},{20,22},{24,26},{28,30},{2,0},{... | collective-permute-start | bytes 221192 | tf_op jit(solution)/shard_map/ppermute | solution.py:366
  24.8 6.8 %collective-permute-start.3 = (bf16[8,32,16,128]{3,2,1,0:T(8,128)(2,1)S(1)}, bf16[8,32,16,128]{3,2,1,0:T(8,128)(2,1)S(1)}, u32[]{:S(2)}, u32[]{:S(2)}) collective-permute-start(bf16[8,32,16,128]{3,2,1,0:T(8,128)(2,1)S(1)} %slice_bitcast_fusion), channel_id=1, source_target_pairs={{0,32},{32,0},{1,33},{33,1},{2,34},{34,2},{3,35},{35,3},{4,36},{36... | collective-permute-start | bytes 3145736 | tf_op jit(solution)/shard_map/ppermute | solution.py:459

commit v7 on v6

--- a/solution.py
+++ b/solution.py
@@ -144,9 +144,9 @@
     return block // per // 2, (block // per) % 2, block % per
 
 
-def groups_of(core, x, y, z):
-    x, y, z = (x + core) % SIZES["x"], (y + core) % SIZES["y"], (z + core) % SIZES["z"]
-    return (x % 2) * 4 + (y % 2) * 2 + z % 2, (x // 2) * 16 + (y // 2) * 4 + z // 2
+def groups_of(core, x_lo, y, z):
+    near = x_lo * 4 + (y + core) % 2 * 2 + (z + core) % 2
+    return near, (y // 2) * (SIZES["z"] // 2) + z // 2
 
 
 def group_lists():
@@ -155,10 +155,13 @@
     for y in range(SIZES["y"]):
         for core in range(2):
             for x in range(SIZES["x"]):
+                pair_x, x_lo = divmod((x + core) % SIZES["x"], 2)
                 for z in range(SIZES["z"]):
-                    in_near, in_far = groups_of(core, x, y, z)
-                    near.setdefault((core, in_far), [None] * 8)[in_near] = index
-                    far.setdefault((core, in_near), [None] * 32)[in_far] = index
+                    pair_y = (y + core) % SIZES["y"] // 2
+                    pair_z = (z + core) % SIZES["z"] // 2
+                    in_near, in_far = groups_of(core, x_lo, y, z)
+                    near.setdefault((core, pair_x, pair_y, pair_z), [None] * 8)[in_near] = index
+                    far.setdefault((core, pair_x, in_near), [None] * 16)[in_far] = index
                     index += 1
     return list(near.values()), list(far.values())
 
@@ -193,16 +196,14 @@
     def put(first, value):
         value = (value * scale).astype(BF16)
         for k in range(value.shape[0] // 16):
-            y, owner, r = pieces_of(first // 16 + k, each)
+            y, owner, p = pieces_of(first // 16 + k, each)
+            near, far = groups_of(owner, p // SIZES["z"], y, p % SIZES["z"])
             slot = jnp.where(me == owner, 0, 1)
-            for h in range(2):
-                p = h * 16 + r
-                near, far = groups_of(owner, p // SIZES["z"], y, p % SIZES["z"])
-                term[slot, near, far] = value[16 * k : 16 * k + 16, 128 * h : 128 * h + 128]
-
-    blank = jnp.zeros((16, 128), BF16)
+            term[slot, near, far] = value[16 * k : 16 * k + 16]
+
+    blank = jnp.zeros((16, chans), BF16)
     for y in range(SIZES["y"]):
-        for p in [h * 16 + r for r in range(per, 16) for h in range(2)]:
+        for p in range(per, 16):
             for owner in range(2):
                 near, far = groups_of(owner, p // SIZES["z"], y, p % SIZES["z"])
                 term[jnp.where(me == owner, 0, 1), near, far] = blank
@@ -327,7 +328,7 @@
             shape_of(n3, chans),
             shape_of(n4, chans),
             shape_of(n4 // 4, chans),
-            shape_of(2, 8, 32, 16, 128),
+            shape_of(2, 8, 16, 16, chans),
         ],
         [
             pltpu.VMEM((n3, chans), F32),
@@ -418,6 +419,18 @@
     )(*parts)
 
 
+def finish_kernel(parts, out):
+    core = lax.axis_index("core")
+    rows = parts.shape[2]
+    for x_lo in range(2):
+        x = jnp.where(core == x_lo, 0, 1)
+        for z in range(parts.shape[1]):
+            first = (x_lo * parts.shape[1] + z) * rows
+            if first < out.shape[0]:
+                value = parts[x, z].astype(F32) + parts[x + 2, z].astype(F32)
+                out[first : first + rows] = value
+
+
 def add_grads(term, got, each):
     everyone = OWNERS + SHARED
     near_groups, far_groups = group_lists()
@@ -428,8 +441,14 @@
     part = lax.all_to_all(part.reshape(far, rows, cols), everyone, 0, 0, axis_index_groups=far_groups, tiled=True)
     part = add_up(part, count=lax.axis_size(SHARED))
     part = lax.all_to_all(part, SHARED, 0, 0, tiled=True)
-    halves = part.reshape(2, -1, cols)[:, :each].astype(F32)
-    return jnp.concatenate([halves[0], halves[1]], axis=1)
+    in_vmem = pl.BlockSpec(memory_space=pltpu.VMEM)
+    return pl.pallas_call(
+        finish_kernel,
+        out_shape=jax.ShapeDtypeStruct((each, cols), F32),
+        in_specs=[in_vmem],
+        out_specs=in_vmem,
+        compiler_params=pltpu.CompilerParams(vmem_limit_bytes=LIMIT),
+    )(part.reshape(SIZES["x"], SIZES["z"], rows, cols))
 
 
 def shards(c3, c4, top_down, lat3_weight, lat4_weight, conv_weight, p3_cot, m4_cot):

time: 89.5 us -> 86.9 us (0.971)
  blocking collectives: 56.3 us -> 53.9 us
    all_to_all x1, blocking collectives: 22.4 us -> 19 us  [add_grads(): lax.all_to_all(part.reshape(far, rows, cols), everyone, 0, 0, axis_index_...]
    all_to_all x1, blocking collectives: 15.3 us -> 16.3 us  [add_grads(): part = lax.all_to_all(part, SHARED, 0, 0, tiled=True)]
where the time goes in v7:
time: 86.9 us; the launch traced here: 86.3 us
  blocking collectives  53.9 us (62%)
  starting transfers between devices  21.3 us (25%)
  Pallas kernels  9.34 us (11%)
  waiting for transfers between devices  0.96 us (1%)
    all_to_all x1, blocking collectives, add_grads(): lax.all_to_all(part.reshape(far, rows, cols), everyone, 0, 0, axis_index_...  19 us
    all_to_all x1, blocking collectives, add_grads(): lax.all_to_all(part.reshape(near, far * rows, cols), everyone, 0, 0, axis...  18.5 us
    all_to_all x1, blocking collectives, add_grads(): part = lax.all_to_all(part, SHARED, 0, 0, tiled=True)  16.3 us
    ppermute x1, starting transfers between devices, swap_borders(): row_a = lax.ppermute(row_a, ROWS, pairs + [(j, i) for i, j in pairs])  11.3 us
    pallas_call x5, Pallas kernels, call(): pl.pallas_call(body, out_shape=list(out_shape) + [jax.ShapeDtypeStruct(x....  8.21 us
    ppermute x1, starting transfers between devices, swap_borders(): col = lax.ppermute(col, 'z_lo', [(0, 1), (1, 0)])  4.83 us
    ppermute x1, starting transfers between devices, shards(): got = lax.ppermute(term[1], 'core', [(0, 1), (1, 0)])  4.54 us
  transfers between devices with their start and end apart: 4, of which 2 were waited for; matrix products, arithmetic and copies ran while one was open for 0% of the time, Pallas kernels for 5%

profile of v7, /device:TPU:1, one launch (start us, length us, event | category | flops | bytes accessed | tf_op | source)
XLA Modules:
  0.0 86.3 jit_solution(15967445488842499542)
XLA Ops:
  0.6 2.5 %shard_map.119 = (bf16[512,256]{1,0:T(8,128)(2,1)S(1)}, bf16[16,256]{1,0:T(8,128)(2,1)S(1)}, bf16[144,256]{1,0:T(8,128)(2,1)S(1)}, bf16[144,256]{1,0:T(8,128)(2,...) custom-call(bf16[128,1024]{1,0:T(8,128)(2,1)} %bitcast.18, ...), custom_call_target="tpu_custom_call" | custom-call | flops 201326592 | bytes 2097152 | tf_op jit(solution)/shard_map/pallas_call | solution.py:51
  3.2 4.8 %collective-permute-start = (bf16[16,256]{1,0:T(8,128)(2,1)S(1)}, bf16[16,256]{1,0:T(8,128)(2,1)S(1)}, u32[]{:S(2)}, u32[]{:S(2)}) collective-permute-start(bf16[16,256]{1,0:T(8,128)(2,1)S(1)} %get-tuple-element.32), channel_id=1, source_target_pairs={{0,1},{1,0},{2,3},{3,2},{4,5},{5,4},{6,7},{7,6},{8,9},{9,8},{10,11... | collective-permute-start | bytes 24584 | tf_op jit(solution)/shard_map/ppermute | solution.py:360
  8.0 1.3 %shard_map.120 = (bf16[2304,256]{1,0:T(8,128)(2,1)S(1)}, bf16[128,256]{1,0:T(8,128)(2,1)S(1)}) custom-call(bf16[2304,256]{1,0:T(8,128)(2,1)} %refs_0_.1, bf16[128,256]{1,0:T(8,128)(2,1)} %bitcast.20, bf16[512,256]{1,0:T(8,128)(2,1)S(1)} %get-tuple-element.30.refs_2_.refs_6_.refs_3_), custom_call_target="tpu_custom_call" | custom-call | bytes 1245184 | tf_op jit(solution)/shard_map/pallas_call | solution.py:51
  9.3 0.0 collective-permute-done.refs_3_.refs_6_
  9.3 0.7 collective-permute-start.2
  10.0 11.3 %collective-permute-start.1 = (bf16[144,256]{1,0:T(8,128)(2,1)S(1)}, bf16[144,256]{1,0:T(8,128)(2,1)S(1)}, u32[]{:S(2)}, u32[]{:S(2)}) collective-permute-start(bf16[144,256]{1,0:T(8,128)(2,1)S(1)} %get-tuple-element.54), channel_id=1, source_target_pairs={{0,2},{4,6},{8,10},{12,14},{16,18},{20,22},{24,26},{28,30},{2,0},{... | collective-permute-start | bytes 221192 | tf_op jit(solution)/shard_map/ppermute | solution.py:367
  21.3 1.4 %shard_map.121 = (f32[512,256]{1,0:T(8,128)S(1)}, f32[2304,256]{1,0:T(8,128)S(1)}) custom-call(bf16[512,256]{1,0:T(8,128)(2,1)S(1)} %get-tuple-element.29.refs_0_, bf16[2304,256]{1,0:T(8,128)(2,1)S(1)} %get-tuple-element.31.refs_1_.refs_2_.refs_0_, bf16[512,256]{1,0:T(8,128)(2,1)S(1)} %get-tuple-element.30.refs_2_.refs_6_.refs_3_, ...), custom_call_target="tpu_custom_call" | custom-call | flops 1207959552 | bytes 4718592 | tf_op jit(solution)/shard_map/pallas_call | solution.py:51
  22.7 0.0 collective-permute-done.2.refs_8_.refs_5_
  22.7 0.6 collective-permute-done.1.refs_7_.refs_4_
  23.3 1.1 %shard_map.122 = (bf16[512,256]{1,0:T(8,128)(2,1)S(1)}, bf16[128,256]{1,0:T(8,128)(2,1)S(1)}, bf16[32,256]{1,0:T(8,128)(2,1)}, bf16[2,8,16,16,256]{4,3,2,1,0:T(8,128)(2,1)S(1)}) custom-call(f32[512,256]{1,0:T(8,128)S(1)} %get-tuple-element.33.refs_0_, f32[2304,256]{1,0:T(8,128)S(1)} %get-tuple-element.34.refs_1_, ...), custom_call_target="tpu_custom_call" | custom-call | flops 251658240 | bytes 5505024 | tf_op jit(solution)/shard_map/pallas_call | solution.py:51
  24.4 0.1 slice_bitcast_fusion
  24.5 4.5 %collective-permute-start.3 = (bf16[8,16,16,256]{3,2,1,0:T(8,128)(2,1)S(1)}, bf16[8,16,16,256]{3,2,1,0:T(8,128)(2,1)S(1)}, u32[]{:S(2)}, u32[]{:S(2)}) collective-permute-start(bf16[8,16,16,256]{3,2,1,0:T(8,128)(2,1)S(1)} %slice_bitcast_fusion), channel_id=1, source_target_pairs={{0,32},{32,0},{1,33},{33,1},{2,34},{34,2},{3,35},{35,3},{4,36},{36... | collective-permute-start | bytes 3145736 | tf_op jit(solution)/shard_map/ppermute | solution.py:478
  29.0 1.9 %shard_map.123 = (bf16[512,256]{1,0:T(8,128)(2,1)}, bf16[512,512]{1,0:T(8,128)(2,1)}, bf16[128,1024]{1,0:T(8,128)(2,1)}) custom-call(bf16[2304,256]{1,0:T(8,128)(2,1)S(1)} %get-tuple-element.31.refs_1_.refs_2_.refs_0_, bf16[512,256]{1,0:T(8,128)(2,1)S(1)} %get-tuple-element.41.refs_1_, bf16[1024,256]{1,0:T(8,128)(2,1)S(1)} %get-tuple-element.42.refs_2_, ...), custom_call_target="tpu_custom_call" | custom-call | flops 805306368 | bytes 3932160 | tf_op jit(solution)/shard_map/pallas_call | solution.py:51
  30.9 0.4 collective-permute-done.3.got
  31.3 0.2 shard_map.124
  31.5 18.5 %all_to_all.15.refs_0_ = bf16[8,256,256]{2,1,0:T(8,128)(2,1)S(1)} all-to-all(bf16[8,256,256]{2,1,0:T(8,128)(2,1)S(1)} %bitcast.14), channel_id=1, replica_groups={{0,1,64,65,8,9,72,73},{2,3,66,67,10,11,74,75},{4,5,68,69,12,13,76,77},{..., dimensions={0} | all-to-all | bytes 2097152 | tf_op jit(solution)/shard_map/all_to_all | solution.py:439
  50.1 0.1 shard_map.125
  50.2 19.0 %all_to_all.16.refs_0_ = bf16[16,16,256]{2,1,0:T(8,128)(2,1)S(1)} all-to-all(bf16[16,16,256]{2,1,0:T(8,128)(2,1)S(1)} %bitcast.16), channel_id=1, replica_groups={{0,2,4,6,128,130,132,134,256,258,260,262,384,386,388,390},{1,3,5,7,129,..., dimensions={0} | all-to-all | bytes 262144 | tf_op jit(solution)/shard_map/all_to_all | solution.py:441
  69.3 16.3 %all_to_all.17 = bf16[32,16,256]{2,1,0:T(8,128)(2,1)S(1)} all-to-all(bf16[32,16,256]{2,1,0:T(8,128)(2,1)S(1)} %shard_map.126), channel_id=1, replica_groups=mesh['y'=8,'core'=2,'x'=4,'z_hi'=4,'z_lo'=2] {'x','z_hi','z_lo'}, dimensions={0} | all-to-all | bytes 524288 | tf_op jit(solution)/shard_map/all_to_all | solution.py:443
  85.6 0.7 shard_map.127
  (2 shorter events, 0.0 us)
Async XLA Ops:
  3.2 6.1 %collective-permute-start = (bf16[16,256]{1,0:T(8,128)(2,1)S(1)}, bf16[16,256]{1,0:T(8,128)(2,1)S(1)}, u32[]{:S(2)}, u32[]{:S(2)}) collective-permute-start(bf16[16,256]{1,0:T(8,128)(2,1)S(1)} %get-tuple-element.32), channel_id=1, source_target_pairs={{0,1},{1,0},{2,3},{3,2},{4,5},{5,4},{6,7},{7,6},{8,9},{9,8},{10,11... | collective-permute-start | bytes 24584 | tf_op jit(solution)/shard_map/ppermute | solution.py:360
  9.3 13.4 %collective-permute-start.2 = (bf16[144,256]{1,0:T(8,128)(2,1)S(1)}, bf16[144,256]{1,0:T(8,128)(2,1)S(1)}, u32[]{:S(2)}, u32[]{:S(2)}) collective-permute-start(bf16[144,256]{1,0:T(8,128)(2,1)S(1)} %get-tuple-element.53), channel_id=1, source_target_pairs={{2,4},{6,8},{10,12},{14,16},{18,20},{22,24},{26,28},{4,2},{8,6},{1... | collective-permute-start | bytes 221192 | tf_op jit(solution)/shard_map/ppermute | solution.py:368
  10.0 13.3 %collective-permute-start.1 = (bf16[144,256]{1,0:T(8,128)(2,1)S(1)}, bf16[144,256]{1,0:T(8,128)(2,1)S(1)}, u32[]{:S(2)}, u32[]{:S(2)}) collective-permute-start(bf16[144,256]{1,0:T(8,128)(2,1)S(1)} %get-tuple-element.54), channel_id=1, source_target_pairs={{0,2},{4,6},{8,10},{12,14},{16,18},{20,22},{24,26},{28,30},{2,0},{... | collective-permute-start | bytes 221192 | tf_op jit(solution)/shard_map/ppermute | solution.py:367
  24.5 6.8 %collective-permute-start.3 = (bf16[8,16,16,256]{3,2,1,0:T(8,128)(2,1)S(1)}, bf16[8,16,16,256]{3,2,1,0:T(8,128)(2,1)S(1)}, u32[]{:S(2)}, u32[]{:S(2)}) collective-permute-start(bf16[8,16,16,256]{3,2,1,0:T(8,128)(2,1)S(1)} %slice_bitcast_fusion), channel_id=1, source_target_pairs={{0,32},{32,0},{1,33},{33,1},{2,34},{34,2},{3,35},{35,3},{4,36},{36... | collective-permute-start | bytes 3145736 | tf_op jit(solution)/shard_map/ppermute | solution.py:478

commit v8 on v7

--- a/solution.py
+++ b/solution.py
@@ -99,7 +99,6 @@
     for start, out in ((first, row_a), (second, row_b)):
         out[:width3] = cot[pl.ds(start, width3)]
         out[width3 : 2 * width3] = m3[pl.ds(start, width3)]
-        out[2 * width3 :] = jnp.zeros((2 * lines, out.shape[1]), BF16)
 
 
 def shift_line(line, left, right):
@@ -110,12 +109,11 @@
     return before.astype(BF16), line.astype(BF16), after.astype(BF16)
 
 
-def outer_lines(place, field, row_a, row_b, lines, width):
+def outer_lines(place, field, row_a, row_b, end_a, end_b, lines, width):
     odd = place[2] == 1
     rows = slice(field * width, (field + 1) * width)
-    corner = slice(2 * width, 2 * width + 2 * lines)
     line_a, line_b = row_a[rows].astype(F32), row_b[rows].astype(F32)
-    ends_a, ends_b = row_a[corner].astype(F32), row_b[corner].astype(F32)
+    ends_a, ends_b = end_a[...].astype(F32), end_b[...].astype(F32)
     first, last = field * lines, (field + 1) * lines - 1
     return (
         (jnp.where(odd, line_a, line_b), jnp.where(odd, ends_a, ends_b)[last : last + 1]),
@@ -144,9 +142,8 @@
     return block // per // 2, (block // per) % 2, block % per
 
 
-def groups_of(core, x_lo, y, z):
-    near = x_lo * 4 + (y + core) % 2 * 2 + (z + core) % 2
-    return near, (y // 2) * (SIZES["z"] // 2) + z // 2
+def groups_of(x_lo, y, z):
+    return x_lo * 4 + y % 2 * 2 + z % 2, (y // 2) * (SIZES["z"] // 2) + z // 2
 
 
 def group_lists():
@@ -155,11 +152,11 @@
     for y in range(SIZES["y"]):
         for core in range(2):
             for x in range(SIZES["x"]):
-                pair_x, x_lo = divmod((x + core) % SIZES["x"], 2)
+                pair_x = (x + core) % SIZES["x"] // 2
                 for z in range(SIZES["z"]):
                     pair_y = (y + core) % SIZES["y"] // 2
                     pair_z = (z + core) % SIZES["z"] // 2
-                    in_near, in_far = groups_of(core, x_lo, y, z)
+                    in_near, in_far = groups_of(x % 2, y, z)
                     near.setdefault((core, pair_x, pair_y, pair_z), [None] * 8)[in_near] = index
                     far.setdefault((core, pair_x, in_near), [None] * 16)[in_far] = index
                     index += 1
@@ -185,7 +182,7 @@
 
 
 def grads_kernel(
-    width, each, scale, place, partial, gradc, conv, m4_cot, c3, c4, m3, row_a, row_b,
+    width, each, scale, place, partial, gradc, conv, m4_cot, c3, c4, m3, row_a, row_b, end_a, end_b,
     m3_grad_b, m4_grad_b, top_grad, term, total, sums, sums5,
 ):
     n3, chans = partial.shape
@@ -197,18 +194,18 @@
         value = (value * scale).astype(BF16)
         for k in range(value.shape[0] // 16):
             y, owner, p = pieces_of(first // 16 + k, each)
-            near, far = groups_of(owner, p // SIZES["z"], y, p % SIZES["z"])
+            near, far = groups_of(p // SIZES["z"], y, p % SIZES["z"])
             slot = jnp.where(me == owner, 0, 1)
             term[slot, near, far] = value[16 * k : 16 * k + 16]
 
     blank = jnp.zeros((16, chans), BF16)
     for y in range(SIZES["y"]):
         for p in range(per, 16):
-            for owner in range(2):
-                near, far = groups_of(owner, p // SIZES["z"], y, p % SIZES["z"])
-                term[jnp.where(me == owner, 0, 1), near, far] = blank
-
-    before, after = outer_lines(place, 0, row_a, row_b, n3 // width, width)
+            near, far = groups_of(p // SIZES["z"], y, p % SIZES["z"])
+            for slot in range(2):
+                term[slot, near, far] = blank
+
+    before, after = outer_lines(place, 0, row_a, row_b, end_a, end_b, n3 // width, width)
     to_the_left = jnp.where(place[1] == 1, 1.0, 0.0)
     total[...] = partial[...]
     added = {}
@@ -259,12 +256,12 @@
 
 
 def outputs_kernel(
-    width, place, conv, lat3, lat4, m3, row_a, row_b, col, m3_grad_b, m4_grad_b,
+    width, place, conv, lat3, lat4, m3, row_a, row_b, end_a, end_b, col, m3_grad_b, m4_grad_b,
     p3, c3_grad, c4_grad, shifted,
 ):
     n3, chans = m3.shape
     fill_inner(place, 1, m3, col, shifted, width)
-    before, after = outer_lines(place, 1, row_a, row_b, n3 // width, width)
+    before, after = outer_lines(place, 1, row_a, row_b, end_a, end_b, n3 // width, width)
     fill_line(place, shifted, 0, *before)
     fill_line(place, shifted, n3 // width + 1, *after)
     total = None
@@ -285,7 +282,7 @@
 def run_merge(width, c3, c4, top, lat3, lat4, cot):
     n3, n4, chans = c3.shape[0], c4.shape[0], lat3.shape[1]
     lines = n3 // width
-    border = shape_of(2 * width + 2 * lines, chans)
+    border = shape_of(2 * width, chans)
     return call(
         functools.partial(merge_kernel, width // 2),
         [shape_of(n3, chans), shape_of(2 * lines, chans), border, border],
@@ -319,7 +316,7 @@
     )
 
 
-def run_grads(width, each, scale, partial, gradc, conv, m4_cot, c3, c4, m3, row_a, row_b):
+def run_grads(width, each, scale, partial, gradc, conv, m4_cot, c3, c4, m3, *borders):
     n3, chans = partial.shape
     n4 = c4.shape[0]
     return call(
@@ -338,11 +335,11 @@
         2 * chans * (c3.size + c4.size + 6 * width * chans),
         2 * (c3.size + c4.size + 4 * conv.size),
         (),
-        (partial, gradc, conv, m4_cot, c3, c4, m3, row_a, row_b),
-    )
-
-
-def run_outputs(width, conv, lat3, lat4, m3, row_a, row_b, col, m3_grad_b, m4_grad_b):
+        (partial, gradc, conv, m4_cot, c3, c4, m3, *borders),
+    )
+
+
+def run_outputs(width, conv, lat3, lat4, m3, row_a, row_b, end_a, end_b, col, m3_grad_b, m4_grad_b):
     n3, chans = m3.shape
     n4 = m4_grad_b.shape[0]
     return call(
@@ -352,21 +349,29 @@
         2 * chans * (n3 * lat3.shape[0] + n4 * lat4.shape[0] + 9 * n3 * chans),
         4 * (n3 * lat3.shape[0] + n4 * lat4.shape[0] + conv.size),
         (),
-        (conv, lat3, lat4, m3, row_a, row_b, col, m3_grad_b, m4_grad_b),
+        (conv, lat3, lat4, m3, row_a, row_b, end_a, end_b, col, m3_grad_b, m4_grad_b),
     )
 
 
 def swap_borders(col, row_a, row_b):
+    n_rows = lax.axis_size(ROWS)
+
+    def both_ways(pairs):
+        return pairs + [(j, i) for i, j in pairs]
+
+    swapped = []
+    for first, row in ((0, row_a), (1, row_b)):
+        pairs = [(i, i + 1) for i in range(first, n_rows - 1, 2)]
+        across = [(2 * i + z, 2 * j + 1 - z) for i, j in pairs for z in range(2)]
+        swapped.append(
+            (
+                lax.ppermute(row, ROWS, both_ways(pairs)),
+                lax.ppermute(col, ROWS + ("z_lo",), both_ways(across)),
+            )
+        )
     col = lax.ppermute(col, "z_lo", [(0, 1), (1, 0)])
-    n_rows = lax.axis_size(ROWS)
-    pairs = [(i, i + 1) for i in range(0, n_rows - 1, 2)]
-    between = [(i, i + 1) for i in range(1, n_rows - 1, 2)]
-    start = (row_a.shape[0] - col.shape[0], 0)
-    row_a = lax.dynamic_update_slice(row_a, col, start)
-    row_b = lax.dynamic_update_slice(row_b, col, start)
-    row_a = lax.ppermute(row_a, ROWS, pairs + [(j, i) for i, j in pairs])
-    row_b = lax.ppermute(row_b, ROWS, between + [(j, i) for i, j in between])
-    return row_a, row_b, col
+    (row_a, end_a), (row_b, end_b) = swapped
+    return row_a, row_b, end_a, end_b, col
 
 
 def add_cores_kernel(term, got, out):
@@ -420,15 +425,12 @@
 
 
 def finish_kernel(parts, out):
-    core = lax.axis_index("core")
     rows = parts.shape[2]
-    for x_lo in range(2):
-        x = jnp.where(core == x_lo, 0, 1)
+    for x in range(2):
         for z in range(parts.shape[1]):
-            first = (x_lo * parts.shape[1] + z) * rows
+            first = (x * parts.shape[1] + z) * rows
             if first < out.shape[0]:
-                value = parts[x, z].astype(F32) + parts[x + 2, z].astype(F32)
-                out[first : first + rows] = value
+                out[first : first + rows] = parts[x, z].astype(F32) + parts[x + 2, z].astype(F32)
 
 
 def add_grads(term, got, each):
@@ -471,9 +473,9 @@
     c4_v, lat4_v, _, c3_v, lat3_v, cot_v = fetched
     conv_v, m4_cot_v = run_fetch(m3, conv_weight, m4_cot.reshape(n4, chans))
     borders = swap_borders(col, row_a, row_b)
-    partial, gradc = run_early(width, cot_v, conv_v, m3, borders[2])
+    partial, gradc = run_early(width, cot_v, conv_v, m3, borders[-1])
     m3_grad_b, m4_grad_b, top_grad, term = run_grads(
-        width, each, scale, partial, gradc, conv_v, m4_cot_v, c3_v, c4_v, m3, *borders[:2]
+        width, each, scale, partial, gradc, conv_v, m4_cot_v, c3_v, c4_v, m3, *borders[:-1]
     )
     got = lax.ppermute(term[1], "core", [(0, 1), (1, 0)])
     p3, c3_grad, c4_grad = run_outputs(

time: 86.9 us -> 93.6 us (1.077)
  blocking collectives: 53.9 us -> 57.4 us
  starting transfers between devices: 21.3 us -> 23.9 us
    all_to_all x1, blocking collectives: 18.5 us -> 26.1 us  [add_grads(): lax.all_to_all(part.reshape(near, far * rows, cols), everyone, 0, 0, axis...]
    ppermute x2 -> x4, starting transfers between devices: 11.9 us -> 14.5 us  [the longest x2 11.9 us: swap_borders(): lax.ppermute(col, ROWS + ('z_lo',), both_ways(across))]
    all_to_all x1, blocking collectives: 19 us -> 16.9 us  [add_grads(): lax.all_to_all(part.reshape(far, rows, cols), everyone, 0, 0, axis_index_...]
    all_to_all x1, blocking collectives: 16.3 us -> 14.4 us  [add_grads(): part = lax.all_to_all(part, SHARED, 0, 0, tiled=True)]
  transfers between devices with their start and end apart: 4 -> 6, of which waited for: 2 -> 2; matrix products, arithmetic and copies ran while one was open for 0% -> 0% of each run, Pallas kernels for 5% -> 5%
where the time goes in v8:
time: 93.6 us; the launch traced here: 93.2 us
  blocking collectives  57.4 us (61%)
  starting transfers between devices  23.9 us (26%)
  Pallas kernels  9.44 us (10%)
  waiting for transfers between devices  1.62 us (2%)
    all_to_all x1, blocking collectives, add_grads(): lax.all_to_all(part.reshape(near, far * rows, cols), everyone, 0, 0, axis...  26.1 us
    all_to_all x1, blocking collectives, add_grads(): lax.all_to_all(part.reshape(far, rows, cols), everyone, 0, 0, axis_index_...  16.9 us
    all_to_all x1, blocking collectives, add_grads(): part = lax.all_to_all(part, SHARED, 0, 0, tiled=True)  14.4 us
    ppermute x2, starting transfers between devices, swap_borders(): lax.ppermute(col, ROWS + ('z_lo',), both_ways(across))  11.9 us
    pallas_call x5, Pallas kernels, call(): pl.pallas_call(body, out_shape=list(out_shape) + [jax.ShapeDtypeStruct(x....  8.31 us
    ppermute x1, starting transfers between devices, swap_borders(): col = lax.ppermute(col, 'z_lo', [(0, 1), (1, 0)])  4.83 us
    ppermute x1, starting transfers between devices, shards(): got = lax.ppermute(term[1], 'core', [(0, 1), (1, 0)])  4.58 us
    ppermute x2, starting transfers between devices, swap_borders(): lax.ppermute(row, ROWS, both_ways(pairs))  2.59 us
  transfers between devices with their start and end apart: 6, of which 2 were waited for; matrix products, arithmetic and copies ran while one was open for 0% of the time, Pallas kernels for 5%

profile of v8, /device:TPU:1, one launch (start us, length us, event | category | flops | bytes accessed | tf_op | source)
XLA Modules:
  0.0 93.2 jit_solution(8845516279885786429)
XLA Ops:
  0.6 2.5 %shard_map.119 = (bf16[512,256]{1,0:T(8,128)(2,1)S(1)}, bf16[16,256]{1,0:T(8,128)(2,1)S(1)}, bf16[128,256]{1,0:T(8,128)(2,1)S(1)}, bf16[128,256]{1,0:T(8,128)(2,...) custom-call(bf16[128,1024]{1,0:T(8,128)(2,1)} %bitcast.18, ...), custom_call_target="tpu_custom_call" | custom-call | flops 201326592 | bytes 2097152 | tf_op jit(solution)/shard_map/pallas_call | solution.py:51
  3.2 4.8 %collective-permute-start = (bf16[16,256]{1,0:T(8,128)(2,1)S(1)}, bf16[16,256]{1,0:T(8,128)(2,1)S(1)}, u32[]{:S(2)}, u32[]{:S(2)}) collective-permute-start(bf16[16,256]{1,0:T(8,128)(2,1)S(1)} %get-tuple-element.32), channel_id=1, source_target_pairs={{0,1},{1,0},{2,3},{3,2},{4,5},{5,4},{6,7},{7,6},{8,9},{9,8},{10,11... | collective-permute-start | bytes 24584 | tf_op jit(solution)/shard_map/ppermute | solution.py:372
  8.0 0.7 collective-permute-start.4
  8.7 11.3 %collective-permute-start.3 = (bf16[16,256]{1,0:T(8,128)(2,1)S(1)}, bf16[16,256]{1,0:T(8,128)(2,1)S(1)}, u32[]{:S(2)}, u32[]{:S(2)}) collective-permute-start(bf16[16,256]{1,0:T(8,128)(2,1)S(1)} %get-tuple-element.32), channel_id=1, source_target_pairs={{0,3},{1,2},{4,7},{5,6},{8,11},{9,10},{12,15},{13,14},{16,19},{17,... | collective-permute-start | bytes 24584 | tf_op jit(solution)/shard_map/ppermute | solution.py:369
  19.9 1.9 %collective-permute-start.1 = (bf16[128,256]{1,0:T(8,128)(2,1)S(1)}, bf16[128,256]{1,0:T(8,128)(2,1)S(1)}, u32[]{:S(2)}, u32[]{:S(2)}) collective-permute-start(bf16[128,256]{1,0:T(8,128)(2,1)S(1)} %get-tuple-element.38), channel_id=1, source_target_pairs={{0,2},{4,6},{8,10},{12,14},{16,18},{20,22},{24,26},{28,30},{2,0},{... | collective-permute-start | bytes 196616 | tf_op jit(solution)/shard_map/ppermute | solution.py:368
  21.9 0.7 collective-permute-start.2
  22.5 1.3 %shard_map.120 = (bf16[2304,256]{1,0:T(8,128)(2,1)S(1)}, bf16[128,256]{1,0:T(8,128)(2,1)S(1)}) custom-call(bf16[2304,256]{1,0:T(8,128)(2,1)} %refs_0_.1, bf16[128,256]{1,0:T(8,128)(2,1)} %bitcast.20, bf16[512,256]{1,0:T(8,128)(2,1)S(1)} %get-tuple-element.30.refs_2_.refs_6_.refs_3_), custom_call_target="tpu_custom_call" | custom-call | bytes 1245184 | tf_op jit(solution)/shard_map/pallas_call | solution.py:51
  23.9 0.0 collective-permute-done.refs_3_.refs_8_
  23.9 1.4 %shard_map.121 = (f32[512,256]{1,0:T(8,128)S(1)}, f32[2304,256]{1,0:T(8,128)S(1)}) custom-call(bf16[512,256]{1,0:T(8,128)(2,1)S(1)} %get-tuple-element.29.refs_0_, bf16[2304,256]{1,0:T(8,128)(2,1)S(1)} %get-tuple-element.31.refs_1_.refs_2_.refs_0_, bf16[512,256]{1,0:T(8,128)(2,1)S(1)} %get-tuple-element.30.refs_2_.refs_6_.refs_3_, ...), custom_call_target="tpu_custom_call" | custom-call | flops 1207959552 | bytes 4718592 | tf_op jit(solution)/shard_map/pallas_call | solution.py:51
  25.3 0.0 collective-permute-done.4.refs_10_.refs_7_
  25.3 0.0 collective-permute-done.3.refs_9_.refs_6_
  25.3 1.2 %collective-permute-done.1.refs_7_.refs_4_ = bf16[128,256]{1,0:T(8,128)(2,1)S(1)} collective-permute-done((bf16[128,256]{1,0:T(8,128)(2,1)S(1)}, bf16[128,256]{1,0:T(8,128)(2,1)S(1)}, u32[]{:S(2)}, u32[]{:S(2)}) %collective-permute-start.1) | collective-permute-done | bytes 65568 | tf_op jit(solution)/shard_map/ppermute | solution.py:368
  26.5 0.0 collective-permute-done.2.refs_8_.refs_5_
  26.6 1.2 %shard_map.122 = (bf16[512,256]{1,0:T(8,128)(2,1)S(1)}, bf16[128,256]{1,0:T(8,128)(2,1)S(1)}, bf16[32,256]{1,0:T(8,128)(2,1)}, bf16[2,8,16,16,256]{4,3,2,1,0:T(8,128)(2,1)S(1)}) custom-call(f32[512,256]{1,0:T(8,128)S(1)} %get-tuple-element.33.refs_0_, f32[2304,256]{1,0:T(8,128)S(1)} %get-tuple-element.34.refs_1_, ...), custom_call_target="tpu_custom_call" | custom-call | flops 251658240 | bytes 5505024 | tf_op jit(solution)/shard_map/pallas_call | solution.py:51
  27.7 0.1 slice_bitcast_fusion
  27.8 4.6 %collective-permute-start.5 = (bf16[8,16,16,256]{3,2,1,0:T(8,128)(2,1)S(1)}, bf16[8,16,16,256]{3,2,1,0:T(8,128)(2,1)S(1)}, u32[]{:S(2)}, u32[]{:S(2)}) collective-permute-start(bf16[8,16,16,256]{3,2,1,0:T(8,128)(2,1)S(1)} %slice_bitcast_fusion), channel_id=1, source_target_pairs={{0,32},{32,0},{1,33},{33,1},{2,34},{34,2},{3,35},{35,3},{4,36},{36... | collective-permute-start | bytes 3145736 | tf_op jit(solution)/shard_map/ppermute | solution.py:480
  32.4 1.9 %shard_map.123 = (bf16[512,256]{1,0:T(8,128)(2,1)}, bf16[512,512]{1,0:T(8,128)(2,1)}, bf16[128,1024]{1,0:T(8,128)(2,1)}) custom-call(bf16[2304,256]{1,0:T(8,128)(2,1)S(1)} %get-tuple-element.31.refs_1_.refs_2_.refs_0_, bf16[512,256]{1,0:T(8,128)(2,1)S(1)} %get-tuple-element.41.refs_1_, bf16[1024,256]{1,0:T(8,128)(2,1)S(1)} %get-tuple-element.42.refs_2_, ...), custom_call_target="tpu_custom_call" | custom-call | flops 805306368 | bytes 3932160 | tf_op jit(solution)/shard_map/pallas_call | solution.py:51
  34.3 0.4 collective-permute-done.5.got
  34.7 0.2 shard_map.124
  34.9 26.1 %all_to_all.15.refs_0_ = bf16[8,256,256]{2,1,0:T(8,128)(2,1)S(1)} all-to-all(bf16[8,256,256]{2,1,0:T(8,128)(2,1)S(1)} %bitcast.14), channel_id=1, replica_groups={{0,1,64,65,8,9,72,73},{2,3,66,67,10,11,74,75},{4,5,68,69,12,13,76,77},{..., dimensions={0} | all-to-all | bytes 2097152 | tf_op jit(solution)/shard_map/all_to_all | solution.py:441
  61.0 0.1 shard_map.125
  61.2 16.9 %all_to_all.16.refs_0_ = bf16[16,16,256]{2,1,0:T(8,128)(2,1)S(1)} all-to-all(bf16[16,16,256]{2,1,0:T(8,128)(2,1)S(1)} %bitcast.16), channel_id=1, replica_groups={{0,2,4,6,128,130,132,134,256,258,260,262,384,386,388,390},{1,3,5,7,129,..., dimensions={0} | all-to-all | bytes 262144 | tf_op jit(solution)/shard_map/all_to_all | solution.py:443
  78.1 14.4 %all_to_all.17 = bf16[32,16,256]{2,1,0:T(8,128)(2,1)S(1)} all-to-all(bf16[32,16,256]{2,1,0:T(8,128)(2,1)S(1)} %shard_map.126), channel_id=1, replica_groups=mesh['y'=8,'core'=2,'x'=4,'z_hi'=4,'z_lo'=2] {'x','z_hi','z_lo'}, dimensions={0} | all-to-all | bytes 524288 | tf_op jit(solution)/shard_map/all_to_all | solution.py:445
  92.5 0.7 shard_map.127
  (1 shorter events, 0.0 us)
Async XLA Ops:
  3.2 20.7 %collective-permute-start = (bf16[16,256]{1,0:T(8,128)(2,1)S(1)}, bf16[16,256]{1,0:T(8,128)(2,1)S(1)}, u32[]{:S(2)}, u32[]{:S(2)}) collective-permute-start(bf16[16,256]{1,0:T(8,128)(2,1)S(1)} %get-tuple-element.32), channel_id=1, source_target_pairs={{0,1},{1,0},{2,3},{3,2},{4,5},{5,4},{6,7},{7,6},{8,9},{9,8},{10,11... | collective-permute-start | bytes 24584 | tf_op jit(solution)/shard_map/ppermute | solution.py:372
  8.0 17.3 %collective-permute-start.4 = (bf16[16,256]{1,0:T(8,128)(2,1)S(1)}, bf16[16,256]{1,0:T(8,128)(2,1)S(1)}, u32[]{:S(2)}, u32[]{:S(2)}) collective-permute-start(bf16[16,256]{1,0:T(8,128)(2,1)S(1)} %get-tuple-element.32), channel_id=1, source_target_pairs={{2,5},{3,4},{6,9},{7,8},{10,13},{11,12},{14,17},{15,16},{18,21},{1... | collective-permute-start | bytes 24584 | tf_op jit(solution)/shard_map/ppermute | solution.py:369
  8.7 16.6 %collective-permute-start.3 = (bf16[16,256]{1,0:T(8,128)(2,1)S(1)}, bf16[16,256]{1,0:T(8,128)(2,1)S(1)}, u32[]{:S(2)}, u32[]{:S(2)}) collective-permute-start(bf16[16,256]{1,0:T(8,128)(2,1)S(1)} %get-tuple-element.32), channel_id=1, source_target_pairs={{0,3},{1,2},{4,7},{5,6},{8,11},{9,10},{12,15},{13,14},{16,19},{17,... | collective-permute-start | bytes 24584 | tf_op jit(solution)/shard_map/ppermute | solution.py:369
  19.9 6.6 %collective-permute-start.1 = (bf16[128,256]{1,0:T(8,128)(2,1)S(1)}, bf16[128,256]{1,0:T(8,128)(2,1)S(1)}, u32[]{:S(2)}, u32[]{:S(2)}) collective-permute-start(bf16[128,256]{1,0:T(8,128)(2,1)S(1)} %get-tuple-element.38), channel_id=1, source_target_pairs={{0,2},{4,6},{8,10},{12,14},{16,18},{20,22},{24,26},{28,30},{2,0},{... | collective-permute-start | bytes 196616 | tf_op jit(solution)/shard_map/ppermute | solution.py:368
  21.9 4.7 %collective-permute-start.2 = (bf16[128,256]{1,0:T(8,128)(2,1)S(1)}, bf16[128,256]{1,0:T(8,128)(2,1)S(1)}, u32[]{:S(2)}, u32[]{:S(2)}) collective-permute-start(bf16[128,256]{1,0:T(8,128)(2,1)S(1)} %get-tuple-element.39), channel_id=1, source_target_pairs={{2,4},{6,8},{10,12},{14,16},{18,20},{22,24},{26,28},{4,2},{8,6},{1... | collective-permute-start | bytes 196616 | tf_op jit(solution)/shard_map/ppermute | solution.py:368
  27.8 6.9 %collective-permute-start.5 = (bf16[8,16,16,256]{3,2,1,0:T(8,128)(2,1)S(1)}, bf16[8,16,16,256]{3,2,1,0:T(8,128)(2,1)S(1)}, u32[]{:S(2)}, u32[]{:S(2)}) collective-permute-start(bf16[8,16,16,256]{3,2,1,0:T(8,128)(2,1)S(1)} %slice_bitcast_fusion), channel_id=1, source_target_pairs={{0,32},{32,0},{1,33},{33,1},{2,34},{34,2},{3,35},{35,3},{4,36},{36... | collective-permute-start | bytes 3145736 | tf_op jit(solution)/shard_map/ppermute | solution.py:480

commit v9 on v7

--- a/solution.py
+++ b/solution.py
@@ -24,7 +24,8 @@
 
 
 def place_of_device():
-    return lax.axis_index("core"), lax.axis_index("z_lo"), lax.axis_index("z_hi") % 2
+    core = lax.axis_index("core")
+    return core, lax.axis_index("z_lo"), (lax.axis_index("z_hi") + core) % 2
 
 
 def call(kernel, out_shape, scratch, flops, moved, fetched, held=()):
@@ -166,6 +167,16 @@
     return list(near.values()), list(far.values())
 
 
+def shared_lists():
+    n = SIZES["x"] * SIZES["z"]
+    lists = []
+    for owner in range(2 * SIZES["y"]):
+        group = [owner * n + i for i in range(n)]
+        turn = owner % 2 * (n // 2)
+        lists.append(group[turn:] + group[:turn])
+    return lists
+
+
 def early_kernel(width, place, cot, conv, m3, col, partial, gradc, shifted):
     n3, chans = cot.shape
     blank = jnp.zeros((3, width, chans), BF16)
@@ -359,13 +370,20 @@
 def swap_borders(col, row_a, row_b):
     col = lax.ppermute(col, "z_lo", [(0, 1), (1, 0)])
     n_rows = lax.axis_size(ROWS)
-    pairs = [(i, i + 1) for i in range(0, n_rows - 1, 2)]
-    between = [(i, i + 1) for i in range(1, n_rows - 1, 2)]
+
+    def pairs(first):
+        found = []
+        for core in range(2):
+            for i in range((first + core) % 2, n_rows - 1, 2):
+                at = core * n_rows + i
+                found += [(at, at + 1), (at + 1, at)]
+        return found
+
     start = (row_a.shape[0] - col.shape[0], 0)
     row_a = lax.dynamic_update_slice(row_a, col, start)
     row_b = lax.dynamic_update_slice(row_b, col, start)
-    row_a = lax.ppermute(row_a, ROWS, pairs + [(j, i) for i, j in pairs])
-    row_b = lax.ppermute(row_b, ROWS, between + [(j, i) for i, j in between])
+    row_a = lax.ppermute(row_a, ("core",) + ROWS, pairs(0))
+    row_b = lax.ppermute(row_b, ("core",) + ROWS, pairs(1))
     return row_a, row_b, col
 
 
@@ -440,7 +458,7 @@
     part = add_up(part)
     part = lax.all_to_all(part.reshape(far, rows, cols), everyone, 0, 0, axis_index_groups=far_groups, tiled=True)
     part = add_up(part, count=lax.axis_size(SHARED))
-    part = lax.all_to_all(part, SHARED, 0, 0, tiled=True)
+    part = lax.all_to_all(part, everyone, 0, 0, axis_index_groups=shared_lists(), tiled=True)
     in_vmem = pl.BlockSpec(memory_space=pltpu.VMEM)
     return pl.pallas_call(
         finish_kernel,

time: 86.9 us -> 87.4 us (level)
    ppermute x1, starting transfers between devices: 4.54 us -> 10.6 us  [shards(): got = lax.ppermute(term[1], 'core', [(0, 1), (1, 0)])]
    ppermute x2, starting transfers between devices: 11.9 us -> 6.47 us  [the longest x1 5.81 us: swap_borders(): row_b = lax.ppermute(row_b, ('core',) + ROWS, pairs(1))]
  transfers between devices with their start and end apart: 4 -> 4, of which waited for: 2 -> 1; matrix products, arithmetic and copies ran while one was open for 0% -> 0% of each run, Pallas kernels for 5% -> 5%
where the time goes in v9:
time: 87.4 us; the launch traced here: 87 us
  blocking collectives  54.6 us (62%)
  starting transfers between devices  21.9 us (25%)
  Pallas kernels  9.3 us (11%)
    all_to_all x1, blocking collectives, add_grads(): lax.all_to_all(part.reshape(far, rows, cols), everyone, 0, 0, axis_index_...  19 us
    all_to_all x1, blocking collectives, add_grads(): lax.all_to_all(part.reshape(near, far * rows, cols), everyone, 0, 0, axis...  18.5 us
    all_to_all x1, blocking collectives, add_grads(): lax.all_to_all(part, everyone, 0, 0, axis_index_groups=shared_lists(), ti...  17 us
    ppermute x1, starting transfers between devices, shards(): got = lax.ppermute(term[1], 'core', [(0, 1), (1, 0)])  10.6 us
    pallas_call x5, Pallas kernels, call(): pl.pallas_call(body, out_shape=list(out_shape) + [jax.ShapeDtypeStruct(x....  8.17 us
    ppermute x1, starting transfers between devices, swap_borders(): row_b = lax.ppermute(row_b, ('core',) + ROWS, pairs(1))  5.81 us
    ppermute x1, starting transfers between devices, swap_borders(): col = lax.ppermute(col, 'z_lo', [(0, 1), (1, 0)])  4.83 us
  transfers between devices with their start and end apart: 4, of which 1 were waited for; matrix products, arithmetic and copies ran while one was open for 0% of the time, Pallas kernels for 5%

profile of v9, /device:TPU:1, one launch (start us, length us, event | category | flops | bytes accessed | tf_op | source)
XLA Modules:
  0.0 87.0 jit_solution(17514249419971081559)
XLA Ops:
  0.6 2.5 %shard_map.119 = (bf16[512,256]{1,0:T(8,128)(2,1)S(1)}, bf16[16,256]{1,0:T(8,128)(2,1)S(1)}, bf16[144,256]{1,0:T(8,128)(2,1)S(1)}, bf16[144,256]{1,0:T(8,128)(2,...) custom-call(bf16[128,1024]{1,0:T(8,128)(2,1)} %bitcast.18, ...), custom_call_target="tpu_custom_call" | custom-call | flops 201326592 | bytes 2097152 | tf_op jit(solution)/shard_map/pallas_call | solution.py:52
  3.2 4.8 %collective-permute-start = (bf16[16,256]{1,0:T(8,128)(2,1)S(1)}, bf16[16,256]{1,0:T(8,128)(2,1)S(1)}, u32[]{:S(2)}, u32[]{:S(2)}) collective-permute-start(bf16[16,256]{1,0:T(8,128)(2,1)S(1)} %get-tuple-element.32), channel_id=1, source_target_pairs={{0,1},{1,0},{2,3},{3,2},{4,5},{5,4},{6,7},{7,6},{8,9},{9,8},{10,11... | collective-permute-start | bytes 24584 | tf_op jit(solution)/shard_map/ppermute | solution.py:371
  8.0 1.3 %shard_map.120 = (bf16[2304,256]{1,0:T(8,128)(2,1)S(1)}, bf16[128,256]{1,0:T(8,128)(2,1)S(1)}) custom-call(bf16[2304,256]{1,0:T(8,128)(2,1)} %refs_0_.1, bf16[128,256]{1,0:T(8,128)(2,1)} %bitcast.20, bf16[512,256]{1,0:T(8,128)(2,1)S(1)} %get-tuple-element.30.refs_2_.refs_6_.refs_3_), custom_call_target="tpu_custom_call" | custom-call | bytes 1245184 | tf_op jit(solution)/shard_map/pallas_call | solution.py:52
  9.3 0.0 collective-permute-done.refs_3_.refs_6_
  9.3 5.8 %collective-permute-start.2 = (bf16[144,256]{1,0:T(8,128)(2,1)S(1)}, bf16[144,256]{1,0:T(8,128)(2,1)S(1)}, u32[]{:S(2)}, u32[]{:S(2)}) collective-permute-start(bf16[144,256]{1,0:T(8,128)(2,1)S(1)} %get-tuple-element.53), channel_id=1, source_target_pairs={{2,4},{4,2},{6,8},{8,6},{10,12},{12,10},{14,16},{16,14},{18,20},{2... | collective-permute-start | bytes 221192 | tf_op jit(solution)/shard_map/ppermute | solution.py:386
  15.1 0.7 collective-permute-start.1
  15.8 1.4 %shard_map.121 = (f32[512,256]{1,0:T(8,128)S(1)}, f32[2304,256]{1,0:T(8,128)S(1)}) custom-call(bf16[512,256]{1,0:T(8,128)(2,1)S(1)} %get-tuple-element.29.refs_0_, bf16[2304,256]{1,0:T(8,128)(2,1)S(1)} %get-tuple-element.31.refs_1_.refs_2_.refs_0_, bf16[512,256]{1,0:T(8,128)(2,1)S(1)} %get-tuple-element.30.refs_2_.refs_6_.refs_3_, ...), custom_call_target="tpu_custom_call" | custom-call | flops 1207959552 | bytes 4718592 | tf_op jit(solution)/shard_map/pallas_call | solution.py:52
  17.2 0.0 collective-permute-done.2.refs_8_.refs_5_
  17.2 0.0 collective-permute-done.1.refs_7_.refs_4_
  17.3 1.0 %shard_map.122 = (bf16[512,256]{1,0:T(8,128)(2,1)S(1)}, bf16[128,256]{1,0:T(8,128)(2,1)S(1)}, bf16[32,256]{1,0:T(8,128)(2,1)}, bf16[2,8,16,16,256]{4,3,2,1,0:T(8,128)(2,1)S(1)}) custom-call(f32[512,256]{1,0:T(8,128)S(1)} %get-tuple-element.33.refs_0_, f32[2304,256]{1,0:T(8,128)S(1)} %get-tuple-element.34.refs_1_, ...), custom_call_target="tpu_custom_call" | custom-call | flops 251658240 | bytes 5505024 | tf_op jit(solution)/shard_map/pallas_call | solution.py:52
  18.3 0.1 slice_bitcast_fusion
  18.4 10.6 %collective-permute-start.3 = (bf16[8,16,16,256]{3,2,1,0:T(8,128)(2,1)S(1)}, bf16[8,16,16,256]{3,2,1,0:T(8,128)(2,1)S(1)}, u32[]{:S(2)}, u32[]{:S(2)}) collective-permute-start(bf16[8,16,16,256]{3,2,1,0:T(8,128)(2,1)S(1)} %slice_bitcast_fusion), channel_id=1, source_target_pairs={{0,32},{32,0},{1,33},{33,1},{2,34},{34,2},{3,35},{35,3},{4,36},{36... | collective-permute-start | bytes 3145736 | tf_op jit(solution)/shard_map/ppermute | solution.py:496
  29.0 1.9 %shard_map.123 = (bf16[512,256]{1,0:T(8,128)(2,1)}, bf16[512,512]{1,0:T(8,128)(2,1)}, bf16[128,1024]{1,0:T(8,128)(2,1)}) custom-call(bf16[2304,256]{1,0:T(8,128)(2,1)S(1)} %get-tuple-element.31.refs_1_.refs_2_.refs_0_, bf16[512,256]{1,0:T(8,128)(2,1)S(1)} %get-tuple-element.41.refs_1_, bf16[1024,256]{1,0:T(8,128)(2,1)S(1)} %get-tuple-element.42.refs_2_, ...), custom_call_target="tpu_custom_call" | custom-call | flops 805306368 | bytes 3932160 | tf_op jit(solution)/shard_map/pallas_call | solution.py:52
  30.9 0.4 collective-permute-done.3.got
  31.3 0.2 shard_map.124
  31.5 18.5 %all_to_all.15.refs_0_ = bf16[8,256,256]{2,1,0:T(8,128)(2,1)S(1)} all-to-all(bf16[8,256,256]{2,1,0:T(8,128)(2,1)S(1)} %bitcast.14), channel_id=1, replica_groups={{0,1,64,65,8,9,72,73},{2,3,66,67,10,11,74,75},{4,5,68,69,12,13,76,77},{..., dimensions={0} | all-to-all | bytes 2097152 | tf_op jit(solution)/shard_map/all_to_all | solution.py:457
  50.0 0.1 shard_map.125
  50.2 19.0 %all_to_all.16.refs_0_ = bf16[16,16,256]{2,1,0:T(8,128)(2,1)S(1)} all-to-all(bf16[16,16,256]{2,1,0:T(8,128)(2,1)S(1)} %bitcast.16), channel_id=1, replica_groups={{0,2,4,6,128,130,132,134,256,258,260,262,384,386,388,390},{1,3,5,7,129,..., dimensions={0} | all-to-all | bytes 262144 | tf_op jit(solution)/shard_map/all_to_all | solution.py:459
  69.3 17.0 %all_to_all.17 = bf16[32,16,256]{2,1,0:T(8,128)(2,1)S(1)} all-to-all(bf16[32,16,256]{2,1,0:T(8,128)(2,1)S(1)} %shard_map.126), channel_id=1, replica_groups={{0,1,2,3,4,5,6,7,8,9,10,11,12,13,14,15,16,17,18,19,20,21,22,23,24,25,26..., dimensions={0} | all-to-all | bytes 524288 | tf_op jit(solution)/shard_map/all_to_all | solution.py:461
  86.3 0.7 shard_map.127
  (2 shorter events, 0.0 us)
Async XLA Ops:
  3.2 6.1 %collective-permute-start = (bf16[16,256]{1,0:T(8,128)(2,1)S(1)}, bf16[16,256]{1,0:T(8,128)(2,1)S(1)}, u32[]{:S(2)}, u32[]{:S(2)}) collective-permute-start(bf16[16,256]{1,0:T(8,128)(2,1)S(1)} %get-tuple-element.32), channel_id=1, source_target_pairs={{0,1},{1,0},{2,3},{3,2},{4,5},{5,4},{6,7},{7,6},{8,9},{9,8},{10,11... | collective-permute-start | bytes 24584 | tf_op jit(solution)/shard_map/ppermute | solution.py:371
  9.3 7.9 %collective-permute-start.2 = (bf16[144,256]{1,0:T(8,128)(2,1)S(1)}, bf16[144,256]{1,0:T(8,128)(2,1)S(1)}, u32[]{:S(2)}, u32[]{:S(2)}) collective-permute-start(bf16[144,256]{1,0:T(8,128)(2,1)S(1)} %get-tuple-element.53), channel_id=1, source_target_pairs={{2,4},{4,2},{6,8},{8,6},{10,12},{12,10},{14,16},{16,14},{18,20},{2... | collective-permute-start | bytes 221192 | tf_op jit(solution)/shard_map/ppermute | solution.py:386
  15.1 2.1 %collective-permute-start.1 = (bf16[144,256]{1,0:T(8,128)(2,1)S(1)}, bf16[144,256]{1,0:T(8,128)(2,1)S(1)}, u32[]{:S(2)}, u32[]{:S(2)}) collective-permute-start(bf16[144,256]{1,0:T(8,128)(2,1)S(1)} %get-tuple-element.54), channel_id=1, source_target_pairs={{0,2},{2,0},{4,6},{6,4},{8,10},{10,8},{12,14},{14,12},{16,18},{18,... | collective-permute-start | bytes 221192 | tf_op jit(solution)/shard_map/ppermute | solution.py:385
  18.4 12.9 %collective-permute-start.3 = (bf16[8,16,16,256]{3,2,1,0:T(8,128)(2,1)S(1)}, bf16[8,16,16,256]{3,2,1,0:T(8,128)(2,1)S(1)}, u32[]{:S(2)}, u32[]{:S(2)}) collective-permute-start(bf16[8,16,16,256]{3,2,1,0:T(8,128)(2,1)S(1)} %slice_bitcast_fusion), channel_id=1, source_target_pairs={{0,32},{32,0},{1,33},{33,1},{2,34},{34,2},{3,35},{35,3},{4,36},{36... | collective-permute-start | bytes 3145736 | tf_op jit(solution)/shard_map/ppermute | solution.py:496

commit v10 on v7

--- a/solution.py
+++ b/solution.py
@@ -166,6 +166,14 @@
     return list(near.values()), list(far.values())
 
 
+def shared_lists():
+    n = SIZES["x"] * SIZES["z"]
+    return [
+        [owner * n + x * SIZES["z"] + z for z in range(SIZES["z"]) for x in range(SIZES["x"])]
+        for owner in range(2 * SIZES["y"])
+    ]
+
+
 def early_kernel(width, place, cot, conv, m3, col, partial, gradc, shifted):
     n3, chans = cot.shape
     blank = jnp.zeros((3, width, chans), BF16)
@@ -424,10 +432,10 @@
     rows = parts.shape[2]
     for x_lo in range(2):
         x = jnp.where(core == x_lo, 0, 1)
-        for z in range(parts.shape[1]):
-            first = (x_lo * parts.shape[1] + z) * rows
+        for z in range(parts.shape[0]):
+            first = (x_lo * parts.shape[0] + z) * rows
             if first < out.shape[0]:
-                value = parts[x, z].astype(F32) + parts[x + 2, z].astype(F32)
+                value = parts[z, x].astype(F32) + parts[z, x + 2].astype(F32)
                 out[first : first + rows] = value
 
 
@@ -440,7 +448,7 @@
     part = add_up(part)
     part = lax.all_to_all(part.reshape(far, rows, cols), everyone, 0, 0, axis_index_groups=far_groups, tiled=True)
     part = add_up(part, count=lax.axis_size(SHARED))
-    part = lax.all_to_all(part, SHARED, 0, 0, tiled=True)
+    part = lax.all_to_all(part, everyone, 0, 0, axis_index_groups=shared_lists(), tiled=True)
     in_vmem = pl.BlockSpec(memory_space=pltpu.VMEM)
     return pl.pallas_call(
         finish_kernel,
@@ -448,7 +456,7 @@
         in_specs=[in_vmem],
         out_specs=in_vmem,
         compiler_params=pltpu.CompilerParams(vmem_limit_bytes=LIMIT),
-    )(part.reshape(SIZES["x"], SIZES["z"], rows, cols))
+    )(part.reshape(SIZES["z"], SIZES["x"], rows, cols))
 
 
 def shards(c3, c4, top_down, lat3_weight, lat4_weight, conv_weight, p3_cot, m4_cot):

time: 86.9 us -> 88.4 us (1.017)
  blocking collectives: 53.9 us -> 55.6 us
    all_to_all x1, blocking collectives: 16.3 us -> 18 us  [add_grads(): lax.all_to_all(part, everyone, 0, 0, axis_index_groups=shared_lists(), ti...]
where the time goes in v10:
time: 88.4 us; the launch traced here: 88 us
  blocking collectives  55.6 us (63%)
  starting transfers between devices  21.3 us (24%)
  Pallas kernels  9.34 us (11%)
  waiting for transfers between devices  0.96 us (1%)
    all_to_all x1, blocking collectives, add_grads(): lax.all_to_all(part.reshape(far, rows, cols), everyone, 0, 0, axis_index_...  19 us
    all_to_all x1, blocking collectives, add_grads(): lax.all_to_all(part.reshape(near, far * rows, cols), everyone, 0, 0, axis...  18.5 us
    all_to_all x1, blocking collectives, add_grads(): lax.all_to_all(part, everyone, 0, 0, axis_index_groups=shared_lists(), ti...  18 us
    ppermute x1, starting transfers between devices, swap_borders(): row_a = lax.ppermute(row_a, ROWS, pairs + [(j, i) for i, j in pairs])  11.3 us
    pallas_call x5, Pallas kernels, call(): pl.pallas_call(body, out_shape=list(out_shape) + [jax.ShapeDtypeStruct(x....  8.21 us
    ppermute x1, starting transfers between devices, swap_borders(): col = lax.ppermute(col, 'z_lo', [(0, 1), (1, 0)])  4.83 us
    ppermute x1, starting transfers between devices, shards(): got = lax.ppermute(term[1], 'core', [(0, 1), (1, 0)])  4.54 us
  transfers between devices with their start and end apart: 4, of which 2 were waited for; matrix products, arithmetic and copies ran while one was open for 0% of the time, Pallas kernels for 5%

profile of v10, /device:TPU:1, one launch (start us, length us, event | category | flops | bytes accessed | tf_op | source)
XLA Modules:
  0.0 88.0 jit_solution(18242252617551356653)
XLA Ops:
  0.6 2.5 %shard_map.119 = (bf16[512,256]{1,0:T(8,128)(2,1)S(1)}, bf16[16,256]{1,0:T(8,128)(2,1)S(1)}, bf16[144,256]{1,0:T(8,128)(2,1)S(1)}, bf16[144,256]{1,0:T(8,128)(2,...) custom-call(bf16[128,1024]{1,0:T(8,128)(2,1)} %bitcast.18, ...), custom_call_target="tpu_custom_call" | custom-call | flops 201326592 | bytes 2097152 | tf_op jit(solution)/shard_map/pallas_call | solution.py:51
  3.2 4.8 %collective-permute-start = (bf16[16,256]{1,0:T(8,128)(2,1)S(1)}, bf16[16,256]{1,0:T(8,128)(2,1)S(1)}, u32[]{:S(2)}, u32[]{:S(2)}) collective-permute-start(bf16[16,256]{1,0:T(8,128)(2,1)S(1)} %get-tuple-element.32), channel_id=1, source_target_pairs={{0,1},{1,0},{2,3},{3,2},{4,5},{5,4},{6,7},{7,6},{8,9},{9,8},{10,11... | collective-permute-start | bytes 24584 | tf_op jit(solution)/shard_map/ppermute | solution.py:368
  8.0 1.3 %shard_map.120 = (bf16[2304,256]{1,0:T(8,128)(2,1)S(1)}, bf16[128,256]{1,0:T(8,128)(2,1)S(1)}) custom-call(bf16[2304,256]{1,0:T(8,128)(2,1)} %refs_0_.1, bf16[128,256]{1,0:T(8,128)(2,1)} %bitcast.20, bf16[512,256]{1,0:T(8,128)(2,1)S(1)} %get-tuple-element.30.refs_2_.refs_6_.refs_3_), custom_call_target="tpu_custom_call" | custom-call | bytes 1245184 | tf_op jit(solution)/shard_map/pallas_call | solution.py:51
  9.3 0.0 collective-permute-done.refs_3_.refs_6_
  9.3 0.7 collective-permute-start.2
  10.0 11.3 %collective-permute-start.1 = (bf16[144,256]{1,0:T(8,128)(2,1)S(1)}, bf16[144,256]{1,0:T(8,128)(2,1)S(1)}, u32[]{:S(2)}, u32[]{:S(2)}) collective-permute-start(bf16[144,256]{1,0:T(8,128)(2,1)S(1)} %get-tuple-element.54), channel_id=1, source_target_pairs={{0,2},{4,6},{8,10},{12,14},{16,18},{20,22},{24,26},{28,30},{2,0},{... | collective-permute-start | bytes 221192 | tf_op jit(solution)/shard_map/ppermute | solution.py:375
  21.3 1.4 %shard_map.121 = (f32[512,256]{1,0:T(8,128)S(1)}, f32[2304,256]{1,0:T(8,128)S(1)}) custom-call(bf16[512,256]{1,0:T(8,128)(2,1)S(1)} %get-tuple-element.29.refs_0_, bf16[2304,256]{1,0:T(8,128)(2,1)S(1)} %get-tuple-element.31.refs_1_.refs_2_.refs_0_, bf16[512,256]{1,0:T(8,128)(2,1)S(1)} %get-tuple-element.30.refs_2_.refs_6_.refs_3_, ...), custom_call_target="tpu_custom_call" | custom-call | flops 1207959552 | bytes 4718592 | tf_op jit(solution)/shard_map/pallas_call | solution.py:51
  22.7 0.0 collective-permute-done.2.refs_8_.refs_5_
  22.7 0.6 collective-permute-done.1.refs_7_.refs_4_
  23.3 1.1 %shard_map.122 = (bf16[512,256]{1,0:T(8,128)(2,1)S(1)}, bf16[128,256]{1,0:T(8,128)(2,1)S(1)}, bf16[32,256]{1,0:T(8,128)(2,1)}, bf16[2,8,16,16,256]{4,3,2,1,0:T(8,128)(2,1)S(1)}) custom-call(f32[512,256]{1,0:T(8,128)S(1)} %get-tuple-element.33.refs_0_, f32[2304,256]{1,0:T(8,128)S(1)} %get-tuple-element.34.refs_1_, ...), custom_call_target="tpu_custom_call" | custom-call | flops 251658240 | bytes 5505024 | tf_op jit(solution)/shard_map/pallas_call | solution.py:51
  24.4 0.1 slice_bitcast_fusion
  24.5 4.5 %collective-permute-start.3 = (bf16[8,16,16,256]{3,2,1,0:T(8,128)(2,1)S(1)}, bf16[8,16,16,256]{3,2,1,0:T(8,128)(2,1)S(1)}, u32[]{:S(2)}, u32[]{:S(2)}) collective-permute-start(bf16[8,16,16,256]{3,2,1,0:T(8,128)(2,1)S(1)} %slice_bitcast_fusion), channel_id=1, source_target_pairs={{0,32},{32,0},{1,33},{33,1},{2,34},{34,2},{3,35},{35,3},{4,36},{36... | collective-permute-start | bytes 3145736 | tf_op jit(solution)/shard_map/ppermute | solution.py:486
  29.0 1.9 %shard_map.123 = (bf16[512,256]{1,0:T(8,128)(2,1)}, bf16[512,512]{1,0:T(8,128)(2,1)}, bf16[128,1024]{1,0:T(8,128)(2,1)}) custom-call(bf16[2304,256]{1,0:T(8,128)(2,1)S(1)} %get-tuple-element.31.refs_1_.refs_2_.refs_0_, bf16[512,256]{1,0:T(8,128)(2,1)S(1)} %get-tuple-element.41.refs_1_, bf16[1024,256]{1,0:T(8,128)(2,1)S(1)} %get-tuple-element.42.refs_2_, ...), custom_call_target="tpu_custom_call" | custom-call | flops 805306368 | bytes 3932160 | tf_op jit(solution)/shard_map/pallas_call | solution.py:51
  30.9 0.4 collective-permute-done.3.got
  31.3 0.2 shard_map.124
  31.5 18.5 %all_to_all.15.refs_0_ = bf16[8,256,256]{2,1,0:T(8,128)(2,1)S(1)} all-to-all(bf16[8,256,256]{2,1,0:T(8,128)(2,1)S(1)} %bitcast.14), channel_id=1, replica_groups={{0,1,64,65,8,9,72,73},{2,3,66,67,10,11,74,75},{4,5,68,69,12,13,76,77},{..., dimensions={0} | all-to-all | bytes 2097152 | tf_op jit(solution)/shard_map/all_to_all | solution.py:447
  50.1 0.1 shard_map.125
  50.2 19.0 %all_to_all.16.refs_0_ = bf16[16,16,256]{2,1,0:T(8,128)(2,1)S(1)} all-to-all(bf16[16,16,256]{2,1,0:T(8,128)(2,1)S(1)} %bitcast.16), channel_id=1, replica_groups={{0,2,4,6,128,130,132,134,256,258,260,262,384,386,388,390},{1,3,5,7,129,..., dimensions={0} | all-to-all | bytes 262144 | tf_op jit(solution)/shard_map/all_to_all | solution.py:449
  69.3 18.0 %all_to_all.17 = bf16[32,16,256]{2,1,0:T(8,128)(2,1)S(1)} all-to-all(bf16[32,16,256]{2,1,0:T(8,128)(2,1)S(1)} %shard_map.126), channel_id=1, replica_groups={{0,8,16,24,1,9,17,25,2,10,18,26,3,11,19,27,4,12,20,28,5,13,21,29,6,14,2..., dimensions={0} | all-to-all | bytes 524288 | tf_op jit(solution)/shard_map/all_to_all | solution.py:451
  87.3 0.7 shard_map.127
  (2 shorter events, 0.0 us)
Async XLA Ops:
  3.2 6.1 %collective-permute-start = (bf16[16,256]{1,0:T(8,128)(2,1)S(1)}, bf16[16,256]{1,0:T(8,128)(2,1)S(1)}, u32[]{:S(2)}, u32[]{:S(2)}) collective-permute-start(bf16[16,256]{1,0:T(8,128)(2,1)S(1)} %get-tuple-element.32), channel_id=1, source_target_pairs={{0,1},{1,0},{2,3},{3,2},{4,5},{5,4},{6,7},{7,6},{8,9},{9,8},{10,11... | collective-permute-start | bytes 24584 | tf_op jit(solution)/shard_map/ppermute | solution.py:368
  9.3 13.4 %collective-permute-start.2 = (bf16[144,256]{1,0:T(8,128)(2,1)S(1)}, bf16[144,256]{1,0:T(8,128)(2,1)S(1)}, u32[]{:S(2)}, u32[]{:S(2)}) collective-permute-start(bf16[144,256]{1,0:T(8,128)(2,1)S(1)} %get-tuple-element.53), channel_id=1, source_target_pairs={{2,4},{6,8},{10,12},{14,16},{18,20},{22,24},{26,28},{4,2},{8,6},{1... | collective-permute-start | bytes 221192 | tf_op jit(solution)/shard_map/ppermute | solution.py:376
  10.0 13.3 %collective-permute-start.1 = (bf16[144,256]{1,0:T(8,128)(2,1)S(1)}, bf16[144,256]{1,0:T(8,128)(2,1)S(1)}, u32[]{:S(2)}, u32[]{:S(2)}) collective-permute-start(bf16[144,256]{1,0:T(8,128)(2,1)S(1)} %get-tuple-element.54), channel_id=1, source_target_pairs={{0,2},{4,6},{8,10},{12,14},{16,18},{20,22},{24,26},{28,30},{2,0},{... | collective-permute-start | bytes 221192 | tf_op jit(solution)/shard_map/ppermute | solution.py:375
  24.5 6.8 %collective-permute-start.3 = (bf16[8,16,16,256]{3,2,1,0:T(8,128)(2,1)S(1)}, bf16[8,16,16,256]{3,2,1,0:T(8,128)(2,1)S(1)}, u32[]{:S(2)}, u32[]{:S(2)}) collective-permute-start(bf16[8,16,16,256]{3,2,1,0:T(8,128)(2,1)S(1)} %slice_bitcast_fusion), channel_id=1, source_target_pairs={{0,32},{32,0},{1,33},{33,1},{2,34},{34,2},{3,35},{35,3},{4,36},{36... | collective-permute-start | bytes 3145736 | tf_op jit(solution)/shard_map/ppermute | solution.py:486

commit v11 on v7

--- a/solution.py
+++ b/solution.py
@@ -166,6 +166,16 @@
     return list(near.values()), list(far.values())
 
 
+def shared_lists():
+    n = SIZES["x"] * SIZES["z"]
+    lists = []
+    for owner in range(2 * SIZES["y"]):
+        group = [owner * n + i for i in range(n)]
+        turn = owner % 2 * (n // 2)
+        lists.append(group[turn:] + group[:turn])
+    return lists
+
+
 def early_kernel(width, place, cot, conv, m3, col, partial, gradc, shifted):
     n3, chans = cot.shape
     blank = jnp.zeros((3, width, chans), BF16)
@@ -440,7 +450,7 @@
     part = add_up(part)
     part = lax.all_to_all(part.reshape(far, rows, cols), everyone, 0, 0, axis_index_groups=far_groups, tiled=True)
     part = add_up(part, count=lax.axis_size(SHARED))
-    part = lax.all_to_all(part, SHARED, 0, 0, tiled=True)
+    part = lax.all_to_all(part, everyone, 0, 0, axis_index_groups=shared_lists(), tiled=True)
     in_vmem = pl.BlockSpec(memory_space=pltpu.VMEM)
     return pl.pallas_call(
         finish_kernel,

time: 86.9 us -> 87.3 us (level)
  no operation moved by 1% of the time
where the time goes in v11:
time: 87.3 us; the launch traced here: 87 us
  blocking collectives  54.5 us (62%)
  starting transfers between devices  21.3 us (24%)
  Pallas kernels  9.34 us (11%)
  waiting for transfers between devices  0.96 us (1%)
    all_to_all x1, blocking collectives, add_grads(): lax.all_to_all(part.reshape(far, rows, cols), everyone, 0, 0, axis_index_...  19 us
    all_to_all x1, blocking collectives, add_grads(): lax.all_to_all(part.reshape(near, far * rows, cols), everyone, 0, 0, axis...  18.5 us
    all_to_all x1, blocking collectives, add_grads(): lax.all_to_all(part, everyone, 0, 0, axis_index_groups=shared_lists(), ti...  16.9 us
    ppermute x1, starting transfers between devices, swap_borders(): row_a = lax.ppermute(row_a, ROWS, pairs + [(j, i) for i, j in pairs])  11.3 us
    pallas_call x5, Pallas kernels, call(): pl.pallas_call(body, out_shape=list(out_shape) + [jax.ShapeDtypeStruct(x....  8.21 us
    ppermute x1, starting transfers between devices, swap_borders(): col = lax.ppermute(col, 'z_lo', [(0, 1), (1, 0)])  4.83 us
    ppermute x1, starting transfers between devices, shards(): got = lax.ppermute(term[1], 'core', [(0, 1), (1, 0)])  4.54 us
  transfers between devices with their start and end apart: 4, of which 2 were waited for; matrix products, arithmetic and copies ran while one was open for 0% of the time, Pallas kernels for 5%

profile of v11, /device:TPU:1, one launch (start us, length us, event | category | flops | bytes accessed | tf_op | source)
XLA Modules:
  0.0 87.0 jit_solution(6969442908227876209)
XLA Ops:
  0.6 2.5 %shard_map.119 = (bf16[512,256]{1,0:T(8,128)(2,1)S(1)}, bf16[16,256]{1,0:T(8,128)(2,1)S(1)}, bf16[144,256]{1,0:T(8,128)(2,1)S(1)}, bf16[144,256]{1,0:T(8,128)(2,...) custom-call(bf16[128,1024]{1,0:T(8,128)(2,1)} %bitcast.18, ...), custom_call_target="tpu_custom_call" | custom-call | flops 201326592 | bytes 2097152 | tf_op jit(solution)/shard_map/pallas_call | solution.py:51
  3.2 4.8 %collective-permute-start = (bf16[16,256]{1,0:T(8,128)(2,1)S(1)}, bf16[16,256]{1,0:T(8,128)(2,1)S(1)}, u32[]{:S(2)}, u32[]{:S(2)}) collective-permute-start(bf16[16,256]{1,0:T(8,128)(2,1)S(1)} %get-tuple-element.32), channel_id=1, source_target_pairs={{0,1},{1,0},{2,3},{3,2},{4,5},{5,4},{6,7},{7,6},{8,9},{9,8},{10,11... | collective-permute-start | bytes 24584 | tf_op jit(solution)/shard_map/ppermute | solution.py:370
  8.0 1.3 %shard_map.120 = (bf16[2304,256]{1,0:T(8,128)(2,1)S(1)}, bf16[128,256]{1,0:T(8,128)(2,1)S(1)}) custom-call(bf16[2304,256]{1,0:T(8,128)(2,1)} %refs_0_.1, bf16[128,256]{1,0:T(8,128)(2,1)} %bitcast.20, bf16[512,256]{1,0:T(8,128)(2,1)S(1)} %get-tuple-element.30.refs_2_.refs_6_.refs_3_), custom_call_target="tpu_custom_call" | custom-call | bytes 1245184 | tf_op jit(solution)/shard_map/pallas_call | solution.py:51
  9.3 0.0 collective-permute-done.refs_3_.refs_6_
  9.3 0.7 collective-permute-start.2
  10.0 11.3 %collective-permute-start.1 = (bf16[144,256]{1,0:T(8,128)(2,1)S(1)}, bf16[144,256]{1,0:T(8,128)(2,1)S(1)}, u32[]{:S(2)}, u32[]{:S(2)}) collective-permute-start(bf16[144,256]{1,0:T(8,128)(2,1)S(1)} %get-tuple-element.54), channel_id=1, source_target_pairs={{0,2},{4,6},{8,10},{12,14},{16,18},{20,22},{24,26},{28,30},{2,0},{... | collective-permute-start | bytes 221192 | tf_op jit(solution)/shard_map/ppermute | solution.py:377
  21.3 1.4 %shard_map.121 = (f32[512,256]{1,0:T(8,128)S(1)}, f32[2304,256]{1,0:T(8,128)S(1)}) custom-call(bf16[512,256]{1,0:T(8,128)(2,1)S(1)} %get-tuple-element.29.refs_0_, bf16[2304,256]{1,0:T(8,128)(2,1)S(1)} %get-tuple-element.31.refs_1_.refs_2_.refs_0_, bf16[512,256]{1,0:T(8,128)(2,1)S(1)} %get-tuple-element.30.refs_2_.refs_6_.refs_3_, ...), custom_call_target="tpu_custom_call" | custom-call | flops 1207959552 | bytes 4718592 | tf_op jit(solution)/shard_map/pallas_call | solution.py:51
  22.7 0.0 collective-permute-done.2.refs_8_.refs_5_
  22.7 0.6 collective-permute-done.1.refs_7_.refs_4_
  23.3 1.1 %shard_map.122 = (bf16[512,256]{1,0:T(8,128)(2,1)S(1)}, bf16[128,256]{1,0:T(8,128)(2,1)S(1)}, bf16[32,256]{1,0:T(8,128)(2,1)}, bf16[2,8,16,16,256]{4,3,2,1,0:T(8,128)(2,1)S(1)}) custom-call(f32[512,256]{1,0:T(8,128)S(1)} %get-tuple-element.33.refs_0_, f32[2304,256]{1,0:T(8,128)S(1)} %get-tuple-element.34.refs_1_, ...), custom_call_target="tpu_custom_call" | custom-call | flops 251658240 | bytes 5505024 | tf_op jit(solution)/shard_map/pallas_call | solution.py:51
  24.4 0.1 slice_bitcast_fusion
  24.5 4.5 %collective-permute-start.3 = (bf16[8,16,16,256]{3,2,1,0:T(8,128)(2,1)S(1)}, bf16[8,16,16,256]{3,2,1,0:T(8,128)(2,1)S(1)}, u32[]{:S(2)}, u32[]{:S(2)}) collective-permute-start(bf16[8,16,16,256]{3,2,1,0:T(8,128)(2,1)S(1)} %slice_bitcast_fusion), channel_id=1, source_target_pairs={{0,32},{32,0},{1,33},{33,1},{2,34},{34,2},{3,35},{35,3},{4,36},{36... | collective-permute-start | bytes 3145736 | tf_op jit(solution)/shard_map/ppermute | solution.py:488
  29.0 1.9 %shard_map.123 = (bf16[512,256]{1,0:T(8,128)(2,1)}, bf16[512,512]{1,0:T(8,128)(2,1)}, bf16[128,1024]{1,0:T(8,128)(2,1)}) custom-call(bf16[2304,256]{1,0:T(8,128)(2,1)S(1)} %get-tuple-element.31.refs_1_.refs_2_.refs_0_, bf16[512,256]{1,0:T(8,128)(2,1)S(1)} %get-tuple-element.41.refs_1_, bf16[1024,256]{1,0:T(8,128)(2,1)S(1)} %get-tuple-element.42.refs_2_, ...), custom_call_target="tpu_custom_call" | custom-call | flops 805306368 | bytes 3932160 | tf_op jit(solution)/shard_map/pallas_call | solution.py:51
  30.9 0.4 collective-permute-done.3.got
  31.3 0.2 shard_map.124
  31.5 18.5 %all_to_all.15.refs_0_ = bf16[8,256,256]{2,1,0:T(8,128)(2,1)S(1)} all-to-all(bf16[8,256,256]{2,1,0:T(8,128)(2,1)S(1)} %bitcast.14), channel_id=1, replica_groups={{0,1,64,65,8,9,72,73},{2,3,66,67,10,11,74,75},{4,5,68,69,12,13,76,77},{..., dimensions={0} | all-to-all | bytes 2097152 | tf_op jit(solution)/shard_map/all_to_all | solution.py:449
  50.1 0.1 shard_map.125
  50.2 19.0 %all_to_all.16.refs_0_ = bf16[16,16,256]{2,1,0:T(8,128)(2,1)S(1)} all-to-all(bf16[16,16,256]{2,1,0:T(8,128)(2,1)S(1)} %bitcast.16), channel_id=1, replica_groups={{0,2,4,6,128,130,132,134,256,258,260,262,384,386,388,390},{1,3,5,7,129,..., dimensions={0} | all-to-all | bytes 262144 | tf_op jit(solution)/shard_map/all_to_all | solution.py:451
  69.3 16.9 %all_to_all.17 = bf16[32,16,256]{2,1,0:T(8,128)(2,1)S(1)} all-to-all(bf16[32,16,256]{2,1,0:T(8,128)(2,1)S(1)} %shard_map.126), channel_id=1, replica_groups={{0,1,2,3,4,5,6,7,8,9,10,11,12,13,14,15,16,17,18,19,20,21,22,23,24,25,26..., dimensions={0} | all-to-all | bytes 524288 | tf_op jit(solution)/shard_map/all_to_all | solution.py:453
  86.2 0.7 shard_map.127
  (2 shorter events, 0.0 us)
Async XLA Ops:
  3.2 6.1 %collective-permute-start = (bf16[16,256]{1,0:T(8,128)(2,1)S(1)}, bf16[16,256]{1,0:T(8,128)(2,1)S(1)}, u32[]{:S(2)}, u32[]{:S(2)}) collective-permute-start(bf16[16,256]{1,0:T(8,128)(2,1)S(1)} %get-tuple-element.32), channel_id=1, source_target_pairs={{0,1},{1,0},{2,3},{3,2},{4,5},{5,4},{6,7},{7,6},{8,9},{9,8},{10,11... | collective-permute-start | bytes 24584 | tf_op jit(solution)/shard_map/ppermute | solution.py:370
  9.3 13.4 %collective-permute-start.2 = (bf16[144,256]{1,0:T(8,128)(2,1)S(1)}, bf16[144,256]{1,0:T(8,128)(2,1)S(1)}, u32[]{:S(2)}, u32[]{:S(2)}) collective-permute-start(bf16[144,256]{1,0:T(8,128)(2,1)S(1)} %get-tuple-element.53), channel_id=1, source_target_pairs={{2,4},{6,8},{10,12},{14,16},{18,20},{22,24},{26,28},{4,2},{8,6},{1... | collective-permute-start | bytes 221192 | tf_op jit(solution)/shard_map/ppermute | solution.py:378
  10.0 13.3 %collective-permute-start.1 = (bf16[144,256]{1,0:T(8,128)(2,1)S(1)}, bf16[144,256]{1,0:T(8,128)(2,1)S(1)}, u32[]{:S(2)}, u32[]{:S(2)}) collective-permute-start(bf16[144,256]{1,0:T(8,128)(2,1)S(1)} %get-tuple-element.54), channel_id=1, source_target_pairs={{0,2},{4,6},{8,10},{12,14},{16,18},{20,22},{24,26},{28,30},{2,0},{... | collective-permute-start | bytes 221192 | tf_op jit(solution)/shard_map/ppermute | solution.py:377
  24.5 6.8 %collective-permute-start.3 = (bf16[8,16,16,256]{3,2,1,0:T(8,128)(2,1)S(1)}, bf16[8,16,16,256]{3,2,1,0:T(8,128)(2,1)S(1)}, u32[]{:S(2)}, u32[]{:S(2)}) collective-permute-start(bf16[8,16,16,256]{3,2,1,0:T(8,128)(2,1)S(1)} %slice_bitcast_fusion), channel_id=1, source_target_pairs={{0,32},{32,0},{1,33},{33,1},{2,34},{34,2},{3,35},{35,3},{4,36},{36... | collective-permute-start | bytes 3145736 | tf_op jit(solution)/shard_map/ppermute | solution.py:488
